TPU v7x, 32 devices: a whole 2x2x4 slice. The times are simulated.
32 devices in a mesh: space: 4 (over z), chaos: 8 (over y, x, core).
Axes of the slice: x: 2, y: 2, z: 4, core: 2. Of those that a mesh axis runs over, the one named last changes fastest.
Arguments:
- field: float32 [448, 8, 8, 128], P('chaos', 'space'), may hold values from -6 to 6
- modes: float32 [21, 8, 8, 128], P(None, 'space'), may hold values from -6 to 6
- send_rows: int32 [8, 64], P('chaos'), may hold values from 0 to 55, as said below
- pick: int32 [448, 41], P('chaos'), may hold values from 0 to 63
- mode_ids: int32 [448, 41], P('chaos'), may hold values from 0 to 20
- coef: float32 [448, 41], P('chaos'), may hold values from -0.15 to 0.15
Outputs:
- first: float32 [448, 8, 8, 128], P('chaos', 'space')
- second: float32 [448, 8, 8, 128], P('chaos', 'space')
Inputs may be any that keep to these rules, and one draw needn't show every extreme that they name: `send_rows`: in row e, each block of 8 entries d * 8 to d * 8 + 7 holds different local terms of owner e.
All inputs are finite; a program needn't handle non-finite values.
Results may differ from a plain program's by a relative error of at most 0.000098.
Values sent between devices are 32-bit elements; how exact they have to be, the bound alone decides.
No kernel may reach another device: no remote copies, remote signals or barrier semaphores. Data moves between devices by JAX's collectives and lax.ppermute only.
A program may use at most 64 MiB of HBM per device.

v0:
```python
import jax
import jax.numpy as jnp
from jax import lax
from jax.sharding import PartitionSpec as P


def padded_2(cells, sides, width):
    for axis, dim in sides:
        count = lax.axis_size(axis)
        ends = count - 1
        head = lax.slice_in_dim(cells, 0, width, axis=dim)
        tail = lax.slice_in_dim(cells, cells.shape[dim] - width, cells.shape[dim], axis=dim)
        cells = jnp.concatenate(
            [
                lax.ppermute(tail, axis, [(i, (i + 1) % count) for i in range(ends)]),
                cells,
                lax.ppermute(head, axis, [((i + 1) % count, i) for i in range(ends)]),
            ],
            axis=dim,
        )
    return cells


def laplace(padded):
    center = padded[:, 1:-1]
    side = jnp.pad(center, ((0, 0), (0, 0), (1, 1), (1, 1)))
    beside = padded[:, 2:] + padded[:, :-2]
    beside = beside + side[:, :, 2:, 1:-1] + side[:, :, :-2, 1:-1]
    beside = beside + side[:, :, 1:-1, 2:] + side[:, :, 1:-1, :-2]
    return 6.0 * center - beside


def per_device(field, modes, send_rows, pick, mode_ids, coef):
    rows_out = send_rows[0]
    count_modes = modes.shape[0]
    flat_modes = modes.reshape(count_modes, -1)
    own_terms, count_slots = pick.shape
    pool_size = rows_out.shape[0]

    def pool_images(values):
        padded = padded_2(values, (("space", 1),), 1)
        outgoing = jnp.take(padded, rows_out, axis=0)
        pool = lax.all_to_all(outgoing, "chaos", split_axis=0, concat_axis=0, tiled=True)
        stencil = laplace(pool)
        return stencil.reshape(pool_size, -1)

    def apply(values):
        images = pool_images(values)
        place = (pick[:, :, None] == jnp.arange(pool_size, dtype=jnp.int32)[None, None, :]).astype(
            jnp.float32
        )
        place = place * coef[:, :, None]
        which = (
            mode_ids[:, :, None] == jnp.arange(count_modes, dtype=jnp.int32)[None, None, :]
        ).astype(jnp.float32)
        weights = jnp.einsum("isp,isk->ikp", place, which, precision=lax.Precision.HIGHEST)
        mixed = jnp.dot(
            weights.reshape(own_terms * count_modes, pool_size),
            images,
            precision=lax.Precision.HIGHEST,
            preferred_element_type=jnp.float32,
        )
        mixed = mixed.reshape(own_terms, count_modes, -1)
        result = jnp.sum(mixed * flat_modes[None], axis=1)
        return result.reshape(values.shape)

    first = apply(field)
    second = apply(first)
    return (first, second)


def solution(mesh):
    in_specs = (
        P("chaos", "space", None, None),
        P(None, "space", None, None),
        P("chaos", None),
        P("chaos", None),
        P("chaos", None),
        P("chaos", None),
    )
    out_specs = (P("chaos", "space", None, None), P("chaos", "space", None, None))
    return jax.shard_map(
        per_device, mesh=mesh, in_specs=in_specs, out_specs=out_specs, check_vma=False
    )
```

profile of v0, /device:TPU:0, one launch (start us, length us, event | category | flops | bytes accessed | tf_op | source)
XLA Modules:
  0.0 85.4 jit_solution(5836833817701981193)
XLA Ops:
  0.6 0.0 copy-start.1
  0.6 1.1 %fusion.20 = (f32[56,1,8,128]{3,2,1,0:T(8,128)S(1)}, f32[56,1,8,128]{3,2,1,0:T(8,128)S(1)}) fusion(f32[56,2,8,128]{3,2,1,0:T(8,128)} %param.8), kind=kLoop, calls=%fused_computation.43 | loop fusion | bytes 917504 | tf_op jit(solution)/shard_map/slice | solution.py:12
  1.8 4.9 %collective-permute-start = (f32[56,1,8,128]{3,2,1,0:T(8,128)S(1)}, f32[56,1,8,128]{3,2,1,0:T(8,128)S(1)}, u32[]{:S(2)}, u32[]{:S(2)}) collective-permute-start(f32[56,1,8,128]{3,2,1,0:T(8,128)S(1)} %get-tuple-element.5), channel_id=1, source_target_pairs={{0,8},{8,16},{16,24},{1,9},{9,17},{17,25},{2,10},{10,18},{18,26},{... | collective-permute-start | bytes 688136 | tf_op jit(solution)/shard_map/ppermute | solution.py:15
  6.7 1.3 %collective-permute-start.1 = (f32[56,1,8,128]{3,2,1,0:T(8,128)S(1)}, f32[56,1,8,128]{3,2,1,0:T(8,128)S(1)}, u32[]{:S(2)}, u32[]{:S(2)}) collective-permute-start(f32[56,1,8,128]{3,2,1,0:T(8,128)S(1)} %get-tuple-element.6), channel_id=1, source_target_pairs={{8,0},{16,8},{24,16},{9,1},{17,9},{25,17},{10,2},{18,10},{26,18},{... | collective-permute-start | bytes 688136 | tf_op jit(solution)/shard_map/ppermute | solution.py:17
  8.0 0.7 compare_select_fusion
  8.7 0.7 compare_and_fusion
  9.4 2.2 %collective-permute-done = f32[56,1,8,128]{3,2,1,0:T(8,128)S(1)} collective-permute-done((f32[56,1,8,128]{3,2,1,0:T(8,128)S(1)}, f32[56,1,8,128]{3,2,1,0:T(8,128)S(1)}, u32[]{:S(2)}, u32[]{:S(2)}) %collective-permute-start) | collective-permute-done | bytes 229408 | tf_op jit(solution)/shard_map/ppermute | solution.py:15
  11.6 4.1 %collective-permute-done.1 = f32[56,1,8,128]{3,2,1,0:T(8,128)S(1)} collective-permute-done((f32[56,1,8,128]{3,2,1,0:T(8,128)S(1)}, f32[56,1,8,128]{3,2,1,0:T(8,128)S(1)}, u32[]{:S(2)}, u32[]{:S(2)}) %collective-permute-start.1) | collective-permute-done | bytes 229408 | tf_op jit(solution)/shard_map/ppermute | solution.py:17
  15.7 0.0 copy-done.1
  15.7 0.1 pad_maximum_fusion
  15.8 0.6 gather_fusion
  16.4 1.1 %broadcast_select_fusion.1 = f32[64,4,8,128]{3,2,1,0:T(8,128)} fusion(f32[64,4,8,128]{3,2,1,0:T(8,128)S(1)} %gather_fusion, pred[64]{0:T(512)(128)(4,1)S(1)} %compare_and_fusion), kind=kLoop, calls=%fused_computation.34 | loop fusion | flops 262144 | bytes 2097216 | tf_op jit(solution)/shard_map/jit(_take)/select_n | solution.py:42
  17.5 0.0 copy-start.3
  17.5 0.0 copy-start.4
  17.5 0.0 copy-start.5
  17.5 0.0 copy-start.2
  17.5 3.9 %all-to-all-start = ((f32[64,4,8,128]{3,2,1,0:T(8,128)}), f32[64,4,8,128]{3,2,1,0:T(8,128)S(1)}, u32[]{:S(2)}, u32[]{:S(2)}) async-start(f32[64,4,8,128]{3,2,1,0:T(8,128)} %broadcast_select_fusion.1), calls=%async_computation | async-start | bytes 2097152 | tf_op jit(solution)/shard_map/all_to_all | solution.py:43
  21.4 0.0 copy-done.3
  21.4 0.1 copy.9
  21.5 0.0 copy-done.4
  21.5 0.1 copy.8
  21.6 0.0 copy-done.5
  21.6 0.1 copy.10
  21.7 0.0 copy-done.2
  21.7 0.1 copy.13
  21.8 2.0 %fusion = f32[56,21,64]{2,1,0:T(8,128)S(1)} fusion(f32[56,41]{1,0:T(8,128)S(1)} %copy.10, s32[56,41]{1,0:T(8,128)S(1)} %copy.9, s32[56,41]{1,0:T(8,128)S(1)} %copy.8), kind=kOutput, calls=%fused_computation.12 | convolution fusion | flops 37371992 | bytes 328608 | tf_op jit(solution)/shard_map/isp,isk->ikp/dot_general | solution.py:56
  23.8 13.0 %all-to-all-done = f32[64,4,8,128]{3,2,1,0:T(8,128)S(1)} async-done(((f32[64,4,8,128]{3,2,1,0:T(8,128)}), f32[64,4,8,128]{3,2,1,0:T(8,128)S(1)}, u32[]{:S(2)}, u32[]{:S(2)}) %all-to-all-start) | async-done | bytes 1048608 | tf_op jit(solution)/shard_map/all_to_all | solution.py:43
  36.9 0.3 fusion.9
  37.2 0.1 reshape.59
  37.3 8.0 %multiply_reduce_fusion.1 = f32[56,2048]{1,0:T(8,128)S(1)} fusion(f32[21,2048]{1,0:T(8,128)S(1)} %bitcast.27, f32[64,2048,1]{1,0,2:T(8,128)S(1)} %reshape.59, f32[56,21,64]{2,1,0:T(8,128)S(1)} %fusion), kind=kOutput, calls=%fused_computation.3 | convolution fusion | flops 1854390272 | bytes 1456128 | tf_op jit(solution)/shard_map/dot_general | solution.py:57
  45.3 0.1 copy.14
  45.4 0.0 copy-start
  45.5 3.5 %collective-permute-start.2 = (f32[56,1,8,128]{3,2,1,0:T(8,128)S(1)}, f32[56,1,8,128]{3,2,1,0:T(8,128)S(1)}, u32[]{:S(2)}, u32[]{:S(2)}) collective-permute-start(f32[56,1,8,128]{3,2,1,0:T(8,128)S(1)} %get-tuple-element.3), channel_id=1, source_target_pairs={{0,8},{8,16},{16,24},{1,9},{9,17},{17,25},{2,10},{10,18},{18,26},{... | collective-permute-start | bytes 688136 | tf_op jit(solution)/shard_map/ppermute | solution.py:15
  49.0 1.3 %collective-permute-start.3 = (f32[56,1,8,128]{3,2,1,0:T(8,128)S(1)}, f32[56,1,8,128]{3,2,1,0:T(8,128)S(1)}, u32[]{:S(2)}, u32[]{:S(2)}) collective-permute-start(f32[56,1,8,128]{3,2,1,0:T(8,128)S(1)} %get-tuple-element.4), channel_id=1, source_target_pairs={{8,0},{16,8},{24,16},{9,1},{17,9},{25,17},{10,2},{18,10},{26,18},{... | collective-permute-start | bytes 688136 | tf_op jit(solution)/shard_map/ppermute | solution.py:17
  50.3 2.2 %collective-permute-done.2 = f32[56,1,8,128]{3,2,1,0:T(8,128)S(1)} collective-permute-done((f32[56,1,8,128]{3,2,1,0:T(8,128)S(1)}, f32[56,1,8,128]{3,2,1,0:T(8,128)S(1)}, u32[]{:S(2)}, u32[]{:S(2)}) %collective-permute-start.2) | collective-permute-done | bytes 229408 | tf_op jit(solution)/shard_map/ppermute | solution.py:15
  52.5 4.4 %collective-permute-done.3 = f32[56,1,8,128]{3,2,1,0:T(8,128)S(1)} collective-permute-done((f32[56,1,8,128]{3,2,1,0:T(8,128)S(1)}, f32[56,1,8,128]{3,2,1,0:T(8,128)S(1)}, u32[]{:S(2)}, u32[]{:S(2)}) %collective-permute-start.3) | collective-permute-done | bytes 229408 | tf_op jit(solution)/shard_map/ppermute | solution.py:17
  56.9 0.1 pad_maximum_fusion.1
  57.0 0.0 copy-done
  57.0 0.6 gather_fusion.1
  57.6 0.1 broadcast_select_fusion
  57.8 18.2 %all_to_all.10 = f32[64,4,8,128]{3,2,1,0:T(8,128)S(1)} all-to-all(f32[64,4,8,128]{3,2,1,0:T(8,128)S(1)} %broadcast_select_fusion), channel_id=1, replica_groups=mesh['space'=4,'chaos'=8] {'chaos'}, dimensions={0} | all-to-all | bytes 2097152 | tf_op jit(solution)/shard_map/all_to_all | solution.py:43
  76.0 0.3 fusion.14
  76.4 0.1 reshape.60
  76.5 8.1 %multiply_reduce_fusion = f32[56,2048]{1,0:T(8,128)S(1)} fusion(f32[21,2048]{1,0:T(8,128)S(1)} %bitcast.28, f32[64,2048,1]{1,0,2:T(8,128)S(1)} %reshape.60, f32[56,21,64]{2,1,0:T(8,128)S(1)} %fusion), kind=kOutput, calls=%fused_computation.2 | convolution fusion | flops 1854390272 | bytes 1456128 | tf_op jit(solution)/shard_map/dot_general | solution.py:57
  84.5 0.8 copy.15
  (5 shorter events, 0.1 us)
Async XLA Ops:
  0.6 15.1 %copy-start.1 = (f32[56,2,8,128]{3,2,1,0:T(8,128)S(1)}, f32[56,2,8,128]{3,2,1,0:T(8,128)}, u32[]{:S(2)}) copy-start(f32[56,2,8,128]{3,2,1,0:T(8,128)} %param.8) | copy-start | bytes 1376260
  1.8 9.8 %collective-permute-start = (f32[56,1,8,128]{3,2,1,0:T(8,128)S(1)}, f32[56,1,8,128]{3,2,1,0:T(8,128)S(1)}, u32[]{:S(2)}, u32[]{:S(2)}) collective-permute-start(f32[56,1,8,128]{3,2,1,0:T(8,128)S(1)} %get-tuple-element.5), channel_id=1, source_target_pairs={{0,8},{8,16},{16,24},{1,9},{9,17},{17,25},{2,10},{10,18},{18,26},{... | collective-permute-start | bytes 688136 | tf_op jit(solution)/shard_map/ppermute | solution.py:15
  6.7 9.0 %collective-permute-start.1 = (f32[56,1,8,128]{3,2,1,0:T(8,128)S(1)}, f32[56,1,8,128]{3,2,1,0:T(8,128)S(1)}, u32[]{:S(2)}, u32[]{:S(2)}) collective-permute-start(f32[56,1,8,128]{3,2,1,0:T(8,128)S(1)} %get-tuple-element.6), channel_id=1, source_target_pairs={{8,0},{16,8},{24,16},{9,1},{17,9},{25,17},{10,2},{18,10},{26,18},{... | collective-permute-start | bytes 688136 | tf_op jit(solution)/shard_map/ppermute | solution.py:17
  17.5 3.9 %copy-start.3 = (s32[56,41]{0,1:T(8,128)S(1)}, s32[56,41]{0,1:T(8,128)}, u32[]{:S(2)}) copy-start(s32[56,41]{0,1:T(8,128)} %param.11) | copy-start | bytes 27556
  17.5 4.0 %copy-start.4 = (s32[56,41]{0,1:T(8,128)S(1)}, s32[56,41]{0,1:T(8,128)}, u32[]{:S(2)}) copy-start(s32[56,41]{0,1:T(8,128)} %param.12) | copy-start | bytes 27556
  17.5 4.1 %copy-start.5 = (f32[56,41]{0,1:T(8,128)S(1)}, f32[56,41]{0,1:T(8,128)}, u32[]{:S(2)}) copy-start(f32[56,41]{0,1:T(8,128)} %param.13) | copy-start | bytes 27556
  17.5 4.1 %copy-start.2 = (f32[21,2,8,128]{3,2,1,0:T(8,128)S(1)}, f32[21,2,8,128]{3,2,1,0:T(8,128)}, u32[]{:S(2)}) copy-start(f32[21,2,8,128]{3,2,1,0:T(8,128)} %param.9) | copy-start | bytes 516100
  17.5 19.3 %all-to-all-start = ((f32[64,4,8,128]{3,2,1,0:T(8,128)}), f32[64,4,8,128]{3,2,1,0:T(8,128)S(1)}, u32[]{:S(2)}, u32[]{:S(2)}) async-start(f32[64,4,8,128]{3,2,1,0:T(8,128)} %broadcast_select_fusion.1), calls=%async_computation | async-start | bytes 2097152 | tf_op jit(solution)/shard_map/all_to_all | solution.py:43
  45.4 11.6 %copy-start = (f32[7,8,16,128]{3,2,1,0:T(8,128)}, f32[7,8,16,128]{3,2,1,0:T(8,128)S(1)}, u32[]{:S(2)}) copy-start(f32[7,8,16,128]{3,2,1,0:T(8,128)S(1)} %copy.14) | copy-start | bytes 1376260
  45.5 7.0 %collective-permute-start.2 = (f32[56,1,8,128]{3,2,1,0:T(8,128)S(1)}, f32[56,1,8,128]{3,2,1,0:T(8,128)S(1)}, u32[]{:S(2)}, u32[]{:S(2)}) collective-permute-start(f32[56,1,8,128]{3,2,1,0:T(8,128)S(1)} %get-tuple-element.3), channel_id=1, source_target_pairs={{0,8},{8,16},{16,24},{1,9},{9,17},{17,25},{2,10},{10,18},{18,26},{... | collective-permute-start | bytes 688136 | tf_op jit(solution)/shard_map/ppermute | solution.py:15
  49.0 7.9 %collective-permute-start.3 = (f32[56,1,8,128]{3,2,1,0:T(8,128)S(1)}, f32[56,1,8,128]{3,2,1,0:T(8,128)S(1)}, u32[]{:S(2)}, u32[]{:S(2)}) collective-permute-start(f32[56,1,8,128]{3,2,1,0:T(8,128)S(1)} %get-tuple-element.4), channel_id=1, source_target_pairs={{8,0},{16,8},{24,16},{9,1},{17,9},{25,17},{10,2},{18,10},{26,18},{... | collective-permute-start | bytes 688136 | tf_op jit(solution)/shard_map/ppermute | solution.py:17
where the time goes:
time: 85.7 us; the launch traced here: 85.4 us
  waiting for transfers between devices  26 us (30%)
  blocking collectives  18.2 us (21%)
  matrix products  18.1 us (21%)
  starting transfers between devices  14.9 us (17%)
  local copies, waits for them, and re-layouts  3.97 us (5%)
  other arithmetic  3.43 us (4%)
    all_to_all x1, blocking collectives, pool_images(): lax.all_to_all(outgoing, 'chaos', split_axis=0, concat_axis=0, tiled=True)  18.2 us
    dot_general x2, matrix products, apply(): jnp.dot(weights.reshape(own_terms * count_modes, pool_size), images, prec...  16.1 us
    all_to_all x1, waiting for transfers between devices, pool_images(): lax.all_to_all(outgoing, 'chaos', split_axis=0, concat_axis=0, tiled=True)  13 us
    ppermute x2, waiting for transfers between devices, padded_2(): lax.ppermute(head, axis, [((i + 1) % count, i) for i in range(ends)])  8.53 us
    ppermute x2, starting transfers between devices, padded_2(): lax.ppermute(tail, axis, [(i, (i + 1) % count) for i in range(ends)])  8.42 us
    ppermute x2, waiting for transfers between devices, padded_2(): lax.ppermute(tail, axis, [(i, (i + 1) % count) for i in range(ends)])  4.41 us
    all_to_all x1, starting transfers between devices, pool_images(): lax.all_to_all(outgoing, 'chaos', split_axis=0, concat_axis=0, tiled=True)  3.87 us
    ppermute x2, starting transfers between devices, padded_2(): lax.ppermute(head, axis, [((i + 1) % count, i) for i in range(ends)])  2.58 us
  transfers between devices with their start and end apart: 5, of which 5 were waited for; matrix products, arithmetic and copies ran while one was open for 4% of the time, Pallas kernels for 0%

commit v1 on v0

v1 whole, which is shorter than its diff:
```python
import jax
import jax.numpy as jnp
from jax import lax
from jax.sharding import PartitionSpec as P

AXES = ("space", "chaos")


def swaps(slabs, owners, first):
    partner = {}
    for left in range(first, slabs - 1, 2):
        partner[left], partner[left + 1] = left + 1, left
    pairs = []
    for s in range(slabs):
        for d in range(owners):
            other = partner[s] * owners + d if s in partner else s * owners + (d ^ 1)
            pairs.append((s * owners + d, other))
    return pairs


def inplane(values):
    side = jnp.pad(values, ((0, 0), (1, 1), (1, 1)))
    return side[:, 2:, 1:-1] + side[:, :-2, 1:-1] + side[:, 1:-1, 2:] + side[:, 1:-1, :-2]


def body(slabs, owners, field, modes, send_rows, pick, mode_ids, coef):
    space, own = lax.axis_index("space"), lax.axis_index("chaos")
    own_terms, slots = pick.shape
    count_modes = modes.shape[0]
    pool_size = send_rows.shape[1]
    cap = pool_size // owners
    chips = owners // 2
    plane = field.shape[2:]
    cells = plane[0] * plane[1]
    pairs_a, pairs_b = swaps(slabs, owners, 0), swaps(slabs, owners, 1)

    odd = space % 2 == 1
    has_a = jnp.where(odd, True, space + 1 < slabs)
    has_b = jnp.where(odd, space + 1 < slabs, space > 0)

    def split(array):
        return jnp.where(odd, array[:, 0], array[:, 1]), jnp.where(odd, array[:, 1], array[:, 0])

    def merge(near, far):
        return jnp.stack([jnp.where(odd, near, far), jnp.where(odd, far, near)], axis=1)

    order = own ^ jnp.arange(owners, dtype=jnp.int32)
    rows = jnp.take(send_rows[0].reshape(owners, cap), order, axis=0)
    place_of = ((pick // cap) ^ own) * cap + pick % cap
    place = (place_of[:, :, None] == jnp.arange(pool_size, dtype=jnp.int32)).astype(jnp.float32)
    place = place * coef[:, :, None]
    which = (mode_ids[:, :, None] == jnp.arange(count_modes, dtype=jnp.int32)).astype(jnp.float32)
    weights = jnp.einsum("isp,isk->ikp", place, which, precision=lax.Precision.HIGHEST)
    weights = weights.reshape(own_terms * count_modes, pool_size)
    mode_planes = jnp.stack(split(modes), axis=1).reshape(count_modes, 2 * cells)

    def apply(near, far):
        halo_a = lax.ppermute(near, AXES, pairs_a)
        halo_b = lax.ppermute(far, AXES, pairs_b)
        image_near = 6.0 * near - inplane(near) - far - jnp.where(has_a, halo_a, 0.0)
        image_far = 6.0 * far - inplane(far) - near - jnp.where(has_b, halo_b, 0.0)
        images = jnp.stack([image_near, image_far], axis=1)
        mine = jnp.take(images, rows[0::2].reshape(-1), axis=0).reshape(chips, cap, 2, *plane)
        others = jnp.take(images, rows[1::2].reshape(-1), axis=0).reshape(chips, cap, 2, *plane)
        others = lax.ppermute(others, "chaos", [(i, i ^ 1) for i in range(owners)])
        blocks = jnp.stack([mine, others], axis=1)
        arrived = [blocks[0]]
        for m in range(1, chips):
            arrived.append(lax.ppermute(blocks[m], "chaos", [(i, i ^ (2 * m)) for i in range(owners)]))
        pool = jnp.concatenate(arrived, axis=0).reshape(pool_size, 2 * cells)
        mixed = jnp.dot(
            weights, pool, precision=lax.Precision.HIGHEST, preferred_element_type=jnp.float32
        ).reshape(own_terms, count_modes, 2 * cells)
        result = jnp.sum(mixed * mode_planes[None], axis=1).reshape(own_terms, 2, *plane)
        return result[:, 0], result[:, 1]

    first = apply(*split(field))
    second = apply(*first)
    return merge(*first), merge(*second)


def solution(mesh):
    slabs, owners = mesh.shape["space"], mesh.shape["chaos"]

    def per_device(*args):
        return body(slabs, owners, *args)

    in_specs = (
        P("chaos", "space", None, None),
        P(None, "space", None, None),
        P("chaos", None),
        P("chaos", None),
        P("chaos", None),
        P("chaos", None),
    )
    out_specs = (P("chaos", "space", None, None), P("chaos", "space", None, None))
    return jax.shard_map(
        per_device, mesh=mesh, in_specs=in_specs, out_specs=out_specs, check_vma=False
    )
```

time: 85.7 us -> 66 us (0.77)
  blocking collectives: 18.2 us -> 0 us
  waiting for transfers between devices: 26 us -> 19.6 us
  local copies, waits for them, and re-layouts: 3.97 us -> 6.43 us
  starting transfers between devices: 14.9 us -> 17.2 us
    all_to_all x1 -> x0, blocking collectives: 18.2 us -> none  [pool_images(): lax.all_to_all(outgoing, 'chaos', split_axis=0, concat_axis=0, tiled=True)]
    all_to_all x1 -> x0, waiting for transfers between devices: 13 us -> none  [pool_images(): lax.all_to_all(outgoing, 'chaos', split_axis=0, concat_axis=0, tiled=True)]
    ppermute x4 -> x12, waiting for transfers between devices: 12.9 us -> 19.6 us  [the longest x6 9.46 us: apply(): lax.ppermute(blocks[m], 'chaos', [(i, i ^ 2 * m) for i in range(owners)])]
    ppermute x4 -> x12, starting transfers between devices: 11 us -> 17.2 us  [the longest x2 9.72 us: apply(): halo_a = lax.ppermute(near, AXES, pairs_a)]
    all_to_all x1 -> x0, starting transfers between devices: 3.87 us -> none  [pool_images(): lax.all_to_all(outgoing, 'chaos', split_axis=0, concat_axis=0, tiled=True)]
    gather x2 -> x5, local copies, waits for them, and re-layouts: 1.27 us -> 2.88 us  [the longest x2 1.16 us: apply(): jnp.take(images, rows[0::2].reshape(-1), axis=0)]
    unnamed x19 -> x21, local copies, waits for them, and re-layouts: 1.29 us -> 2.8 us
    slice x4 -> x2, local copies, waits for them, and re-layouts: 1.24 us -> 0.04 us  [the longest x1 0.02 us: apply(): rows[1::2].reshape(-1)]
  transfers between devices with their start and end apart: 5 -> 12, of which waited for: 5 -> 9; matrix products, arithmetic and copies ran while one was open for 4% -> 11% of each run, Pallas kernels for 0% -> 0%
where the time goes in v1:
time: 66 us; the launch traced here: 65.8 us
  waiting for transfers between devices  19.6 us (30%)
  matrix products  18.1 us (27%)
  starting transfers between devices  17.2 us (26%)
  local copies, waits for them, and re-layouts  6.43 us (10%)
  other arithmetic  3.47 us (5%)
  between operations  1.03 us (2%)
    dot_general x2, matrix products, apply(): jnp.dot(weights, pool, precision=lax.Precision.HIGHEST, preferred_element...  16.1 us
    ppermute x2, starting transfers between devices, apply(): halo_a = lax.ppermute(near, AXES, pairs_a)  9.72 us
    ppermute x6, waiting for transfers between devices, apply(): lax.ppermute(blocks[m], 'chaos', [(i, i ^ 2 * m) for i in range(owners)])  9.46 us
    ppermute x2, waiting for transfers between devices, apply(): halo_a = lax.ppermute(near, AXES, pairs_a)  7.99 us
    ppermute x6, starting transfers between devices, apply(): lax.ppermute(blocks[m], 'chaos', [(i, i ^ 2 * m) for i in range(owners)])  7.11 us
    unnamed x21, local copies, waits for them, and re-layouts  2.8 us
    dot_general x1, matrix products, body(): jnp.einsum('isp,isk->ikp', place, which, precision=lax.Precision.HIGHEST)  1.98 us
    ppermute x2, waiting for transfers between devices, apply(): halo_b = lax.ppermute(far, AXES, pairs_b)  1.41 us
  transfers between devices with their start and end apart: 12, of which 9 were waited for; matrix products, arithmetic and copies ran while one was open for 11% of the time, Pallas kernels for 0%

profile of v1, /device:TPU:0, one launch (start us, length us, event | category | flops | bytes accessed | tf_op | source)
XLA Modules:
  0.0 65.8 jit_solution(9470463890435202700)
XLA Ops:
  0.6 0.0 copy-start.5
  0.6 0.0 copy-start.1
  0.7 1.1 %fusion.36 = f32[56,8,128]{2,1,0:T(8,128)S(1)} fusion(f32[56,2,8,128]{3,2,1,0:T(8,128)} %param.8, pred[]{:T(512)S(6)} %eq.18), kind=kLoop, calls=%fused_computation.85 | loop fusion | flops 57344 | bytes 688129 | tf_op jit(solution)/shard_map/jit(_where)/select_n | solution.py:42
  1.8 3.1 %collective-permute-start = (f32[56,8,128]{2,1,0:T(8,128)S(1)}, f32[56,8,128]{2,1,0:T(8,128)S(1)}, u32[]{:S(2)}, u32[]{:S(2)}) collective-permute-start(f32[56,8,128]{2,1,0:T(8,128)S(1)} %fusion.36), channel_id=1, source_target_pairs={{0,8},{1,9},{2,10},{3,11},{4,12},{5,13},{6,14},{7,15},{8,0},{9,1},... | collective-permute-start | bytes 688136 | tf_op jit(solution)/shard_map/ppermute | solution.py:58
  4.9 0.5 broadcast.117
  5.4 0.7 %reduce.3 = s32[64]{0:T(128)S(1)} reduce(s32[1,64]{1,0:T(1,128)S(1)} %copy-done.5, s32[]{:T(128)} %broadcast.117), dimensions={0}, to_apply=%param.10.reduce_sub_computation.3 | reduce | bytes 516 | tf_op args[2]
  6.1 0.1 reshape_squeeze.3
  6.2 0.6 gather_fusion
  6.8 0.1 broadcast_select_fusion.4
  6.9 0.1 reshape.72
  7.0 0.1 reshape.71
  7.1 0.0 copy-start.2
  7.2 3.4 %collective-permute-done = f32[56,8,128]{2,1,0:T(8,128)S(1)} collective-permute-done((f32[56,8,128]{2,1,0:T(8,128)S(1)}, f32[56,8,128]{2,1,0:T(8,128)S(1)}, u32[]{:S(2)}, u32[]{:S(2)}) %collective-permute-start) | collective-permute-done | bytes 229408 | tf_op jit(solution)/shard_map/ppermute | solution.py:58
  10.5 0.2 fusion.14
  10.7 0.1 collective-permute-start.1
  10.9 1.4 %collective-permute-done.1 = f32[56,8,128]{2,1,0:T(8,128)S(1)} collective-permute-done((f32[56,8,128]{2,1,0:T(8,128)S(1)}, f32[56,8,128]{2,1,0:T(8,128)S(1)}, u32[]{:S(2)}, u32[]{:S(2)}) %collective-permute-start.1) | collective-permute-done | bytes 229408 | tf_op jit(solution)/shard_map/ppermute | solution.py:59
  12.3 0.2 fusion.21
  12.5 0.6 gather_fusion.2
  13.1 0.1 broadcast_select_fusion.2
  13.2 0.0 copy-start.3
  13.2 0.0 copy-start.4
  13.2 0.1 copy.45
  13.3 0.2 collective-permute-start.2
  13.6 0.1 copy.63
  13.6 0.1 copy.41
  13.7 0.2 copy-done.3
  14.0 0.1 copy.40
  14.0 0.1 copy.42
  14.1 0.6 gather_fusion.1
  14.7 0.1 broadcast_select_fusion.3
  14.8 0.1 copy.46
  14.9 0.0 collective-permute-done.2
  15.0 1.7 %collective-permute-start.3 = (f32[2,8,2,8,128]{4,1,3,2,0:T(8,128)S(1)}, f32[2,8,2,8,128]{4,1,3,2,0:T(8,128)S(1)}, u32[]{:S(2)}, u32[]{:S(2)}) collective-permute-start(f32[2,8,2,8,128]{4,1,3,2,0:T(8,128)S(1)} %get-tuple-element.14), channel_id=1, source_target_pairs={{0,2},{1,3},{2,0},{3,1},{4,6},{5,7},{6,4},{7,5},{8,10},{9,11},{10,... | collective-permute-start | bytes 393224 | tf_op jit(solution)/shard_map/ppermute | solution.py:69
  16.7 1.5 %collective-permute-start.4 = (f32[2,8,2,8,128]{4,1,3,2,0:T(8,128)S(1)}, f32[2,8,2,8,128]{4,1,3,2,0:T(8,128)S(1)}, u32[]{:S(2)}, u32[]{:S(2)}) collective-permute-start(f32[2,8,2,8,128]{4,1,3,2,0:T(8,128)S(1)} %get-tuple-element.16), channel_id=1, source_target_pairs={{0,4},{1,5},{2,6},{3,7},{4,0},{5,1},{6,2},{7,3},{8,12},{9,13},{10,... | collective-permute-start | bytes 393224 | tf_op jit(solution)/shard_map/ppermute | solution.py:69
  18.2 0.3 collective-permute-start.5
  18.5 2.0 %fusion = f32[56,21,64]{2,1,0:T(8,128)S(1)} fusion(f32[56,41]{1,0:T(8,128)S(1)} %copy.42, s32[56,41]{1,0:T(8,128)S(1)} %copy.41, s32[56,41]{1,0:T(8,128)S(1)} %copy.40), kind=kOutput, calls=%fused_computation.23 | convolution fusion | flops 37371992 | bytes 328608 | tf_op jit(solution)/shard_map/isp,isk->ikp/dot_general | solution.py:53
  20.5 0.2 collective-permute-done.3
  20.8 4.0 %collective-permute-done.4 = f32[2,8,2,8,128]{4,1,3,2,0:T(8,128)S(1)} collective-permute-done((f32[2,8,2,8,128]{4,1,3,2,0:T(8,128)S(1)}, f32[2,8,2,8,128]{4,1,3,2,0:T(8,128)S(1)}, u32[]{:S(2)}, u32[]{:S(2)}) %collective-permute-start.4) | collective-permute-done | bytes 131104 | tf_op jit(solution)/shard_map/ppermute | solution.py:69
  24.8 0.0 collective-permute-done.5
  24.8 8.0 %multiply_reduce_fusion.1 = f32[56,2048]{1,0:T(8,128)S(1)} fusion(f32[21,2048]{1,0:T(8,128)S(1)} %bitcast.117, f32[64,2048,1]{1,0,2:T(8,128)S(1)} %bitcast.112, f32[56,21,64]{2,1,0:T(8,128)S(1)} %fusion), kind=kOutput, calls=%fused_computation.6 | convolution fusion | flops 1854390272 | bytes 1456128 | tf_op jit(solution)/shard_map/dot_general | solution.py:71
  32.9 0.1 copy.64
  33.0 6.6 %collective-permute-start.6 = (f32[56,8,128]{2,1,0:T(8,128)S(1)}, f32[56,8,128]{2,1,0:T(8,128)S(1)}, u32[]{:S(2)}, u32[]{:S(2)}) collective-permute-start(f32[56,8,128]{2,1,0:T(8,128)S(1)} %get-tuple-element.21), channel_id=1, source_target_pairs={{0,8},{1,9},{2,10},{3,11},{4,12},{5,13},{6,14},{7,15},{8,0},{9,1},... | collective-permute-start | bytes 688136 | tf_op jit(solution)/shard_map/ppermute | solution.py:58
  39.6 0.0 collective-permute-start.7
  39.6 4.6 %collective-permute-done.6 = f32[56,8,128]{2,1,0:T(8,128)S(1)} collective-permute-done((f32[56,8,128]{2,1,0:T(8,128)S(1)}, f32[56,8,128]{2,1,0:T(8,128)S(1)}, u32[]{:S(2)}, u32[]{:S(2)}) %collective-permute-start.6) | collective-permute-done | bytes 229408 | tf_op jit(solution)/shard_map/ppermute | solution.py:58
  44.3 0.0 collective-permute-done.7
  44.3 0.3 fusion.28
  44.6 0.6 gather_fusion.4
  45.2 0.1 broadcast_select_fusion
  45.3 0.1 copy.51
  45.4 0.1 collective-permute-start.8
  45.5 0.6 gather_fusion.3
  46.1 0.1 broadcast_select_fusion.1
  46.2 0.1 copy.52
  46.3 0.7 %collective-permute-done.8 = f32[4,8,2,8,128]{4,1,3,2,0:T(8,128)S(1)} collective-permute-done((f32[4,8,2,8,128]{4,1,3,2,0:T(8,128)S(1)}, f32[4,8,2,8,128]{4,1,3,2,0:T(8,128)S(1)}, u32[]{:S(2)}, u32[]{:S(2)}) %collective-permute-start.8) | collective-permute-done | bytes 262176 | tf_op jit(solution)/shard_map/ppermute | solution.py:65
  47.1 1.7 %collective-permute-start.10 = (f32[2,8,2,8,128]{4,1,3,2,0:T(8,128)S(1)}, f32[2,8,2,8,128]{4,1,3,2,0:T(8,128)S(1)}, u32[]{:S(2)}, u32[]{:S(2)}) collective-permute-start(f32[2,8,2,8,128]{4,1,3,2,0:T(8,128)S(1)} %get-tuple-element.12), channel_id=1, source_target_pairs={{0,4},{1,5},{2,6},{3,7},{4,0},{5,1},{6,2},{7,3},{8,12},{9,13},{10,... | collective-permute-start | bytes 393224 | tf_op jit(solution)/shard_map/ppermute | solution.py:69
  48.8 1.5 %collective-permute-start.11 = (f32[2,8,2,8,128]{4,1,3,2,0:T(8,128)S(1)}, f32[2,8,2,8,128]{4,1,3,2,0:T(8,128)S(1)}, u32[]{:S(2)}, u32[]{:S(2)}) collective-permute-start(f32[2,8,2,8,128]{4,1,3,2,0:T(8,128)S(1)} %get-tuple-element.11), channel_id=1, source_target_pairs={{0,6},{1,7},{2,4},{3,5},{4,2},{5,3},{6,0},{7,1},{8,14},{9,15},{10,... | collective-permute-start | bytes 393224 | tf_op jit(solution)/shard_map/ppermute | solution.py:69
  50.3 0.4 collective-permute-start.9
  50.7 0.8 %copy.56 = f32[56,2,8,128]{3,2,1,0:T(8,128)} copy(f32[56,2,8,128]{3,2,0,1:T(8,128)S(1)} %pad_maximum_fusion.3) | data formatting | bytes 917504
  51.5 3.4 %collective-permute-done.10 = f32[2,8,2,8,128]{4,1,3,2,0:T(8,128)S(1)} collective-permute-done((f32[2,8,2,8,128]{4,1,3,2,0:T(8,128)S(1)}, f32[2,8,2,8,128]{4,1,3,2,0:T(8,128)S(1)}, u32[]{:S(2)}, u32[]{:S(2)}) %collective-permute-start.10) | collective-permute-done | bytes 131104 | tf_op jit(solution)/shard_map/ppermute | solution.py:69
  54.9 1.2 %collective-permute-done.11 = f32[2,8,2,8,128]{4,1,3,2,0:T(8,128)S(1)} collective-permute-done((f32[2,8,2,8,128]{4,1,3,2,0:T(8,128)S(1)}, f32[2,8,2,8,128]{4,1,3,2,0:T(8,128)S(1)}, u32[]{:S(2)}, u32[]{:S(2)}) %collective-permute-start.11) | collective-permute-done | bytes 131104 | tf_op jit(solution)/shard_map/ppermute | solution.py:69
  56.1 0.7 collective-permute-done.9
  56.7 8.0 %multiply_reduce_fusion = f32[56,2048]{1,0:T(8,128)S(1)} fusion(f32[21,2048]{1,0:T(8,128)S(1)} %bitcast.118, f32[64,2048,1]{1,0,2:T(8,128)S(1)} %bitcast.111, f32[56,21,64]{2,1,0:T(8,128)S(1)} %fusion), kind=kOutput, calls=%fused_computation.5 | convolution fusion | flops 1854390272 | bytes 1456128 | tf_op jit(solution)/shard_map/dot_general | solution.py:71
  64.8 0.1 copy.65
  65.0 0.8 %copy.57 = f32[56,2,8,128]{3,2,1,0:T(8,128)} copy(f32[56,2,8,128]{3,2,0,1:T(8,128)S(1)} %pad_maximum_fusion.5) | data formatting | bytes 917504
  (32 shorter events, 0.6 us)
Async XLA Ops:
  0.6 4.8 %copy-start.5 = (s32[1,64]{1,0:T(1,128)S(1)}, s32[1,64]{1,0:T(1,128)}, u32[]{:S(2)}) copy-start(s32[1,64]{1,0:T(1,128)} %param.10) | copy-start | bytes 772
  0.6 6.4 %copy-start.1 = (f32[21,2,8,128]{3,2,1,0:T(8,128)S(1)}, f32[21,2,8,128]{3,2,1,0:T(8,128)}, u32[]{:S(2)}) copy-start(f32[21,2,8,128]{3,2,1,0:T(8,128)} %param.9) | copy-start | bytes 516100
  0.7 9.8 %copy-start = (f32[56,2,8,128]{3,2,1,0:T(8,128)S(1)}, f32[56,2,8,128]{3,2,1,0:T(8,128)}, u32[]{:S(2)}) copy-start(f32[56,2,8,128]{3,2,1,0:T(8,128)} %param.8) | copy-start | bytes 1376260
  1.8 8.7 %collective-permute-start = (f32[56,8,128]{2,1,0:T(8,128)S(1)}, f32[56,8,128]{2,1,0:T(8,128)S(1)}, u32[]{:S(2)}, u32[]{:S(2)}) collective-permute-start(f32[56,8,128]{2,1,0:T(8,128)S(1)} %fusion.36), channel_id=1, source_target_pairs={{0,8},{1,9},{2,10},{3,11},{4,12},{5,13},{6,14},{7,15},{8,0},{9,1},... | collective-permute-start | bytes 688136 | tf_op jit(solution)/shard_map/ppermute | solution.py:58
  7.1 3.7 %copy-start.2 = (s32[56,41]{0,1:T(8,128)S(1)}, s32[56,41]{0,1:T(8,128)}, u32[]{:S(2)}) copy-start(s32[56,41]{0,1:T(8,128)} %param.11) | copy-start | bytes 27556
  10.7 1.6 %collective-permute-start.1 = (f32[56,8,128]{2,1,0:T(8,128)S(1)}, f32[56,8,128]{2,1,0:T(8,128)S(1)}, u32[]{:S(2)}, u32[]{:S(2)}) collective-permute-start(f32[56,8,128]{2,1,0:T(8,128)S(1)} %get-tuple-element.8), channel_id=1, source_target_pairs={{0,1},{1,0},{2,3},{3,2},{4,5},{5,4},{6,7},{7,6},{8,16},{9,17},{10,... | collective-permute-start | bytes 688136 | tf_op jit(solution)/shard_map/ppermute | solution.py:59
  13.2 0.7 %copy-start.3 = (s32[56,41]{0,1:T(8,128)S(1)}, s32[56,41]{0,1:T(8,128)}, u32[]{:S(2)}) copy-start(s32[56,41]{0,1:T(8,128)} %param.12) | copy-start | bytes 27556
  13.2 0.8 %copy-start.4 = (f32[56,41]{0,1:T(8,128)S(1)}, f32[56,41]{0,1:T(8,128)}, u32[]{:S(2)}) copy-start(f32[56,41]{0,1:T(8,128)} %param.13) | copy-start | bytes 27556
  13.3 1.6 %collective-permute-start.2 = (f32[4,8,2,8,128]{4,1,3,2,0:T(8,128)S(1)}, f32[4,8,2,8,128]{4,1,3,2,0:T(8,128)S(1)}, u32[]{:S(2)}, u32[]{:S(2)}) collective-permute-start(f32[4,8,2,8,128]{4,1,3,2,0:T(8,128)S(1)} %copy.45), channel_id=1, source_target_pairs={{0,1},{1,0},{2,3},{3,2},{4,5},{5,4},{6,7},{7,6},{8,9},{9,8},{10,11... | collective-permute-start | bytes 786440 | tf_op jit(solution)/shard_map/ppermute | solution.py:65
  15.0 5.8 %collective-permute-start.3 = (f32[2,8,2,8,128]{4,1,3,2,0:T(8,128)S(1)}, f32[2,8,2,8,128]{4,1,3,2,0:T(8,128)S(1)}, u32[]{:S(2)}, u32[]{:S(2)}) collective-permute-start(f32[2,8,2,8,128]{4,1,3,2,0:T(8,128)S(1)} %get-tuple-element.14), channel_id=1, source_target_pairs={{0,2},{1,3},{2,0},{3,1},{4,6},{5,7},{6,4},{7,5},{8,10},{9,11},{10,... | collective-permute-start | bytes 393224 | tf_op jit(solution)/shard_map/ppermute | solution.py:69
  16.7 8.1 %collective-permute-start.4 = (f32[2,8,2,8,128]{4,1,3,2,0:T(8,128)S(1)}, f32[2,8,2,8,128]{4,1,3,2,0:T(8,128)S(1)}, u32[]{:S(2)}, u32[]{:S(2)}) collective-permute-start(f32[2,8,2,8,128]{4,1,3,2,0:T(8,128)S(1)} %get-tuple-element.16), channel_id=1, source_target_pairs={{0,4},{1,5},{2,6},{3,7},{4,0},{5,1},{6,2},{7,3},{8,12},{9,13},{10,... | collective-permute-start | bytes 393224 | tf_op jit(solution)/shard_map/ppermute | solution.py:69
  18.2 6.6 %collective-permute-start.5 = (f32[2,8,2,8,128]{4,1,3,2,0:T(8,128)S(1)}, f32[2,8,2,8,128]{4,1,3,2,0:T(8,128)S(1)}, u32[]{:S(2)}, u32[]{:S(2)}) collective-permute-start(f32[2,8,2,8,128]{4,1,3,2,0:T(8,128)S(1)} %get-tuple-element.15), channel_id=1, source_target_pairs={{0,6},{1,7},{2,4},{3,5},{4,2},{5,3},{6,0},{7,1},{8,14},{9,15},{10,... | collective-permute-start | bytes 393224 | tf_op jit(solution)/shard_map/ppermute | solution.py:69
  33.0 11.3 %collective-permute-start.6 = (f32[56,8,128]{2,1,0:T(8,128)S(1)}, f32[56,8,128]{2,1,0:T(8,128)S(1)}, u32[]{:S(2)}, u32[]{:S(2)}) collective-permute-start(f32[56,8,128]{2,1,0:T(8,128)S(1)} %get-tuple-element.21), channel_id=1, source_target_pairs={{0,8},{1,9},{2,10},{3,11},{4,12},{5,13},{6,14},{7,15},{8,0},{9,1},... | collective-permute-start | bytes 688136 | tf_op jit(solution)/shard_map/ppermute | solution.py:58
  39.6 4.6 %collective-permute-start.7 = (f32[56,8,128]{2,1,0:T(8,128)S(1)}, f32[56,8,128]{2,1,0:T(8,128)S(1)}, u32[]{:S(2)}, u32[]{:S(2)}) collective-permute-start(f32[56,8,128]{2,1,0:T(8,128)S(1)} %get-tuple-element.22), channel_id=1, source_target_pairs={{0,1},{1,0},{2,3},{3,2},{4,5},{5,4},{6,7},{7,6},{8,16},{9,17},{10,... | collective-permute-start | bytes 688136 | tf_op jit(solution)/shard_map/ppermute | solution.py:59
  45.4 1.6 %collective-permute-start.8 = (f32[4,8,2,8,128]{4,1,3,2,0:T(8,128)S(1)}, f32[4,8,2,8,128]{4,1,3,2,0:T(8,128)S(1)}, u32[]{:S(2)}, u32[]{:S(2)}) collective-permute-start(f32[4,8,2,8,128]{4,1,3,2,0:T(8,128)S(1)} %copy.51), channel_id=1, source_target_pairs={{0,1},{1,0},{2,3},{3,2},{4,5},{5,4},{6,7},{7,6},{8,9},{9,8},{10,11... | collective-permute-start | bytes 786440 | tf_op jit(solution)/shard_map/ppermute | solution.py:65
  47.1 7.8 %collective-permute-start.10 = (f32[2,8,2,8,128]{4,1,3,2,0:T(8,128)S(1)}, f32[2,8,2,8,128]{4,1,3,2,0:T(8,128)S(1)}, u32[]{:S(2)}, u32[]{:S(2)}) collective-permute-start(f32[2,8,2,8,128]{4,1,3,2,0:T(8,128)S(1)} %get-tuple-element.12), channel_id=1, source_target_pairs={{0,4},{1,5},{2,6},{3,7},{4,0},{5,1},{6,2},{7,3},{8,12},{9,13},{10,... | collective-permute-start | bytes 393224 | tf_op jit(solution)/shard_map/ppermute | solution.py:69
  48.8 7.3 %collective-permute-start.11 = (f32[2,8,2,8,128]{4,1,3,2,0:T(8,128)S(1)}, f32[2,8,2,8,128]{4,1,3,2,0:T(8,128)S(1)}, u32[]{:S(2)}, u32[]{:S(2)}) collective-permute-start(f32[2,8,2,8,128]{4,1,3,2,0:T(8,128)S(1)} %get-tuple-element.11), channel_id=1, source_target_pairs={{0,6},{1,7},{2,4},{3,5},{4,2},{5,3},{6,0},{7,1},{8,14},{9,15},{10,... | collective-permute-start | bytes 393224 | tf_op jit(solution)/shard_map/ppermute | solution.py:69
  50.3 6.4 %collective-permute-start.9 = (f32[2,8,2,8,128]{4,1,3,2,0:T(8,128)S(1)}, f32[2,8,2,8,128]{4,1,3,2,0:T(8,128)S(1)}, u32[]{:S(2)}, u32[]{:S(2)}) collective-permute-start(f32[2,8,2,8,128]{4,1,3,2,0:T(8,128)S(1)} %get-tuple-element.10), channel_id=1, source_target_pairs={{0,2},{1,3},{2,0},{3,1},{4,6},{5,7},{6,4},{7,5},{8,10},{9,11},{10,... | collective-permute-start | bytes 393224 | tf_op jit(solution)/shard_map/ppermute | solution.py:69

commit v2 on v1

v2 whole, which is shorter than its diff:
```python
import functools

import jax
import jax.numpy as jnp
from jax import lax
from jax.experimental import pallas as pl
from jax.experimental.pallas import tpu as pltpu
from jax.sharding import PartitionSpec as P

AXES = ("space", "chaos")
VMEM = pl.BlockSpec(memory_space=pltpu.VMEM)
SMEM = pl.BlockSpec(memory_space=pltpu.SMEM)
LIMIT = 32 * 1024 * 1024


def swaps(slabs, owners, first):
    partner = {}
    for left in range(first, slabs - 1, 2):
        partner[left], partner[left + 1] = left + 1, left
    pairs = []
    for s in range(slabs):
        for d in range(owners):
            other = partner[s] * owners + d if s in partner else s * owners + (d ^ 1)
            pairs.append((s * owners + d, other))
    return pairs


def images_kernel(parity, chips, cap, info, rows, near, far, halo_a, halo_b, out):
    own, has_a, has_b = info[0], info[1] > 0, info[2] > 0
    gx, gy = near.shape[1:]
    sub = lax.broadcasted_iota(jnp.int32, (gx, gy), 0)
    lane = lax.broadcasted_iota(jnp.int32, (gx, gy), 1)
    zero = jnp.zeros((gx, gy), jnp.float32)

    def laplace(center, other, halo):
        beside = jnp.where(sub > 0, pltpu.roll(center, 1, 0), zero)
        beside = beside + jnp.where(sub < gx - 1, pltpu.roll(center, gx - 1, 0), zero)
        beside = beside + jnp.where(lane > 0, pltpu.roll(center, 1, 1), zero)
        beside = beside + jnp.where(lane < gy - 1, pltpu.roll(center, gy - 1, 1), zero)
        return 6.0 * center - (beside + (other + halo))

    for chip in range(chips):
        start = (own ^ (2 * chip + parity)) * cap
        for c in range(cap):
            term = rows[0, start + c]
            a, b = near[term], far[term]
            ha = jnp.where(has_a, halo_a[term], zero)
            hb = jnp.where(has_b, halo_b[term], zero)
            base = chip * 2 * gx * cap + c
            out[pl.ds(base, gx, stride=cap), :] = laplace(a, b, ha)
            out[pl.ds(base + gx * cap, gx, stride=cap), :] = laplace(b, a, hb)


def images(parity, chips, cap, info, rows, near, far, halo_a, halo_b):
    gx, gy = near.shape[1:]
    out = pl.pallas_call(
        functools.partial(images_kernel, parity, chips, cap),
        out_shape=jax.ShapeDtypeStruct((chips * 2 * gx * cap, gy), jnp.float32),
        in_specs=[SMEM, SMEM, VMEM, VMEM, VMEM, VMEM],
        out_specs=VMEM,
        compiler_params=pltpu.CompilerParams(vmem_limit_bytes=LIMIT),
        cost_estimate=pl.CostEstimate(flops=chips * 2 * gx * cap * gy * 8, bytes_accessed=1 << 20, transcendentals=0),
        name=f"images_{parity}",
    )(info, rows, near, far, halo_a, halo_b)
    return out.reshape(chips, 2, gx, cap, gy)


def product_kernel(plane, count_modes, weights, modes, *rest):
    blocks, out = rest[:-1], rest[-1]
    gx, gy = modes.shape[1:]
    own_terms = weights.shape[0] // count_modes

    def column(g):
        parts = [block[half, plane, g] for block in blocks for half in range(2)]
        full = jnp.concatenate(parts, axis=0)
        high = full.astype(jnp.bfloat16)
        low = (full - high.astype(jnp.float32)).astype(jnp.bfloat16)
        return jnp.concatenate([high, low, high], axis=0)

    for g in range(0, gx, 2):
        pool = jnp.concatenate([column(g), column(g + 1)], axis=1)
        mixed = jnp.dot(weights[...], pool, preferred_element_type=jnp.float32)
        for side in range(2):
            total = jnp.zeros((own_terms, gy), jnp.float32)
            for k in range(count_modes):
                part = mixed[k * own_terms : (k + 1) * own_terms, side * gy : (side + 1) * gy]
                total = total + part * modes[k, pl.ds(g + side, 1), :]
            out[pl.ds(g + side, own_terms, stride=gx), :] = total


def product(plane, weights, modes, blocks):
    count_modes, gx, gy = modes.shape
    own_terms = weights.shape[0] // count_modes
    out = pl.pallas_call(
        functools.partial(product_kernel, plane, count_modes),
        out_shape=jax.ShapeDtypeStruct((own_terms * gx, gy), jnp.float32),
        in_specs=[VMEM] * (2 + len(blocks)),
        out_specs=VMEM,
        compiler_params=pltpu.CompilerParams(vmem_limit_bytes=LIMIT),
        cost_estimate=pl.CostEstimate(
            flops=2 * weights.shape[0] * weights.shape[1] * gx * gy, bytes_accessed=1 << 20, transcendentals=0
        ),
        name=f"product_{plane}",
    )(weights, modes, *blocks)
    return out.reshape(own_terms, gx, gy)


def body(slabs, owners, field, modes, send_rows, pick, mode_ids, coef):
    space, own = lax.axis_index("space"), lax.axis_index("chaos")
    own_terms = pick.shape[0]
    count_modes = modes.shape[0]
    pool_size = send_rows.shape[1]
    cap = pool_size // owners
    chips = owners // 2
    pairs_a, pairs_b = swaps(slabs, owners, 0), swaps(slabs, owners, 1)

    odd = space % 2 == 1
    near_at = jnp.where(odd, 0, 1)
    has_a = jnp.where(odd, True, space + 1 < slabs)
    has_b = jnp.where(odd, space + 1 < slabs, space > 0)
    info = jnp.stack([own, has_a.astype(jnp.int32), has_b.astype(jnp.int32)]).astype(jnp.int32)

    def split(array):
        return (
            lax.dynamic_index_in_dim(array, near_at, 1, keepdims=False),
            lax.dynamic_index_in_dim(array, 1 - near_at, 1, keepdims=False),
        )

    def merge(near, far):
        return jnp.stack([jnp.where(odd, near, far), jnp.where(odd, far, near)], axis=1)

    place_of = ((pick // cap) ^ own) * cap + pick % cap
    place = (place_of[:, :, None] == jnp.arange(pool_size, dtype=jnp.int32)).astype(jnp.float32)
    place = place * coef[:, :, None]
    which = (mode_ids[:, :, None] == jnp.arange(count_modes, dtype=jnp.int32)).astype(jnp.float32)
    weights = jnp.einsum("isp,isk->kip", place, which, precision=lax.Precision.HIGHEST)
    weights = weights.reshape(count_modes * own_terms, pool_size)
    high = lax.reduce_precision(weights, 8, 7)
    weights = jnp.concatenate([high, high, weights - high], axis=1).astype(jnp.bfloat16)
    mode_planes = split(modes)

    def apply(near, far):
        halo_a = lax.ppermute(near, AXES, pairs_a)
        halo_b = lax.ppermute(far, AXES, pairs_b)
        inputs = (info, send_rows, near, far, halo_a, halo_b)
        others = images(1, chips, cap, *inputs)
        others = lax.ppermute(others, "chaos", [(i, i ^ 1) for i in range(owners)])
        mine = images(0, chips, cap, *inputs)
        blocks = [jnp.stack([mine[m], others[m]]) for m in range(chips)]
        for m in range(1, chips):
            blocks[m] = lax.ppermute(blocks[m], "chaos", [(i, i ^ (2 * m)) for i in range(owners)])
        return tuple(product(plane, weights, mode_planes[plane], blocks) for plane in range(2))

    first = apply(*split(field))
    second = apply(*first)
    return merge(*first), merge(*second)


def solution(mesh):
    slabs, owners = mesh.shape["space"], mesh.shape["chaos"]

    def per_device(*args):
        return body(slabs, owners, *args)

    in_specs = (
        P("chaos", "space", None, None),
        P(None, "space", None, None),
        P("chaos", None),
        P("chaos", None),
        P("chaos", None),
        P("chaos", None),
    )
    out_specs = (P("chaos", "space", None, None), P("chaos", "space", None, None))
    return jax.shard_map(
        per_device, mesh=mesh, in_specs=in_specs, out_specs=out_specs, check_vma=False
    )
```

time: 66 us -> 48.2 us (0.73)
  matrix products: 18.1 us -> 1.98 us
  Pallas kernels: 0 us -> 6.22 us
  local copies, waits for them, and re-layouts: 6.43 us -> 1.57 us
  starting transfers between devices: 17.2 us -> 14.8 us
  other arithmetic: 3.47 us -> 1.65 us
  waiting for transfers between devices: 19.6 us -> 20.9 us
    dot_general x3 -> x1, matrix products: 18.1 us -> 1.98 us  [body(): jnp.einsum('isp,isk->kip', place, which, precision=lax.Precision.HIGHEST)]
    pallas_call x0 -> x8, Pallas kernels: none -> 6.22 us  [the longest x4 3.19 us: product(): pl.pallas_call(functools.partial(product_kernel, plane, count_modes), out...]
    ppermute x2, starting transfers between devices: 9.72 us -> 6.73 us  [apply(): halo_a = lax.ppermute(near, AXES, pairs_a)]
    gather x5 -> x0, local copies, waits for them, and re-layouts: 2.88 us -> none  [the longest x2 1.16 us: apply(): jnp.take(images, rows[0::2].reshape(-1), axis=0)]
    unnamed x21 -> x12, local copies, waits for them, and re-layouts: 2.8 us -> 0.19 us
    ppermute x6, waiting for transfers between devices: 9.46 us -> 11.6 us  [apply(): lax.ppermute(blocks[m], 'chaos', [(i, i ^ 2 * m) for i in range(owners)])]
    select_n x10 -> x0, other arithmetic: 1.65 us -> none  [the longest x2 1.15 us: split(): jnp.where(odd, array[:, 0], array[:, 1])]
    ppermute x2, waiting for transfers between devices: 1.41 us -> 0.01 us  [apply(): halo_b = lax.ppermute(far, AXES, pairs_b)]
  transfers between devices with their start and end apart: 12 -> 12, of which waited for: 9 -> 9; matrix products, arithmetic and copies ran while one was open for 11% -> 6% of each run, Pallas kernels for 0% -> 5%
where the time goes in v2:
time: 48.2 us; the launch traced here: 48 us
  waiting for transfers between devices  20.9 us (43%)
  starting transfers between devices  14.8 us (31%)
  Pallas kernels  6.22 us (13%)
  matrix products  1.98 us (4%)
  other arithmetic  1.65 us (3%)
  local copies, waits for them, and re-layouts  1.57 us (3%)
  between operations  0.9 us (2%)
    ppermute x6, waiting for transfers between devices, apply(): lax.ppermute(blocks[m], 'chaos', [(i, i ^ 2 * m) for i in range(owners)])  11.6 us
    ppermute x2, waiting for transfers between devices, apply(): halo_a = lax.ppermute(near, AXES, pairs_a)  8.18 us
    ppermute x6, starting transfers between devices, apply(): lax.ppermute(blocks[m], 'chaos', [(i, i ^ 2 * m) for i in range(owners)])  7.36 us
    ppermute x2, starting transfers between devices, apply(): halo_a = lax.ppermute(near, AXES, pairs_a)  6.73 us
    pallas_call x4, Pallas kernels, product(): pl.pallas_call(functools.partial(product_kernel, plane, count_modes), out...  3.19 us
    pallas_call x4, Pallas kernels, images(): pl.pallas_call(functools.partial(images_kernel, parity, chips, cap), out_...  3.03 us
    dot_general x1, matrix products, body(): jnp.einsum('isp,isk->kip', place, which, precision=lax.Precision.HIGHEST)  1.98 us
    ppermute x2, waiting for transfers between devices, apply(): others = lax.ppermute(others, 'chaos', [(i, i ^ 1) for i in range(owners)])  1.14 us
  transfers between devices with their start and end apart: 12, of which 9 were waited for; matrix products, arithmetic and copies ran while one was open for 6% of the time, Pallas kernels for 5%

profile of v2, /device:TPU:0, one launch (start us, length us, event | category | flops | bytes accessed | tf_op | source)
XLA Modules:
  0.0 48.0 jit_solution(11283984924944058262)
XLA Ops:
  0.6 0.0 copy-start.2
  0.6 0.0 copy-start.3
  0.7 0.0 copy-start.4
  0.7 1.1 %dynamic-slice_bitcast_fusion = (f32[56,8,128]{2,1,0:T(8,128)S(1)}, f32[56,8,128]{2,1,0:T(8,128)S(1)}) fusion(f32[56,2,8,128]{3,2,1,0:T(8,128)} %param.6, s32[]{:T(128)S(6)} %select_n.105, s32[]{:T(128)S(6)} %select_n.102), kind=kLoop, calls=%fused_computation.19 | loop fusion | bytes 917512 | tf_op jit(solution)/shard_map/jit(dynamic_index_in_dim)/squeeze | solution.py:126
  1.8 0.5 %collective-permute-start.1 = (f32[56,8,128]{2,1,0:T(8,128)S(1)}, f32[56,8,128]{2,1,0:T(8,128)S(1)}, u32[]{:S(2)}, u32[]{:S(2)}) collective-permute-start(f32[56,8,128]{2,1,0:T(8,128)S(1)} %get-tuple-element.8.far), channel_id=1, source_target_pairs={{0,1},{1,0},{2,3},{3,2},{4,5},{5,4},{6,7},{7,6},{8,16},{9,17},{10,... | collective-permute-start | bytes 688136 | tf_op jit(solution)/shard_map/ppermute | solution.py:144
  2.3 4.1 %collective-permute-start = (f32[56,8,128]{2,1,0:T(8,128)S(1)}, f32[56,8,128]{2,1,0:T(8,128)S(1)}, u32[]{:S(2)}, u32[]{:S(2)}) collective-permute-start(f32[56,8,128]{2,1,0:T(8,128)S(1)} %get-tuple-element.9.near), channel_id=1, source_target_pairs={{0,8},{1,9},{2,10},{3,11},{4,12},{5,13},{6,14},{7,15},{8,0},{9,1},... | collective-permute-start | bytes 688136 | tf_op jit(solution)/shard_map/ppermute | solution.py:143
  6.4 0.0 copy-done.2
  6.5 0.1 copy.9
  6.6 0.0 copy-done.3
  6.6 0.1 copy.8
  6.6 0.0 copy-done.4
  6.6 0.1 copy.10
  6.7 2.0 %fusion.2 = f32[21,56,64]{2,0,1:T(8,128)S(1)} fusion(f32[56,41]{1,0:T(8,128)S(1)} %copy.10, s32[56,41]{1,0:T(8,128)S(1)} %copy.9, s32[56,41]{1,0:T(8,128)S(1)} %copy.8), kind=kOutput, calls=%fused_computation.3 | convolution fusion | flops 37371992 | bytes 328608 | tf_op jit(solution)/shard_map/isp,isk->kip/dot_general | solution.py:136
  8.7 0.1 copy.11
  8.8 0.0 copy-start
  8.9 0.1 reduce-precision_convert_fusion
  9.0 0.1 pad_add_fusion.info
  9.1 0.0 collective-permute-done.1.halo_b
  9.1 2.7 %collective-permute-done.halo_a = f32[56,8,128]{2,1,0:T(8,128)S(1)} collective-permute-done((f32[56,8,128]{2,1,0:T(8,128)S(1)}, f32[56,8,128]{2,1,0:T(8,128)S(1)}, u32[]{:S(2)}, u32[]{:S(2)}) %collective-permute-start) | collective-permute-done | bytes 229408 | tf_op jit(solution)/shard_map/ppermute | solution.py:143
  11.8 0.0 copy-done
  11.8 0.8 %images_1.2 = f32[512,128]{1,0:T(8,128)S(1)} custom-call(s32[3]{0:T(128)S(1)} %pad_add_fusion.info, s32[1,64]{1,0:T(1,128)S(1)} %copy-done, f32[56,8,128]{2,1,0:T(8,128)S(1)} %get-tuple-element.9.near, f32[56,8,128]{2,1,0:T(8,128)S(1)} %get-tuple-element.8.far, f32[56,8,128]{2,1,0:T(8,128)S(1)} %collective-permute-done.halo_a, ...), custom_call_target="tpu_custom_call" | custom-call | flops 524288 | bytes 1048576 | tf_op jit(solution)/shard_map/images_1/pallas_call | solution.py:56
  12.5 0.1 collective-permute-start.2
  12.6 0.3 pad_maximum_fusion.weights
  12.9 0.8 %images_0.2 = f32[512,128]{1,0:T(8,128)S(1)} custom-call(s32[3]{0:T(128)S(1)} %pad_add_fusion.info, s32[1,64]{1,0:T(1,128)S(1)} %copy-done, f32[56,8,128]{2,1,0:T(8,128)S(1)} %get-tuple-element.9.near, f32[56,8,128]{2,1,0:T(8,128)S(1)} %get-tuple-element.8.far, f32[56,8,128]{2,1,0:T(8,128)S(1)} %collective-permute-done.halo_a, ...), custom_call_target="tpu_custom_call" | custom-call | flops 524288 | bytes 1048576 | tf_op jit(solution)/shard_map/images_0/pallas_call | solution.py:56
  13.7 0.0 copy-start.1
  13.7 0.4 collective-permute-done.2
  14.2 1.6 %collective-permute-start.3 = (f32[2,2,8,8,128]{4,3,2,1,0:T(8,128)S(1)}, f32[2,2,8,8,128]{4,3,2,1,0:T(8,128)S(1)}, u32[]{:S(2)}, u32[]{:S(2)}) collective-permute-start(f32[2,2,8,8,128]{4,3,2,1,0:T(8,128)S(1)} %pad_maximum_fusion.4), channel_id=1, source_target_pairs={{0,2},{1,3},{2,0},{3,1},{4,6},{5,7},{6,4},{7,5},{8,10},{9,11},{10,... | collective-permute-start | bytes 393224 | tf_op jit(solution)/shard_map/ppermute | solution.py:151
  15.7 1.6 %collective-permute-start.4 = (f32[2,2,8,8,128]{4,3,2,1,0:T(8,128)S(1)}, f32[2,2,8,8,128]{4,3,2,1,0:T(8,128)S(1)}, u32[]{:S(2)}, u32[]{:S(2)}) collective-permute-start(f32[2,2,8,8,128]{4,3,2,1,0:T(8,128)S(1)} %pad_maximum_fusion.5), channel_id=1, source_target_pairs={{0,4},{1,5},{2,6},{3,7},{4,0},{5,1},{6,2},{7,3},{8,12},{9,13},{10,... | collective-permute-start | bytes 393224 | tf_op jit(solution)/shard_map/ppermute | solution.py:151
  17.3 0.5 %collective-permute-start.5 = (f32[2,2,8,8,128]{4,3,2,1,0:T(8,128)S(1)}, f32[2,2,8,8,128]{4,3,2,1,0:T(8,128)S(1)}, u32[]{:S(2)}, u32[]{:S(2)}) collective-permute-start(f32[2,2,8,8,128]{4,3,2,1,0:T(8,128)S(1)} %pad_maximum_fusion.6), channel_id=1, source_target_pairs={{0,6},{1,7},{2,4},{3,5},{4,2},{5,3},{6,0},{7,1},{8,14},{9,15},{10,... | collective-permute-start | bytes 393224 | tf_op jit(solution)/shard_map/ppermute | solution.py:151
  17.9 0.0 copy-done.1
  17.9 2.0 %collective-permute-done.3.rest_1_ = f32[2,2,8,8,128]{4,3,2,1,0:T(8,128)S(1)} collective-permute-done((f32[2,2,8,8,128]{4,3,2,1,0:T(8,128)S(1)}, f32[2,2,8,8,128]{4,3,2,1,0:T(8,128)S(1)}, u32[]{:S(2)}, u32[]{:S(2)}) %collective-permute-start.3) | collective-permute-done | bytes 131104 | tf_op jit(solution)/shard_map/ppermute | solution.py:151
  20.0 3.9 %collective-permute-done.4.rest_2_ = f32[2,2,8,8,128]{4,3,2,1,0:T(8,128)S(1)} collective-permute-done((f32[2,2,8,8,128]{4,3,2,1,0:T(8,128)S(1)}, f32[2,2,8,8,128]{4,3,2,1,0:T(8,128)S(1)}, u32[]{:S(2)}, u32[]{:S(2)}) %collective-permute-start.4) | collective-permute-done | bytes 131104 | tf_op jit(solution)/shard_map/ppermute | solution.py:151
  23.9 0.0 collective-permute-done.5.rest_3_
  23.9 0.8 %product_1.2 = f32[448,128]{1,0:T(8,128)S(1)} custom-call(bf16[1176,192]{1,0:T(8,128)(2,1)S(1)} %pad_maximum_fusion.weights, f32[21,8,128]{2,1,0:T(8,128)S(1)} %get-tuple-element.27.modes, f32[2,2,8,8,128]{4,3,2,1,0:T(8,128)S(1)} %pad_maximum_fusion.3.rest_0_, f32[2,2,8,8,128]{4,3,2,1,0:T(8,128)S(1)} %collective-permute-done.3.rest_1_, ...), custom_call_target="tpu_custom_call" | custom-call | flops 462422016 | bytes 1048576 | tf_op jit(solution)/shard_map/product_1/pallas_call | solution.py:94
  24.7 0.1 collective-permute-start.7
  24.8 0.8 %product_0.2 = f32[448,128]{1,0:T(8,128)S(1)} custom-call(bf16[1176,192]{1,0:T(8,128)(2,1)S(1)} %pad_maximum_fusion.weights, f32[21,8,128]{2,1,0:T(8,128)S(1)} %get-tuple-element.26.modes, f32[2,2,8,8,128]{4,3,2,1,0:T(8,128)S(1)} %pad_maximum_fusion.3.rest_0_, f32[2,2,8,8,128]{4,3,2,1,0:T(8,128)S(1)} %collective-permute-done.3.rest_1_, ...), custom_call_target="tpu_custom_call" | custom-call | flops 462422016 | bytes 1048576 | tf_op jit(solution)/shard_map/product_0/pallas_call | solution.py:94
  25.6 2.6 %collective-permute-start.6 = (f32[56,8,128]{2,1,0:T(8,128)S(1)}, f32[56,8,128]{2,1,0:T(8,128)S(1)}, u32[]{:S(2)}, u32[]{:S(2)}) collective-permute-start(f32[56,8,128]{2,1,0:T(8,128)S(1)} %bitcast.47), channel_id=1, source_target_pairs={{0,8},{1,9},{2,10},{3,11},{4,12},{5,13},{6,14},{7,15},{8,0},{9,1},... | collective-permute-start | bytes 688136 | tf_op jit(solution)/shard_map/ppermute | solution.py:143
  28.1 0.0 collective-permute-done.7.halo_b
  28.1 5.5 %collective-permute-done.6.halo_a = f32[56,8,128]{2,1,0:T(8,128)S(1)} collective-permute-done((f32[56,8,128]{2,1,0:T(8,128)S(1)}, f32[56,8,128]{2,1,0:T(8,128)S(1)}, u32[]{:S(2)}, u32[]{:S(2)}) %collective-permute-start.6) | collective-permute-done | bytes 229408 | tf_op jit(solution)/shard_map/ppermute | solution.py:143
  33.6 0.8 %images_1.3 = f32[512,128]{1,0:T(8,128)S(1)} custom-call(s32[3]{0:T(128)S(1)} %pad_add_fusion.info, s32[1,64]{1,0:T(1,128)S(1)} %copy-done, f32[56,8,128]{2,1,0:T(8,128)S(1)} %bitcast.48, f32[56,8,128]{2,1,0:T(8,128)S(1)} %bitcast.45, f32[56,8,128]{2,1,0:T(8,128)S(1)} %collective-permute-done.6.halo_a, f32[56,8,128]{2,1,0:T(8,128)S(1)} %collective-permute-done.7.halo_b), custom_call_target="tpu_custom_call" | custom-call | flops 524288 | bytes 1048576 | tf_op jit(solution)/shard_map/images_1/pallas_call | solution.py:56
  34.4 0.1 collective-permute-start.8
  34.5 0.8 %images_0.3 = f32[512,128]{1,0:T(8,128)S(1)} custom-call(s32[3]{0:T(128)S(1)} %pad_add_fusion.info, s32[1,64]{1,0:T(1,128)S(1)} %copy-done, f32[56,8,128]{2,1,0:T(8,128)S(1)} %bitcast.49, f32[56,8,128]{2,1,0:T(8,128)S(1)} %bitcast.46, f32[56,8,128]{2,1,0:T(8,128)S(1)} %collective-permute-done.6.halo_a, f32[56,8,128]{2,1,0:T(8,128)S(1)} %collective-permute-done.7.halo_b), custom_call_target="tpu_custom_call" | custom-call | flops 524288 | bytes 1048576 | tf_op jit(solution)/shard_map/images_0/pallas_call | solution.py:56
  35.3 0.7 %collective-permute-done.8 = f32[4,2,8,8,128]{4,3,2,1,0:T(8,128)S(1)} collective-permute-done((f32[4,2,8,8,128]{4,3,2,1,0:T(8,128)S(1)}, f32[4,2,8,8,128]{4,3,2,1,0:T(8,128)S(1)}, u32[]{:S(2)}, u32[]{:S(2)}) %collective-permute-start.8) | collective-permute-done | bytes 262176 | tf_op jit(solution)/shard_map/ppermute | solution.py:147
  36.0 1.2 %collective-permute-start.9 = (f32[2,2,8,8,128]{4,3,2,1,0:T(8,128)S(1)}, f32[2,2,8,8,128]{4,3,2,1,0:T(8,128)S(1)}, u32[]{:S(2)}, u32[]{:S(2)}) collective-permute-start(f32[2,2,8,8,128]{4,3,2,1,0:T(8,128)S(1)} %pad_maximum_fusion.8), channel_id=1, source_target_pairs={{0,2},{1,3},{2,0},{3,1},{4,6},{5,7},{6,4},{7,5},{8,10},{9,11},{10,... | collective-permute-start | bytes 393224 | tf_op jit(solution)/shard_map/ppermute | solution.py:151
  37.3 1.0 %collective-permute-start.10 = (f32[2,2,8,8,128]{4,3,2,1,0:T(8,128)S(1)}, f32[2,2,8,8,128]{4,3,2,1,0:T(8,128)S(1)}, u32[]{:S(2)}, u32[]{:S(2)}) collective-permute-start(f32[2,2,8,8,128]{4,3,2,1,0:T(8,128)S(1)} %pad_maximum_fusion.9), channel_id=1, source_target_pairs={{0,4},{1,5},{2,6},{3,7},{4,0},{5,1},{6,2},{7,3},{8,12},{9,13},{10,... | collective-permute-start | bytes 393224 | tf_op jit(solution)/shard_map/ppermute | solution.py:151
  38.2 1.5 %collective-permute-start.11 = (f32[2,2,8,8,128]{4,3,2,1,0:T(8,128)S(1)}, f32[2,2,8,8,128]{4,3,2,1,0:T(8,128)S(1)}, u32[]{:S(2)}, u32[]{:S(2)}) collective-permute-start(f32[2,2,8,8,128]{4,3,2,1,0:T(8,128)S(1)} %pad_maximum_fusion.10), channel_id=1, source_target_pairs={{0,6},{1,7},{2,4},{3,5},{4,2},{5,3},{6,0},{7,1},{8,14},{9,15},{10,... | collective-permute-start | bytes 393224 | tf_op jit(solution)/shard_map/ppermute | solution.py:151
  39.8 2.4 %collective-permute-done.9.rest_1_ = f32[2,2,8,8,128]{4,3,2,1,0:T(8,128)S(1)} collective-permute-done((f32[2,2,8,8,128]{4,3,2,1,0:T(8,128)S(1)}, f32[2,2,8,8,128]{4,3,2,1,0:T(8,128)S(1)}, u32[]{:S(2)}, u32[]{:S(2)}) %collective-permute-start.9) | collective-permute-done | bytes 131104 | tf_op jit(solution)/shard_map/ppermute | solution.py:151
  42.2 1.7 %collective-permute-done.10.rest_2_ = f32[2,2,8,8,128]{4,3,2,1,0:T(8,128)S(1)} collective-permute-done((f32[2,2,8,8,128]{4,3,2,1,0:T(8,128)S(1)}, f32[2,2,8,8,128]{4,3,2,1,0:T(8,128)S(1)}, u32[]{:S(2)}, u32[]{:S(2)}) %collective-permute-start.10) | collective-permute-done | bytes 131104 | tf_op jit(solution)/shard_map/ppermute | solution.py:151
  43.9 1.5 %collective-permute-done.11.rest_3_ = f32[2,2,8,8,128]{4,3,2,1,0:T(8,128)S(1)} collective-permute-done((f32[2,2,8,8,128]{4,3,2,1,0:T(8,128)S(1)}, f32[2,2,8,8,128]{4,3,2,1,0:T(8,128)S(1)}, u32[]{:S(2)}, u32[]{:S(2)}) %collective-permute-start.11) | collective-permute-done | bytes 131104 | tf_op jit(solution)/shard_map/ppermute | solution.py:151
  45.4 0.8 %product_1.3 = f32[448,128]{1,0:T(8,128)S(1)} custom-call(bf16[1176,192]{1,0:T(8,128)(2,1)S(1)} %pad_maximum_fusion.weights, f32[21,8,128]{2,1,0:T(8,128)S(1)} %get-tuple-element.27.modes, f32[2,2,8,8,128]{4,3,2,1,0:T(8,128)S(1)} %pad_maximum_fusion.7.rest_0_, f32[2,2,8,8,128]{4,3,2,1,0:T(8,128)S(1)} %collective-permute-done.9.rest_1_, ...), custom_call_target="tpu_custom_call" | custom-call | flops 462422016 | bytes 1048576 | tf_op jit(solution)/shard_map/product_1/pallas_call | solution.py:94
  46.2 0.8 %product_0.3 = f32[448,128]{1,0:T(8,128)S(1)} custom-call(bf16[1176,192]{1,0:T(8,128)(2,1)S(1)} %pad_maximum_fusion.weights, f32[21,8,128]{2,1,0:T(8,128)S(1)} %get-tuple-element.26.modes, f32[2,2,8,8,128]{4,3,2,1,0:T(8,128)S(1)} %pad_maximum_fusion.7.rest_0_, f32[2,2,8,8,128]{4,3,2,1,0:T(8,128)S(1)} %collective-permute-done.9.rest_1_, ...), custom_call_target="tpu_custom_call" | custom-call | flops 462422016 | bytes 1048576 | tf_op jit(solution)/shard_map/product_0/pallas_call | solution.py:94
  47.1 1.0 %pad_maximum_fusion.1 = (f32[56,2,8,128]{3,2,1,0:T(8,128)}, f32[56,2,8,128]{3,2,1,0:T(8,128)}) fusion(f32[56,1,8,128]{3,2,1,0:T(8,128)S(1)} %get-tuple-element.7, f32[56,1,8,128]{3,2,1,0:T(8,128)S(1)} %get-tuple-element.6, f32[56,1,8,128]{3,2,1,0:T(8,128)S(1)} %get-tuple-element.5, f32[56,1,8,128]{3,2,1,0:T(8,128)S(1)} %get-tuple-element.4), kind=kLoop, calls=%fused_computation.12 | loop fusion | flops 229376 | bytes 1835008 | tf_op jit(solution)/shard_map/stack | solution.py:130
  (16 shorter events, 0.3 us)
Async XLA Ops:
  0.6 5.8 %copy-start.2 = (s32[56,41]{0,1:T(8,128)S(1)}, s32[56,41]{0,1:T(8,128)}, u32[]{:S(2)}) copy-start(s32[56,41]{0,1:T(8,128)} %param.9) | copy-start | bytes 27556
  0.6 5.9 %copy-start.3 = (s32[56,41]{0,1:T(8,128)S(1)}, s32[56,41]{0,1:T(8,128)}, u32[]{:S(2)}) copy-start(s32[56,41]{0,1:T(8,128)} %param.10) | copy-start | bytes 27556
  0.7 6.0 %copy-start.4 = (f32[56,41]{0,1:T(8,128)S(1)}, f32[56,41]{0,1:T(8,128)}, u32[]{:S(2)}) copy-start(f32[56,41]{0,1:T(8,128)} %param.11) | copy-start | bytes 27556
  1.8 7.3 %collective-permute-start.1 = (f32[56,8,128]{2,1,0:T(8,128)S(1)}, f32[56,8,128]{2,1,0:T(8,128)S(1)}, u32[]{:S(2)}, u32[]{:S(2)}) collective-permute-start(f32[56,8,128]{2,1,0:T(8,128)S(1)} %get-tuple-element.8.far), channel_id=1, source_target_pairs={{0,1},{1,0},{2,3},{3,2},{4,5},{5,4},{6,7},{7,6},{8,16},{9,17},{10,... | collective-permute-start | bytes 688136 | tf_op jit(solution)/shard_map/ppermute | solution.py:144
  2.3 9.5 %collective-permute-start = (f32[56,8,128]{2,1,0:T(8,128)S(1)}, f32[56,8,128]{2,1,0:T(8,128)S(1)}, u32[]{:S(2)}, u32[]{:S(2)}) collective-permute-start(f32[56,8,128]{2,1,0:T(8,128)S(1)} %get-tuple-element.9.near), channel_id=1, source_target_pairs={{0,8},{1,9},{2,10},{3,11},{4,12},{5,13},{6,14},{7,15},{8,0},{9,1},... | collective-permute-start | bytes 688136 | tf_op jit(solution)/shard_map/ppermute | solution.py:143
  8.8 2.9 %copy-start = (s32[1,64]{1,0:T(1,128)S(1)}, s32[1,64]{1,0:T(1,128)}, u32[]{:S(2)}) copy-start(s32[1,64]{1,0:T(1,128)} %rows.7) | copy-start | bytes 772
  12.5 1.6 %collective-permute-start.2 = (f32[4,2,8,8,128]{4,3,2,1,0:T(8,128)S(1)}, f32[4,2,8,8,128]{4,3,2,1,0:T(8,128)S(1)}, u32[]{:S(2)}, u32[]{:S(2)}) collective-permute-start(f32[4,2,8,8,128]{4,3,2,1,0:T(8,128)S(1)} %bitcast.50), channel_id=1, source_target_pairs={{0,1},{1,0},{2,3},{3,2},{4,5},{5,4},{6,7},{7,6},{8,9},{9,8},{10,11... | collective-permute-start | bytes 786440 | tf_op jit(solution)/shard_map/ppermute | solution.py:147
  13.7 4.2 %copy-start.1 = (f32[21,2,8,128]{3,2,1,0:T(8,128)S(1)}, f32[21,2,8,128]{3,2,1,0:T(8,128)}, u32[]{:S(2)}) copy-start(f32[21,2,8,128]{3,2,1,0:T(8,128)} %param.7) | copy-start | bytes 516100
  14.2 5.8 %collective-permute-start.3 = (f32[2,2,8,8,128]{4,3,2,1,0:T(8,128)S(1)}, f32[2,2,8,8,128]{4,3,2,1,0:T(8,128)S(1)}, u32[]{:S(2)}, u32[]{:S(2)}) collective-permute-start(f32[2,2,8,8,128]{4,3,2,1,0:T(8,128)S(1)} %pad_maximum_fusion.4), channel_id=1, source_target_pairs={{0,2},{1,3},{2,0},{3,1},{4,6},{5,7},{6,4},{7,5},{8,10},{9,11},{10,... | collective-permute-start | bytes 393224 | tf_op jit(solution)/shard_map/ppermute | solution.py:151
  15.7 8.1 %collective-permute-start.4 = (f32[2,2,8,8,128]{4,3,2,1,0:T(8,128)S(1)}, f32[2,2,8,8,128]{4,3,2,1,0:T(8,128)S(1)}, u32[]{:S(2)}, u32[]{:S(2)}) collective-permute-start(f32[2,2,8,8,128]{4,3,2,1,0:T(8,128)S(1)} %pad_maximum_fusion.5), channel_id=1, source_target_pairs={{0,4},{1,5},{2,6},{3,7},{4,0},{5,1},{6,2},{7,3},{8,12},{9,13},{10,... | collective-permute-start | bytes 393224 | tf_op jit(solution)/shard_map/ppermute | solution.py:151
  17.3 6.5 %collective-permute-start.5 = (f32[2,2,8,8,128]{4,3,2,1,0:T(8,128)S(1)}, f32[2,2,8,8,128]{4,3,2,1,0:T(8,128)S(1)}, u32[]{:S(2)}, u32[]{:S(2)}) collective-permute-start(f32[2,2,8,8,128]{4,3,2,1,0:T(8,128)S(1)} %pad_maximum_fusion.6), channel_id=1, source_target_pairs={{0,6},{1,7},{2,4},{3,5},{4,2},{5,3},{6,0},{7,1},{8,14},{9,15},{10,... | collective-permute-start | bytes 393224 | tf_op jit(solution)/shard_map/ppermute | solution.py:151
  24.7 3.5 %collective-permute-start.7 = (f32[56,8,128]{2,1,0:T(8,128)S(1)}, f32[56,8,128]{2,1,0:T(8,128)S(1)}, u32[]{:S(2)}, u32[]{:S(2)}) collective-permute-start(f32[56,8,128]{2,1,0:T(8,128)S(1)} %bitcast.44), channel_id=1, source_target_pairs={{0,1},{1,0},{2,3},{3,2},{4,5},{5,4},{6,7},{7,6},{8,16},{9,17},{10,... | collective-permute-start | bytes 688136 | tf_op jit(solution)/shard_map/ppermute | solution.py:144
  25.6 8.1 %collective-permute-start.6 = (f32[56,8,128]{2,1,0:T(8,128)S(1)}, f32[56,8,128]{2,1,0:T(8,128)S(1)}, u32[]{:S(2)}, u32[]{:S(2)}) collective-permute-start(f32[56,8,128]{2,1,0:T(8,128)S(1)} %bitcast.47), channel_id=1, source_target_pairs={{0,8},{1,9},{2,10},{3,11},{4,12},{5,13},{6,14},{7,15},{8,0},{9,1},... | collective-permute-start | bytes 688136 | tf_op jit(solution)/shard_map/ppermute | solution.py:143
  34.4 1.6 %collective-permute-start.8 = (f32[4,2,8,8,128]{4,3,2,1,0:T(8,128)S(1)}, f32[4,2,8,8,128]{4,3,2,1,0:T(8,128)S(1)}, u32[]{:S(2)}, u32[]{:S(2)}) collective-permute-start(f32[4,2,8,8,128]{4,3,2,1,0:T(8,128)S(1)} %bitcast.51), channel_id=1, source_target_pairs={{0,1},{1,0},{2,3},{3,2},{4,5},{5,4},{6,7},{7,6},{8,9},{9,8},{10,11... | collective-permute-start | bytes 786440 | tf_op jit(solution)/shard_map/ppermute | solution.py:147
  36.0 6.1 %collective-permute-start.9 = (f32[2,2,8,8,128]{4,3,2,1,0:T(8,128)S(1)}, f32[2,2,8,8,128]{4,3,2,1,0:T(8,128)S(1)}, u32[]{:S(2)}, u32[]{:S(2)}) collective-permute-start(f32[2,2,8,8,128]{4,3,2,1,0:T(8,128)S(1)} %pad_maximum_fusion.8), channel_id=1, source_target_pairs={{0,2},{1,3},{2,0},{3,1},{4,6},{5,7},{6,4},{7,5},{8,10},{9,11},{10,... | collective-permute-start | bytes 393224 | tf_op jit(solution)/shard_map/ppermute | solution.py:151
  37.3 6.6 %collective-permute-start.10 = (f32[2,2,8,8,128]{4,3,2,1,0:T(8,128)S(1)}, f32[2,2,8,8,128]{4,3,2,1,0:T(8,128)S(1)}, u32[]{:S(2)}, u32[]{:S(2)}) collective-permute-start(f32[2,2,8,8,128]{4,3,2,1,0:T(8,128)S(1)} %pad_maximum_fusion.9), channel_id=1, source_target_pairs={{0,4},{1,5},{2,6},{3,7},{4,0},{5,1},{6,2},{7,3},{8,12},{9,13},{10,... | collective-permute-start | bytes 393224 | tf_op jit(solution)/shard_map/ppermute | solution.py:151
  38.2 7.2 %collective-permute-start.11 = (f32[2,2,8,8,128]{4,3,2,1,0:T(8,128)S(1)}, f32[2,2,8,8,128]{4,3,2,1,0:T(8,128)S(1)}, u32[]{:S(2)}, u32[]{:S(2)}) collective-permute-start(f32[2,2,8,8,128]{4,3,2,1,0:T(8,128)S(1)} %pad_maximum_fusion.10), channel_id=1, source_target_pairs={{0,6},{1,7},{2,4},{3,5},{4,2},{5,3},{6,0},{7,1},{8,14},{9,15},{10,... | collective-permute-start | bytes 393224 | tf_op jit(solution)/shard_map/ppermute | solution.py:151

commit v3 on v2

--- a/solution.py
+++ b/solution.py
@@ -9,6 +9,7 @@
 
 AXES = ("space", "chaos")
 VMEM = pl.BlockSpec(memory_space=pltpu.VMEM)
+ANY = pl.BlockSpec(memory_space=pl.ANY)
 SMEM = pl.BlockSpec(memory_space=pltpu.SMEM)
 LIMIT = 32 * 1024 * 1024
 
@@ -25,48 +26,51 @@
     return pairs
 
 
-def images_kernel(parity, chips, cap, info, rows, near, far, halo_a, halo_b, out):
-    own, has_a, has_b = info[0], info[1] > 0, info[2] > 0
-    gx, gy = near.shape[1:]
+def images_kernel(plane, parities, chips, cap, rows, flags, center, other, halo, *rest):
+    outs = rest[-len(parities) :]
+    gx, gy = center.shape[1:]
     sub = lax.broadcasted_iota(jnp.int32, (gx, gy), 0)
     lane = lax.broadcasted_iota(jnp.int32, (gx, gy), 1)
     zero = jnp.zeros((gx, gy), jnp.float32)
+    inside = flags[pl.ds(plane, 1), :] > 0
+    terms = rows[...]
 
-    def laplace(center, other, halo):
-        beside = jnp.where(sub > 0, pltpu.roll(center, 1, 0), zero)
-        beside = beside + jnp.where(sub < gx - 1, pltpu.roll(center, gx - 1, 0), zero)
-        beside = beside + jnp.where(lane > 0, pltpu.roll(center, 1, 1), zero)
-        beside = beside + jnp.where(lane < gy - 1, pltpu.roll(center, gy - 1, 1), zero)
-        return 6.0 * center - (beside + (other + halo))
+    def laplace(term):
+        middle = center[term]
+        beside = jnp.where(sub > 0, pltpu.roll(middle, 1, 0), zero)
+        beside = beside + jnp.where(sub < gx - 1, pltpu.roll(middle, gx - 1, 0), zero)
+        beside = beside + jnp.where(lane > 0, pltpu.roll(middle, 1, 1), zero)
+        beside = beside + jnp.where(lane < gy - 1, pltpu.roll(middle, gy - 1, 1), zero)
+        beside = beside + (other[term] + jnp.where(inside, halo[term], zero))
+        return 6.0 * middle - beside
 
-    for chip in range(chips):
-        start = (own ^ (2 * chip + parity)) * cap
-        for c in range(cap):
-            term = rows[0, start + c]
-            a, b = near[term], far[term]
-            ha = jnp.where(has_a, halo_a[term], zero)
-            hb = jnp.where(has_b, halo_b[term], zero)
-            base = chip * 2 * gx * cap + c
-            out[pl.ds(base, gx, stride=cap), :] = laplace(a, b, ha)
-            out[pl.ds(base + gx * cap, gx, stride=cap), :] = laplace(b, a, hb)
+    for parity, out in zip(parities, outs):
+        for chip in range(chips):
+            at = (2 * chip + parity) * cap
+            made = [laplace(terms[0, at + c]) for c in range(cap)]
+            for c in range(cap):
+                out[pl.ds((chip * 2 + plane) * gx * cap + c, gx, stride=cap), :] = made[c]
 
 
-def images(parity, chips, cap, info, rows, near, far, halo_a, halo_b):
-    gx, gy = near.shape[1:]
-    out = pl.pallas_call(
-        functools.partial(images_kernel, parity, chips, cap),
-        out_shape=jax.ShapeDtypeStruct((chips * 2 * gx * cap, gy), jnp.float32),
-        in_specs=[SMEM, SMEM, VMEM, VMEM, VMEM, VMEM],
-        out_specs=VMEM,
+def images(plane, parities, chips, cap, rows, flags, center, other, halo, partial=()):
+    gx, gy = center.shape[1:]
+    out = jax.ShapeDtypeStruct((chips * 2 * gx * cap, gy), jnp.float32)
+    return pl.pallas_call(
+        functools.partial(images_kernel, plane, parities, chips, cap),
+        out_shape=[out] * len(parities),
+        in_specs=[VMEM] * (5 + len(partial)),
+        out_specs=[VMEM] * len(parities),
+        input_output_aliases={5 + i: i for i in range(len(partial))},
         compiler_params=pltpu.CompilerParams(vmem_limit_bytes=LIMIT),
-        cost_estimate=pl.CostEstimate(flops=chips * 2 * gx * cap * gy * 8, bytes_accessed=1 << 20, transcendentals=0),
-        name=f"images_{parity}",
-    )(info, rows, near, far, halo_a, halo_b)
-    return out.reshape(chips, 2, gx, cap, gy)
+        cost_estimate=pl.CostEstimate(
+            flops=len(parities) * chips * gx * cap * gy * 8, bytes_accessed=1 << 19, transcendentals=0
+        ),
+        name=f"images_{plane}_{len(parities)}_{parities[0]}",
+    )(rows, flags, center, other, halo, *partial)
 
 
-def product_kernel(plane, count_modes, weights, modes, *rest):
-    blocks, out = rest[:-1], rest[-1]
+def product_kernel(plane, count_modes, order, weights, modes, *rest):
+    blocks, out = [rest[order.index(m)] for m in range(len(order))], rest[-1]
     gx, gy = modes.shape[1:]
     own_terms = weights.shape[0] // count_modes
 
@@ -88,20 +92,20 @@
             out[pl.ds(g + side, own_terms, stride=gx), :] = total
 
 
-def product(plane, weights, modes, blocks):
+def product(plane, weights, modes, blocks, order, after=()):
     count_modes, gx, gy = modes.shape
     own_terms = weights.shape[0] // count_modes
     out = pl.pallas_call(
-        functools.partial(product_kernel, plane, count_modes),
+        functools.partial(product_kernel, plane, count_modes, order),
         out_shape=jax.ShapeDtypeStruct((own_terms * gx, gy), jnp.float32),
-        in_specs=[VMEM] * (2 + len(blocks)),
+        in_specs=[VMEM] * (2 + len(blocks)) + [ANY] * len(after),
         out_specs=VMEM,
         compiler_params=pltpu.CompilerParams(vmem_limit_bytes=LIMIT),
         cost_estimate=pl.CostEstimate(
             flops=2 * weights.shape[0] * weights.shape[1] * gx * gy, bytes_accessed=1 << 20, transcendentals=0
         ),
         name=f"product_{plane}",
-    )(weights, modes, *blocks)
+    )(weights, modes, *[blocks[m] for m in order], *after)
     return out.reshape(own_terms, gx, gy)
 
 
@@ -118,7 +122,7 @@
     near_at = jnp.where(odd, 0, 1)
     has_a = jnp.where(odd, True, space + 1 < slabs)
     has_b = jnp.where(odd, space + 1 < slabs, space > 0)
-    info = jnp.stack([own, has_a.astype(jnp.int32), has_b.astype(jnp.int32)]).astype(jnp.int32)
+    flags = jnp.broadcast_to(jnp.stack([has_a, has_b]).astype(jnp.int32)[:, None], (2, field.shape[3]))
 
     def split(array):
         return (
@@ -129,6 +133,7 @@
     def merge(near, far):
         return jnp.stack([jnp.where(odd, near, far), jnp.where(odd, far, near)], axis=1)
 
+    rows = jnp.take(send_rows.reshape(owners, cap), own ^ jnp.arange(owners), axis=0).reshape(1, pool_size)
     place_of = ((pick // cap) ^ own) * cap + pick % cap
     place = (place_of[:, :, None] == jnp.arange(pool_size, dtype=jnp.int32)).astype(jnp.float32)
     place = place * coef[:, :, None]
@@ -142,14 +147,17 @@
     def apply(near, far):
         halo_a = lax.ppermute(near, AXES, pairs_a)
         halo_b = lax.ppermute(far, AXES, pairs_b)
-        inputs = (info, send_rows, near, far, halo_a, halo_b)
-        others = images(1, chips, cap, *inputs)
-        others = lax.ppermute(others, "chaos", [(i, i ^ 1) for i in range(owners)])
-        mine = images(0, chips, cap, *inputs)
+        first_plane = images(0, (1, 0), chips, cap, rows, flags, near, far, halo_a)
+        (others,) = images(1, (1,), chips, cap, rows, flags, far, near, halo_b, first_plane[:1])
+        shape = (chips, 2, field.shape[2], cap, field.shape[3])
+        others = lax.ppermute(others.reshape(shape), "chaos", [(i, i ^ 1) for i in range(owners)])
+        (mine,) = images(1, (0,), chips, cap, rows, flags, far, near, halo_b, first_plane[1:])
+        mine = mine.reshape(shape)
         blocks = [jnp.stack([mine[m], others[m]]) for m in range(chips)]
-        for m in range(1, chips):
+        order = sorted(range(chips), key=lambda m: (m > 0, -bin(m).count("1"), m))
+        for m in order[1:]:
             blocks[m] = lax.ppermute(blocks[m], "chaos", [(i, i ^ (2 * m)) for i in range(owners)])
-        return tuple(product(plane, weights, mode_planes[plane], blocks) for plane in range(2))
+        return tuple(product(plane, weights, mode_planes[plane], blocks, order) for plane in range(2))
 
     first = apply(*split(field))
     second = apply(*first)

time: 48.2 us -> 45.8 us (0.950)
  starting transfers between devices: 14.8 us -> 12.9 us
  waiting for transfers between devices: 20.9 us -> 19.4 us
  local copies, waits for them, and re-layouts: 1.57 us -> 2.87 us
  Pallas kernels: 6.22 us -> 5.21 us
  other arithmetic: 1.65 us -> 2.39 us
    ppermute x2, waiting for transfers between devices: 8.18 us -> 5.33 us  [apply(): halo_a = lax.ppermute(near, AXES, pairs_a)]
    ppermute x2, starting transfers between devices: 6.73 us -> 5.25 us  [apply(): halo_a = lax.ppermute(near, AXES, pairs_a)]
    squeeze x1 -> x2, local copies, waits for them, and re-layouts: 0.01 us -> 1.1 us  [split(): lax.dynamic_index_in_dim(array, near_at, 1, keepdims=False)]
    squeeze x1 -> x0, local copies, waits for them, and re-layouts: 1.09 us -> none  [split(): lax.dynamic_index_in_dim(array, 1 - near_at, 1, keepdims=False)]
    ppermute x2, waiting for transfers between devices: 1.14 us -> 2.17 us  [apply(): lax.ppermute(others.reshape(shape), 'chaos', [(i, i ^ 1) for i in range(o...]
    pallas_call x8 -> x10, Pallas kernels: 6.22 us -> 5.21 us  [the longest x4 3.19 us: product(): pl.pallas_call(functools.partial(product_kernel, plane, count_modes, orde...]
    unnamed x0 -> x1, other arithmetic: none -> 0.66 us
    gather x0 -> x1, local copies, waits for them, and re-layouts: none -> 0.56 us  [body(): jnp.take(send_rows.reshape(owners, cap), own ^ jnp.arange(owners), axis=0)]
  transfers between devices with their start and end apart: 12 -> 12, of which waited for: 9 -> 8; matrix products, arithmetic and copies ran while one was open for 6% -> 11% of each run, Pallas kernels for 5% -> 5%
where the time goes in v3:
time: 45.8 us; the launch traced here: 45.6 us
  waiting for transfers between devices  19.4 us (42%)
  starting transfers between devices  12.9 us (28%)
  Pallas kernels  5.21 us (11%)
  local copies, waits for them, and re-layouts  2.87 us (6%)
  other arithmetic  2.39 us (5%)
  matrix products  1.98 us (4%)
  between operations  0.96 us (2%)
    ppermute x6, waiting for transfers between devices, apply(): lax.ppermute(blocks[m], 'chaos', [(i, i ^ 2 * m) for i in range(owners)])  11.9 us
    ppermute x6, starting transfers between devices, apply(): lax.ppermute(blocks[m], 'chaos', [(i, i ^ 2 * m) for i in range(owners)])  7.4 us
    ppermute x2, waiting for transfers between devices, apply(): halo_a = lax.ppermute(near, AXES, pairs_a)  5.33 us
    ppermute x2, starting transfers between devices, apply(): halo_a = lax.ppermute(near, AXES, pairs_a)  5.25 us
    pallas_call x4, Pallas kernels, product(): pl.pallas_call(functools.partial(product_kernel, plane, count_modes, orde...  3.19 us
    ppermute x2, waiting for transfers between devices, apply(): lax.ppermute(others.reshape(shape), 'chaos', [(i, i ^ 1) for i in range(o...  2.17 us
    pallas_call x6, Pallas kernels, images(): pl.pallas_call(functools.partial(images_kernel, plane, parities, chips, c...  2.01 us
    dot_general x1, matrix products, body(): jnp.einsum('isp,isk->kip', place, which, precision=lax.Precision.HIGHEST)  1.98 us
  transfers between devices with their start and end apart: 12, of which 8 were waited for; matrix products, arithmetic and copies ran while one was open for 11% of the time, Pallas kernels for 5%

profile of v3, /device:TPU:0, one launch (start us, length us, event | category | flops | bytes accessed | tf_op | source)
XLA Modules:
  0.0 45.6 jit_solution(6523658321268979782)
XLA Ops:
  0.6 0.0 copy-start.4
  0.6 0.0 copy-start.1
  0.7 0.0 copy-start.2
  0.7 0.0 copy-start.3
  0.7 1.1 %dynamic-slice_bitcast_fusion = (f32[56,8,128]{2,1,0:T(8,128)S(1)}, f32[56,8,128]{2,1,0:T(8,128)S(1)}) fusion(f32[56,2,8,128]{3,2,1,0:T(8,128)} %param.6, s32[]{:T(128)S(6)} %select_n.132, s32[]{:T(128)S(6)} %select_n.139), kind=kLoop, calls=%fused_computation.20 | loop fusion | bytes 917512 | tf_op jit(solution)/shard_map/jit(dynamic_index_in_dim)/squeeze | solution.py:129
  1.8 3.1 %collective-permute-start.1 = (f32[56,8,128]{2,1,0:T(8,128)S(1)}, f32[56,8,128]{2,1,0:T(8,128)S(1)}, u32[]{:S(2)}, u32[]{:S(2)}) collective-permute-start(f32[56,8,128]{2,1,0:T(8,128)S(1)} %get-tuple-element.16.center.other), channel_id=1, source_target_pairs={{0,8},{1,9},{2,10},{3,11},{4,12},{5,13},{6,14},{7,15},{8,0},{9,1},... | collective-permute-start | bytes 688136 | tf_op jit(solution)/shard_map/ppermute | solution.py:148
  4.9 0.0 collective-permute-start
  4.9 0.5 %broadcast.121 = s32[]{:T(128)} broadcast(s32[]{:T(128)} %constant.71.clone.1), dimensions={} | broadcast | bytes 8 | tf_op args[2]
  5.4 0.0 copy-done.4
  5.4 0.7 %reduce.3 = s32[64]{0:T(128)S(1)} reduce(s32[1,64]{1,0:T(1,128)S(1)} %copy-done.4, s32[]{:T(128)} %broadcast.121), dimensions={0}, to_apply=%param.8.reduce_sub_computation.3 | reduce | bytes 516 | tf_op args[2]
  6.1 0.1 reshape.174
  6.2 0.0 copy-done.1
  6.2 0.1 copy.13
  6.3 0.0 copy-done.2
  6.3 0.1 copy.12
  6.4 0.0 copy-done.3
  6.4 0.1 copy.14
  6.5 2.0 %fusion.2 = f32[21,56,64]{2,0,1:T(8,128)S(1)} fusion(f32[56,41]{1,0:T(8,128)S(1)} %copy.14, s32[56,41]{1,0:T(8,128)S(1)} %copy.13, s32[56,41]{1,0:T(8,128)S(1)} %copy.12), kind=kOutput, calls=%fused_computation.4 | convolution fusion | flops 37371992 | bytes 328608 | tf_op jit(solution)/shard_map/isp,isk->kip/dot_general | solution.py:141
  8.5 0.1 copy.15
  8.6 0.1 reduce-precision_convert_fusion
  8.7 0.6 %gather_fusion = s32[8,8]{1,0:T(8,128)S(1)} fusion(s32[8,8]{1,0:T(8,128)S(1)} %reshape.174, s32[1024]{0:T(1024)S(1)} %pad_clamp_fusion), kind=kCustom, calls=%fused_computation | custom fusion | bytes 544 | tf_op jit(solution)/shard_map/jit(_take)/gather | solution.py:136
  9.3 0.1 broadcast_select_fusion
  9.3 0.1 select_n.136.rows
  9.4 0.1 add_convert_fusion
  9.5 1.0 %collective-permute-done.1.halo = f32[56,8,128]{2,1,0:T(8,128)S(1)} collective-permute-done((f32[56,8,128]{2,1,0:T(8,128)S(1)}, f32[56,8,128]{2,1,0:T(8,128)S(1)}, u32[]{:S(2)}, u32[]{:S(2)}) %collective-permute-start.1) | collective-permute-done | bytes 229408 | tf_op jit(solution)/shard_map/ppermute | solution.py:148
  10.5 0.1 broadcast_in_dim.14.flags
  10.5 0.5 %images_0_2_1.2 = (f32[512,128]{1,0:T(8,128)S(1)}, f32[512,128]{1,0:T(8,128)S(1)}) custom-call(s32[1,64]{1,0:T(1,128)S(1)} %select_n.136.rows, s32[2,128]{1,0:T(2,128)S(1)} %broadcast_in_dim.14.flags, f32[56,8,128]{2,1,0:T(8,128)S(1)} %get-tuple-element.16.center.other, f32[56,8,128]{2,1,0:T(8,128)S(1)} %get-tuple-element.17.other.center, ...), custom_call_target="tpu_custom_call" | custom-call | flops 524288 | bytes 524288 | tf_op jit(solution)/shard_map/images_0_2_1/pallas_call | solution.py:58
  11.1 0.0 collective-permute-done.halo
  11.1 0.2 images_1_1_1.2
  11.3 0.1 collective-permute-start.2
  11.4 0.3 pad_maximum_fusion.weights
  11.7 0.2 images_1_1_0.2
  12.0 0.0 copy-start
  12.0 0.9 %collective-permute-done.2 = f32[4,2,8,8,128]{4,3,2,1,0:T(8,128)S(1)} collective-permute-done((f32[4,2,8,8,128]{4,3,2,1,0:T(8,128)S(1)}, f32[4,2,8,8,128]{4,3,2,1,0:T(8,128)S(1)}, u32[]{:S(2)}, u32[]{:S(2)}) %collective-permute-start.2) | collective-permute-done | bytes 262176 | tf_op jit(solution)/shard_map/ppermute | solution.py:153
  13.0 2.7 %collective-permute-start.3 = (f32[2,2,8,8,128]{4,3,2,1,0:T(8,128)S(1)}, f32[2,2,8,8,128]{4,3,2,1,0:T(8,128)S(1)}, u32[]{:S(2)}, u32[]{:S(2)}) collective-permute-start(f32[2,2,8,8,128]{4,3,2,1,0:T(8,128)S(1)} %pad_maximum_fusion.4), channel_id=1, source_target_pairs={{0,6},{1,7},{2,4},{3,5},{4,2},{5,3},{6,0},{7,1},{8,14},{9,15},{10,... | collective-permute-start | bytes 393224 | tf_op jit(solution)/shard_map/ppermute | solution.py:159
  15.7 0.6 %collective-permute-start.4 = (f32[2,2,8,8,128]{4,3,2,1,0:T(8,128)S(1)}, f32[2,2,8,8,128]{4,3,2,1,0:T(8,128)S(1)}, u32[]{:S(2)}, u32[]{:S(2)}) collective-permute-start(f32[2,2,8,8,128]{4,3,2,1,0:T(8,128)S(1)} %pad_maximum_fusion.5), channel_id=1, source_target_pairs={{0,2},{1,3},{2,0},{3,1},{4,6},{5,7},{6,4},{7,5},{8,10},{9,11},{10,... | collective-permute-start | bytes 393224 | tf_op jit(solution)/shard_map/ppermute | solution.py:159
  16.3 0.4 collective-permute-start.5
  16.7 0.0 copy-done
  16.7 3.6 %collective-permute-done.3.rest_1_ = f32[2,2,8,8,128]{4,3,2,1,0:T(8,128)S(1)} collective-permute-done((f32[2,2,8,8,128]{4,3,2,1,0:T(8,128)S(1)}, f32[2,2,8,8,128]{4,3,2,1,0:T(8,128)S(1)}, u32[]{:S(2)}, u32[]{:S(2)}) %collective-permute-start.3) | collective-permute-done | bytes 131104 | tf_op jit(solution)/shard_map/ppermute | solution.py:159
  20.3 2.2 %collective-permute-done.4.rest_2_ = f32[2,2,8,8,128]{4,3,2,1,0:T(8,128)S(1)} collective-permute-done((f32[2,2,8,8,128]{4,3,2,1,0:T(8,128)S(1)}, f32[2,2,8,8,128]{4,3,2,1,0:T(8,128)S(1)}, u32[]{:S(2)}, u32[]{:S(2)}) %collective-permute-start.4) | collective-permute-done | bytes 131104 | tf_op jit(solution)/shard_map/ppermute | solution.py:159
  22.5 0.0 collective-permute-done.5.rest_3_
  22.5 0.8 %product_0.2 = f32[448,128]{1,0:T(8,128)S(1)} custom-call(bf16[1176,192]{1,0:T(8,128)(2,1)S(1)} %pad_maximum_fusion.weights, f32[21,8,128]{2,1,0:T(8,128)S(1)} %get-tuple-element.34.modes, f32[2,2,8,8,128]{4,3,2,1,0:T(8,128)S(1)} %pad_maximum_fusion.3.rest_0_, f32[2,2,8,8,128]{4,3,2,1,0:T(8,128)S(1)} %collective-permute-done.3.rest_1_, ...), custom_call_target="tpu_custom_call" | custom-call | flops 462422016 | bytes 1048576 | tf_op jit(solution)/shard_map/product_0/pallas_call | solution.py:98
  23.3 2.2 %collective-permute-start.7 = (f32[56,8,128]{2,1,0:T(8,128)S(1)}, f32[56,8,128]{2,1,0:T(8,128)S(1)}, u32[]{:S(2)}, u32[]{:S(2)}) collective-permute-start(f32[56,8,128]{2,1,0:T(8,128)S(1)} %bitcast.45), channel_id=1, source_target_pairs={{0,8},{1,9},{2,10},{3,11},{4,12},{5,13},{6,14},{7,15},{8,0},{9,1},... | collective-permute-start | bytes 688136 | tf_op jit(solution)/shard_map/ppermute | solution.py:148
  25.5 0.8 %product_1.2 = f32[448,128]{1,0:T(8,128)S(1)} custom-call(bf16[1176,192]{1,0:T(8,128)(2,1)S(1)} %pad_maximum_fusion.weights, f32[21,8,128]{2,1,0:T(8,128)S(1)} %get-tuple-element.35.modes, f32[2,2,8,8,128]{4,3,2,1,0:T(8,128)S(1)} %pad_maximum_fusion.3.rest_0_, f32[2,2,8,8,128]{4,3,2,1,0:T(8,128)S(1)} %collective-permute-done.3.rest_1_, ...), custom_call_target="tpu_custom_call" | custom-call | flops 462422016 | bytes 1048576 | tf_op jit(solution)/shard_map/product_1/pallas_call | solution.py:98
  26.3 0.1 collective-permute-start.6
  26.4 4.3 %collective-permute-done.7.halo = f32[56,8,128]{2,1,0:T(8,128)S(1)} collective-permute-done((f32[56,8,128]{2,1,0:T(8,128)S(1)}, f32[56,8,128]{2,1,0:T(8,128)S(1)}, u32[]{:S(2)}, u32[]{:S(2)}) %collective-permute-start.7) | collective-permute-done | bytes 229408 | tf_op jit(solution)/shard_map/ppermute | solution.py:148
  30.7 0.5 %images_0_2_1.3 = (f32[512,128]{1,0:T(8,128)S(1)}, f32[512,128]{1,0:T(8,128)S(1)}) custom-call(s32[1,64]{1,0:T(1,128)S(1)} %select_n.136.rows, s32[2,128]{1,0:T(2,128)S(1)} %broadcast_in_dim.14.flags, f32[56,8,128]{2,1,0:T(8,128)S(1)} %bitcast.46, f32[56,8,128]{2,1,0:T(8,128)S(1)} %bitcast.50, f32[56,8,128]{2,1,0:T(8,128)S(1)} %collective-permute-done.7.halo), custom_call_target="tpu_custom_call" | custom-call | flops 524288 | bytes 524288 | tf_op jit(solution)/shard_map/images_0_2_1/pallas_call | solution.py:58
  31.2 0.0 collective-permute-done.6.halo
  31.2 0.2 images_1_1_1.3
  31.5 0.1 collective-permute-start.8
  31.6 0.2 images_1_1_0.3
  31.9 1.2 %collective-permute-done.8 = f32[4,2,8,8,128]{4,3,2,1,0:T(8,128)S(1)} collective-permute-done((f32[4,2,8,8,128]{4,3,2,1,0:T(8,128)S(1)}, f32[4,2,8,8,128]{4,3,2,1,0:T(8,128)S(1)}, u32[]{:S(2)}, u32[]{:S(2)}) %collective-permute-start.8) | collective-permute-done | bytes 262176 | tf_op jit(solution)/shard_map/ppermute | solution.py:153
  33.1 3.0 %collective-permute-start.9 = (f32[2,2,8,8,128]{4,3,2,1,0:T(8,128)S(1)}, f32[2,2,8,8,128]{4,3,2,1,0:T(8,128)S(1)}, u32[]{:S(2)}, u32[]{:S(2)}) collective-permute-start(f32[2,2,8,8,128]{4,3,2,1,0:T(8,128)S(1)} %pad_maximum_fusion.8), channel_id=1, source_target_pairs={{0,6},{1,7},{2,4},{3,5},{4,2},{5,3},{6,0},{7,1},{8,14},{9,15},{10,... | collective-permute-start | bytes 393224 | tf_op jit(solution)/shard_map/ppermute | solution.py:159
  36.2 0.6 %collective-permute-start.10 = (f32[2,2,8,8,128]{4,3,2,1,0:T(8,128)S(1)}, f32[2,2,8,8,128]{4,3,2,1,0:T(8,128)S(1)}, u32[]{:S(2)}, u32[]{:S(2)}) collective-permute-start(f32[2,2,8,8,128]{4,3,2,1,0:T(8,128)S(1)} %pad_maximum_fusion.9), channel_id=1, source_target_pairs={{0,2},{1,3},{2,0},{3,1},{4,6},{5,7},{6,4},{7,5},{8,10},{9,11},{10,... | collective-permute-start | bytes 393224 | tf_op jit(solution)/shard_map/ppermute | solution.py:159
  36.8 0.1 collective-permute-start.11
  36.9 3.5 %collective-permute-done.9.rest_1_ = f32[2,2,8,8,128]{4,3,2,1,0:T(8,128)S(1)} collective-permute-done((f32[2,2,8,8,128]{4,3,2,1,0:T(8,128)S(1)}, f32[2,2,8,8,128]{4,3,2,1,0:T(8,128)S(1)}, u32[]{:S(2)}, u32[]{:S(2)}) %collective-permute-start.9) | collective-permute-done | bytes 131104 | tf_op jit(solution)/shard_map/ppermute | solution.py:159
  40.4 2.6 %collective-permute-done.10.rest_2_ = f32[2,2,8,8,128]{4,3,2,1,0:T(8,128)S(1)} collective-permute-done((f32[2,2,8,8,128]{4,3,2,1,0:T(8,128)S(1)}, f32[2,2,8,8,128]{4,3,2,1,0:T(8,128)S(1)}, u32[]{:S(2)}, u32[]{:S(2)}) %collective-permute-start.10) | collective-permute-done | bytes 131104 | tf_op jit(solution)/shard_map/ppermute | solution.py:159
  43.0 0.0 collective-permute-done.11.rest_3_
  43.0 0.8 %product_1.3 = f32[448,128]{1,0:T(8,128)S(1)} custom-call(bf16[1176,192]{1,0:T(8,128)(2,1)S(1)} %pad_maximum_fusion.weights, f32[21,8,128]{2,1,0:T(8,128)S(1)} %get-tuple-element.35.modes, f32[2,2,8,8,128]{4,3,2,1,0:T(8,128)S(1)} %pad_maximum_fusion.7.rest_0_, f32[2,2,8,8,128]{4,3,2,1,0:T(8,128)S(1)} %collective-permute-done.9.rest_1_, ...), custom_call_target="tpu_custom_call" | custom-call | flops 462422016 | bytes 1048576 | tf_op jit(solution)/shard_map/product_1/pallas_call | solution.py:98
  43.8 0.8 %product_0.3 = f32[448,128]{1,0:T(8,128)S(1)} custom-call(bf16[1176,192]{1,0:T(8,128)(2,1)S(1)} %pad_maximum_fusion.weights, f32[21,8,128]{2,1,0:T(8,128)S(1)} %get-tuple-element.34.modes, f32[2,2,8,8,128]{4,3,2,1,0:T(8,128)S(1)} %pad_maximum_fusion.7.rest_0_, f32[2,2,8,8,128]{4,3,2,1,0:T(8,128)S(1)} %collective-permute-done.9.rest_1_, ...), custom_call_target="tpu_custom_call" | custom-call | flops 462422016 | bytes 1048576 | tf_op jit(solution)/shard_map/product_0/pallas_call | solution.py:98
  44.7 1.0 %pad_maximum_fusion.1 = (f32[56,2,8,128]{3,2,1,0:T(8,128)}, f32[56,2,8,128]{3,2,1,0:T(8,128)}) fusion(f32[56,1,8,128]{3,2,1,0:T(8,128)S(1)} %get-tuple-element.15, f32[56,1,8,128]{3,2,1,0:T(8,128)S(1)} %get-tuple-element.14, f32[56,1,8,128]{3,2,1,0:T(8,128)S(1)} %get-tuple-element.13, f32[56,1,8,128]{3,2,1,0:T(8,128)S(1)} %get-tuple-element.12), kind=kLoop, calls=%fused_computation.13 | loop fusion | flops 229376 | bytes 1835008 | tf_op jit(solution)/shard_map/stack | solution.py:134
  (19 shorter events, 0.3 us)
Async XLA Ops:
  0.6 4.8 %copy-start.4 = (s32[1,64]{1,0:T(1,128)S(1)}, s32[1,64]{1,0:T(1,128)}, u32[]{:S(2)}) copy-start(s32[1,64]{1,0:T(1,128)} %param.8) | copy-start | bytes 772
  0.6 5.5 %copy-start.1 = (s32[56,41]{0,1:T(8,128)S(1)}, s32[56,41]{0,1:T(8,128)}, u32[]{:S(2)}) copy-start(s32[56,41]{0,1:T(8,128)} %param.9) | copy-start | bytes 27556
  0.7 5.6 %copy-start.2 = (s32[56,41]{0,1:T(8,128)S(1)}, s32[56,41]{0,1:T(8,128)}, u32[]{:S(2)}) copy-start(s32[56,41]{0,1:T(8,128)} %param.10) | copy-start | bytes 27556
  0.7 5.7 %copy-start.3 = (f32[56,41]{0,1:T(8,128)S(1)}, f32[56,41]{0,1:T(8,128)}, u32[]{:S(2)}) copy-start(f32[56,41]{0,1:T(8,128)} %param.11) | copy-start | bytes 27556
  1.8 8.7 %collective-permute-start.1 = (f32[56,8,128]{2,1,0:T(8,128)S(1)}, f32[56,8,128]{2,1,0:T(8,128)S(1)}, u32[]{:S(2)}, u32[]{:S(2)}) collective-permute-start(f32[56,8,128]{2,1,0:T(8,128)S(1)} %get-tuple-element.16.center.other), channel_id=1, source_target_pairs={{0,8},{1,9},{2,10},{3,11},{4,12},{5,13},{6,14},{7,15},{8,0},{9,1},... | collective-permute-start | bytes 688136 | tf_op jit(solution)/shard_map/ppermute | solution.py:148
  4.9 6.2 %collective-permute-start = (f32[56,8,128]{2,1,0:T(8,128)S(1)}, f32[56,8,128]{2,1,0:T(8,128)S(1)}, u32[]{:S(2)}, u32[]{:S(2)}) collective-permute-start(f32[56,8,128]{2,1,0:T(8,128)S(1)} %get-tuple-element.17.other.center), channel_id=1, source_target_pairs={{0,1},{1,0},{2,3},{3,2},{4,5},{5,4},{6,7},{7,6},{8,16},{9,17},{10,... | collective-permute-start | bytes 688136 | tf_op jit(solution)/shard_map/ppermute | solution.py:149
  11.3 1.6 %collective-permute-start.2 = (f32[4,2,8,8,128]{4,3,2,1,0:T(8,128)S(1)}, f32[4,2,8,8,128]{4,3,2,1,0:T(8,128)S(1)}, u32[]{:S(2)}, u32[]{:S(2)}) collective-permute-start(f32[4,2,8,8,128]{4,3,2,1,0:T(8,128)S(1)} %bitcast.53), channel_id=1, source_target_pairs={{0,1},{1,0},{2,3},{3,2},{4,5},{5,4},{6,7},{7,6},{8,9},{9,8},{10,11... | collective-permute-start | bytes 786440 | tf_op jit(solution)/shard_map/ppermute | solution.py:153
  12.0 4.7 %copy-start = (f32[21,2,8,128]{3,2,1,0:T(8,128)S(1)}, f32[21,2,8,128]{3,2,1,0:T(8,128)}, u32[]{:S(2)}) copy-start(f32[21,2,8,128]{3,2,1,0:T(8,128)} %param.7) | copy-start | bytes 516100
  13.0 7.3 %collective-permute-start.3 = (f32[2,2,8,8,128]{4,3,2,1,0:T(8,128)S(1)}, f32[2,2,8,8,128]{4,3,2,1,0:T(8,128)S(1)}, u32[]{:S(2)}, u32[]{:S(2)}) collective-permute-start(f32[2,2,8,8,128]{4,3,2,1,0:T(8,128)S(1)} %pad_maximum_fusion.4), channel_id=1, source_target_pairs={{0,6},{1,7},{2,4},{3,5},{4,2},{5,3},{6,0},{7,1},{8,14},{9,15},{10,... | collective-permute-start | bytes 393224 | tf_op jit(solution)/shard_map/ppermute | solution.py:159
  15.7 6.8 %collective-permute-start.4 = (f32[2,2,8,8,128]{4,3,2,1,0:T(8,128)S(1)}, f32[2,2,8,8,128]{4,3,2,1,0:T(8,128)S(1)}, u32[]{:S(2)}, u32[]{:S(2)}) collective-permute-start(f32[2,2,8,8,128]{4,3,2,1,0:T(8,128)S(1)} %pad_maximum_fusion.5), channel_id=1, source_target_pairs={{0,2},{1,3},{2,0},{3,1},{4,6},{5,7},{6,4},{7,5},{8,10},{9,11},{10,... | collective-permute-start | bytes 393224 | tf_op jit(solution)/shard_map/ppermute | solution.py:159
  16.3 6.2 %collective-permute-start.5 = (f32[2,2,8,8,128]{4,3,2,1,0:T(8,128)S(1)}, f32[2,2,8,8,128]{4,3,2,1,0:T(8,128)S(1)}, u32[]{:S(2)}, u32[]{:S(2)}) collective-permute-start(f32[2,2,8,8,128]{4,3,2,1,0:T(8,128)S(1)} %pad_maximum_fusion.6), channel_id=1, source_target_pairs={{0,4},{1,5},{2,6},{3,7},{4,0},{5,1},{6,2},{7,3},{8,12},{9,13},{10,... | collective-permute-start | bytes 393224 | tf_op jit(solution)/shard_map/ppermute | solution.py:159
  23.3 7.4 %collective-permute-start.7 = (f32[56,8,128]{2,1,0:T(8,128)S(1)}, f32[56,8,128]{2,1,0:T(8,128)S(1)}, u32[]{:S(2)}, u32[]{:S(2)}) collective-permute-start(f32[56,8,128]{2,1,0:T(8,128)S(1)} %bitcast.45), channel_id=1, source_target_pairs={{0,8},{1,9},{2,10},{3,11},{4,12},{5,13},{6,14},{7,15},{8,0},{9,1},... | collective-permute-start | bytes 688136 | tf_op jit(solution)/shard_map/ppermute | solution.py:148
  26.3 5.0 %collective-permute-start.6 = (f32[56,8,128]{2,1,0:T(8,128)S(1)}, f32[56,8,128]{2,1,0:T(8,128)S(1)}, u32[]{:S(2)}, u32[]{:S(2)}) collective-permute-start(f32[56,8,128]{2,1,0:T(8,128)S(1)} %bitcast.49), channel_id=1, source_target_pairs={{0,1},{1,0},{2,3},{3,2},{4,5},{5,4},{6,7},{7,6},{8,16},{9,17},{10,... | collective-permute-start | bytes 688136 | tf_op jit(solution)/shard_map/ppermute | solution.py:149
  31.5 1.6 %collective-permute-start.8 = (f32[4,2,8,8,128]{4,3,2,1,0:T(8,128)S(1)}, f32[4,2,8,8,128]{4,3,2,1,0:T(8,128)S(1)}, u32[]{:S(2)}, u32[]{:S(2)}) collective-permute-start(f32[4,2,8,8,128]{4,3,2,1,0:T(8,128)S(1)} %bitcast.54), channel_id=1, source_target_pairs={{0,1},{1,0},{2,3},{3,2},{4,5},{5,4},{6,7},{7,6},{8,9},{9,8},{10,11... | collective-permute-start | bytes 786440 | tf_op jit(solution)/shard_map/ppermute | solution.py:153
  33.1 7.3 %collective-permute-start.9 = (f32[2,2,8,8,128]{4,3,2,1,0:T(8,128)S(1)}, f32[2,2,8,8,128]{4,3,2,1,0:T(8,128)S(1)}, u32[]{:S(2)}, u32[]{:S(2)}) collective-permute-start(f32[2,2,8,8,128]{4,3,2,1,0:T(8,128)S(1)} %pad_maximum_fusion.8), channel_id=1, source_target_pairs={{0,6},{1,7},{2,4},{3,5},{4,2},{5,3},{6,0},{7,1},{8,14},{9,15},{10,... | collective-permute-start | bytes 393224 | tf_op jit(solution)/shard_map/ppermute | solution.py:159
  36.2 6.9 %collective-permute-start.10 = (f32[2,2,8,8,128]{4,3,2,1,0:T(8,128)S(1)}, f32[2,2,8,8,128]{4,3,2,1,0:T(8,128)S(1)}, u32[]{:S(2)}, u32[]{:S(2)}) collective-permute-start(f32[2,2,8,8,128]{4,3,2,1,0:T(8,128)S(1)} %pad_maximum_fusion.9), channel_id=1, source_target_pairs={{0,2},{1,3},{2,0},{3,1},{4,6},{5,7},{6,4},{7,5},{8,10},{9,11},{10,... | collective-permute-start | bytes 393224 | tf_op jit(solution)/shard_map/ppermute | solution.py:159
  36.8 6.2 %collective-permute-start.11 = (f32[2,2,8,8,128]{4,3,2,1,0:T(8,128)S(1)}, f32[2,2,8,8,128]{4,3,2,1,0:T(8,128)S(1)}, u32[]{:S(2)}, u32[]{:S(2)}) collective-permute-start(f32[2,2,8,8,128]{4,3,2,1,0:T(8,128)S(1)} %pad_maximum_fusion.10), channel_id=1, source_target_pairs={{0,4},{1,5},{2,6},{3,7},{4,0},{5,1},{6,2},{7,3},{8,12},{9,13},{10,... | collective-permute-start | bytes 393224 | tf_op jit(solution)/shard_map/ppermute | solution.py:159

commit v4 on v1

v4 whole, which is shorter than its diff:
```python
import functools

import jax
import jax.numpy as jnp
from jax import lax
from jax.experimental import pallas as pl
from jax.experimental.pallas import tpu as pltpu
from jax.sharding import PartitionSpec as P

AXES = ("space", "chaos")
ANY = pl.BlockSpec(memory_space=pl.ANY)
VMEM = pl.BlockSpec(memory_space=pltpu.VMEM)
BATCH = 8
PARAMS = pltpu.CompilerParams(vmem_limit_bytes=32 * 1024 * 1024)


def cost(flops):
    return pl.CostEstimate(flops=flops, bytes_accessed=1 << 20, transcendentals=0)


def slab_pairs(slabs, owners):
    pairs = []
    for s in range(slabs):
        for d in range(owners):
            beside = s + 1 if d % 2 else s - 1
            other = beside * owners + (d ^ 1) if 0 <= beside < slabs else s * owners + (d ^ 2 if owners > 2 else d)
            pairs.append((s * owners + d, other))
    return pairs


def local_kernel(center_own, center_beside, other_own, other_beside, *rest):
    gx, gy = center_own.shape[1:]
    sub = lax.broadcasted_iota(jnp.int32, (gx, gy), 0)
    lane = lax.broadcasted_iota(jnp.int32, (gx, gy), 1)
    zero = jnp.zeros((gx, gy), jnp.float32)

    def laplace(middle, other):
        beside = jnp.where(sub > 0, pltpu.roll(middle, 1, 0), zero)
        beside = beside + jnp.where(sub < gx - 1, pltpu.roll(middle, gx - 1, 0), zero)
        beside = beside + jnp.where(lane > 0, pltpu.roll(middle, 1, 1), zero)
        beside = beside + jnp.where(lane < gy - 1, pltpu.roll(middle, gy - 1, 1), zero)
        return 6.0 * middle - (beside + other)

    for center, other, out in zip((center_own, center_beside), (other_own, other_beside), rest[-2:]):
        for start in range(0, center.shape[0], BATCH):
            terms = range(start, min(start + BATCH, center.shape[0]))
            made = [laplace(center[term], other[term]) for term in terms]
            for term, value in zip(terms, made):
                out[term] = value


def local(centers, others, after=()):
    out = jax.ShapeDtypeStruct(centers[0].shape, jnp.float32)
    return pl.pallas_call(
        local_kernel,
        out_shape=[out, out],
        in_specs=[VMEM] * 4 + [ANY] * len(after),
        out_specs=[VMEM] * 2,
        compiler_params=PARAMS,
        cost_estimate=cost(out.size * 16),
        name="local",
    )(*centers, *others, *after)


def images_kernel(a, blocks, chips, cap, rows, flag, partial, halo, *rest):
    outs = rest[-len(chips) :]
    gx, gy = partial.shape[1:]
    zero = jnp.zeros((gx, gy), jnp.float32)
    inside = flag[...] > 0
    terms = rows[...]
    for m, out in zip(chips, outs):
        for n in range(4 * m, 4 * m + 4):
            if blocks[n][0] == a:
                picked = [terms[0, blocks[n][1] * cap + c] for c in range(cap)]
                made = [partial[term] - jnp.where(inside, halo[term], zero) for term in picked]
                for c in range(cap):
                    out[pl.ds((n - 4 * m) * gx * cap + c, gx, stride=cap), :] = made[c]


def images(a, blocks, chips, cap, rows, flag, partial, halos, begun=(), after=()):
    gx, gy = halos[a].shape[1:]
    out = jax.ShapeDtypeStruct((4 * gx * cap, gy), jnp.float32)
    return pl.pallas_call(
        functools.partial(images_kernel, a, blocks, chips, cap),
        out_shape=[out] * len(chips),
        in_specs=[VMEM] * (4 + len(begun)) + [ANY] * len(after),
        out_specs=[VMEM] * len(chips),
        input_output_aliases={4 + i: i for i in range(len(begun))},
        compiler_params=PARAMS,
        cost_estimate=cost(out.size * len(chips)),
        name=f"images_{a}_{chips[0]}",
    )(rows[a], flag, partial[a], halos[a], *begun, *after)


def product_kernel(b, cap, count, weights, modes, *rest):
    arrays, out = rest[:count], rest[-1]
    halves = weights[...].astype(jnp.bfloat16)
    both = jnp.concatenate([halves, halves], axis=1)
    count_modes, gx, gy = modes.shape
    own_terms = weights.shape[0] // count_modes

    def column(g):
        starts = [((b * 2 + (a ^ b)) * gx + g) * cap for a in range(2)]
        full = jnp.concatenate([array[start : start + cap, :] for array in arrays for start in starts], axis=0)
        high = full.astype(jnp.bfloat16)
        low = (full - high.astype(jnp.float32)).astype(jnp.bfloat16)
        return jnp.concatenate([high, high, low, low], axis=0)

    for g in range(0, gx, 2):
        pool = jnp.concatenate([column(g), column(g + 1)], axis=1)
        mixed = jnp.dot(both, pool, preferred_element_type=jnp.float32)
        for side in range(2):
            total = jnp.zeros((own_terms, gy), jnp.float32)
            for k in range(count_modes):
                part = mixed[k * own_terms : (k + 1) * own_terms, side * gy : (side + 1) * gy]
                total = total + part * modes[k, pl.ds(g + side, 1), :]
            out[pl.ds(g + side, own_terms, stride=gx), :] = total


def product(b, cap, weights, modes, arrays, after=()):
    count_modes, gx, gy = modes.shape
    own_terms = weights.shape[0] // count_modes
    out = pl.pallas_call(
        functools.partial(product_kernel, b, cap, len(arrays)),
        out_shape=jax.ShapeDtypeStruct((own_terms * gx, gy), jnp.float32),
        in_specs=[VMEM] * (2 + len(arrays)) + [ANY] * len(after),
        out_specs=VMEM,
        compiler_params=PARAMS,
        cost_estimate=cost(4 * weights.shape[0] * weights.shape[1] * gx * gy),
        name=f"product_{b}",
    )(weights, modes, *arrays, *after)
    return out.reshape(own_terms, gx, gy)


def write_kernel(here, there, out, *rest):
    sems = rest[-1]
    core = lax.rem(lax.axis_index("chaos"), 2)
    copies = [
        pltpu.make_async_copy(here, out.at[:, core], sems.at[0]),
        pltpu.make_async_copy(there, out.at[:, 1 - core], sems.at[1]),
    ]
    for copy in copies:
        copy.start()
    for token in rest[:-1]:
        token[...] = jnp.zeros_like(token)
    for copy in copies:
        copy.wait()


def write(here, there, token):
    terms, gx, gy = here.shape
    return pl.pallas_call(
        write_kernel,
        out_shape=[jax.ShapeDtypeStruct((terms, 2, gx, gy), jnp.float32)]
        + [jax.ShapeDtypeStruct((gx, gy), jnp.float32)] * token,
        in_specs=[VMEM] * 2,
        out_specs=[ANY] + [VMEM] * token,
        scratch_shapes=[pltpu.SemaphoreType.DMA((2,))],
        compiler_params=PARAMS,
        name="write",
    )(here, there)


def body(slabs, owners, field, modes, send_rows, pick, mode_ids, coef):
    space, own = lax.axis_index("space"), lax.axis_index("chaos")
    core = own % 2
    own_terms = pick.shape[0]
    count_modes = modes.shape[0]
    pool_size = send_rows.shape[1]
    cap = pool_size // owners
    chips = owners // 2
    to_slab = slab_pairs(slabs, owners)

    def across(array):
        return lax.ppermute(array, "chaos", [(i, i ^ 1) for i in range(owners)])

    def plane(array, at):
        return lax.dynamic_index_in_dim(array, at, 1, keepdims=False)

    here, there = plane(field, core), plane(field, 1 - core)
    here_beside = across(there)
    send_rows, pick, mode_ids, coef, other, here_beside = lax.optimization_barrier(
        (send_rows, pick, mode_ids, coef, here, here_beside)
    )
    rows_beside, there_beside = across(send_rows), across(other)

    inside = jnp.where(core == 0, space > 0, space + 1 < slabs)
    flag = jnp.broadcast_to(inside.astype(jnp.int32), (1, field.shape[3]))

    def from_own(listed, index):
        for bit in range(owners.bit_length() - 1):
            size = cap << bit
            parts = [listed[:, start : start + size] for start in range(0, pool_size, size)]
            turned = jnp.concatenate([parts[n ^ 1] for n in range(len(parts))], axis=1)
            listed = jnp.where((index >> bit) & 1 == 1, turned, listed)
        return listed

    rows = from_own(send_rows, own), from_own(rows_beside, own ^ 1)
    blocks = tuple((a, 2 * m + (b ^ a)) for m in range(chips) for b in range(2) for a in range(2))

    entry = ((pick // cap) ^ own) * cap + pick % cap
    place = (entry[:, :, None] == jnp.arange(pool_size, dtype=jnp.int32)).astype(jnp.float32)
    place = place * coef[:, :, None]
    which = (mode_ids[:, :, None] == jnp.arange(count_modes, dtype=jnp.int32)).astype(jnp.float32)
    weights = jnp.einsum("isp,isk->kip", place, which, precision=lax.Precision.HIGHEST)
    weights = weights.reshape(count_modes * own_terms, pool_size)

    high = lax.reduce_precision(weights, 8, 7)
    weights = jnp.concatenate([high, weights - high], axis=1)
    weights = weights.astype(jnp.bfloat16), across(weights)
    mode_plane = plane(modes, core)

    order = sorted(range(1, chips), key=lambda m: (-bin(m).count("1"), m))

    def exchange(centers, others):
        halos = [lax.ppermute(center, AXES, to_slab) for center in centers]
        inputs = (cap, rows, flag, local(centers, others, halos[:1]), halos[::-1])
        begun = images(1, blocks, (*order, 0), *inputs)
        sent = images(0, blocks, order, *inputs, begun[:-1])
        (kept,) = images(0, blocks, (0,), *inputs, begun[-1:], sent[-1:])
        arrays = {m: lax.ppermute(x, "chaos", [(i, i ^ (2 * m)) for i in range(owners)]) for m, x in zip(order, sent)}
        return [kept, *(arrays[m] for m in range(1, chips))]

    pool = exchange((here, here_beside), (there, there_beside))
    own_first = product(0, cap, weights[0], mode_plane, pool)
    first = own_first, product(1, cap, weights[1], mode_plane, pool, (own_first,))
    beside = [across(x) for x in first]
    out, token = write(own_first, beside[1], True)
    pool = exchange(first, beside[::-1])
    theirs = across(product(1, cap, weights[1], mode_plane, pool, (token,)))
    mine = product(0, cap, weights[0], mode_plane, pool)
    return out, *write(mine, theirs, False)


def solution(mesh):
    slabs, owners = mesh.shape["space"], mesh.shape["chaos"]

    def per_device(*args):
        return body(slabs, owners, *args)

    in_specs = (
        P("chaos", "space", None, None),
        P(None, "space", None, None),
        P("chaos", None),
        P("chaos", None),
        P("chaos", None),
        P("chaos", None),
    )
    out_specs = (P("chaos", "space", None, None), P("chaos", "space", None, None))
    return jax.shard_map(
        per_device, mesh=mesh, in_specs=in_specs, out_specs=out_specs, check_vma=False
    )
```

time: 66 us -> 44 us (0.67)
  matrix products: 18.1 us -> 1.98 us
  Pallas kernels: 0 us -> 6.45 us
  local copies, waits for them, and re-layouts: 6.43 us -> 2.17 us
  waiting for transfers between devices: 19.6 us -> 16.3 us
  other arithmetic: 3.47 us -> 0.68 us
  starting transfers between devices: 17.2 us -> 15.3 us
    dot_general x3 -> x1, matrix products: 18.1 us -> 1.98 us  [body(): jnp.einsum('isp,isk->kip', place, which, precision=lax.Precision.HIGHEST)]
    pallas_call x0 -> x14, Pallas kernels: none -> 6.45 us  [the longest x4 3.23 us: product(): pl.pallas_call(functools.partial(product_kernel, b, cap, len(arrays)), ou...]
    ppermute x12 -> x17, waiting for transfers between devices: 19.6 us -> 16.3 us  [the longest x6 10.8 us: exchange(): lax.ppermute(x, 'chaos', [(i, i ^ 2 * m) for i in range(owners)])]
    gather x5 -> x0, local copies, waits for them, and re-layouts: 2.88 us -> none  [the longest x2 1.16 us: apply(): jnp.take(images, rows[0::2].reshape(-1), axis=0)]
    unnamed x21 -> x10, local copies, waits for them, and re-layouts: 2.8 us -> 0.03 us
    ppermute x12 -> x17, starting transfers between devices: 17.2 us -> 15.3 us  [the longest x6 7.11 us: exchange(): lax.ppermute(x, 'chaos', [(i, i ^ 2 * m) for i in range(owners)])]
    select_n x12 -> x6, other arithmetic: 1.72 us -> 0.32 us  [from_own(): listed = jnp.where(index >> bit & 1 == 1, turned, listed)]
    squeeze x1 -> x2, local copies, waits for them, and re-layouts: 0.03 us -> 1.12 us  [plane(): return lax.dynamic_index_in_dim(array, at, 1, keepdims=False)]
  transfers between devices with their start and end apart: 12 -> 17, of which waited for: 9 -> 9; matrix products, arithmetic and copies ran while one was open for 11% -> 8% of each run, Pallas kernels for 0% -> 11%
where the time goes in v4:
time: 44 us; the launch traced here: 43.8 us
  waiting for transfers between devices  16.3 us (37%)
  starting transfers between devices  15.3 us (35%)
  Pallas kernels  6.45 us (15%)
  local copies, waits for them, and re-layouts  2.17 us (5%)
  matrix products  1.98 us (4%)
  between operations  0.88 us (2%)
  other arithmetic  0.68 us (2%)
    ppermute x6, waiting for transfers between devices, exchange(): lax.ppermute(x, 'chaos', [(i, i ^ 2 * m) for i in range(owners)])  10.8 us
    ppermute x6, starting transfers between devices, exchange(): lax.ppermute(x, 'chaos', [(i, i ^ 2 * m) for i in range(owners)])  7.11 us
    ppermute x4, starting transfers between devices, exchange(): halos = [lax.ppermute(center, AXES, to_slab) for center in centers]  6.5 us
    ppermute x4, waiting for transfers between devices, exchange(): halos = [lax.ppermute(center, AXES, to_slab) for center in centers]  4.87 us
    pallas_call x4, Pallas kernels, product(): pl.pallas_call(functools.partial(product_kernel, b, cap, len(arrays)), ou...  3.23 us
    dot_general x1, matrix products, body(): jnp.einsum('isp,isk->kip', place, which, precision=lax.Precision.HIGHEST)  1.98 us
    ppermute x7, starting transfers between devices, across(): return lax.ppermute(array, 'chaos', [(i, i ^ 1) for i in range(owners)])  1.71 us
    pallas_call x2, Pallas kernels, write(): pl.pallas_call(write_kernel, out_shape=[jax.ShapeDtypeStruct((terms, 2, g...  1.57 us
  transfers between devices with their start and end apart: 17, of which 9 were waited for; matrix products, arithmetic and copies ran while one was open for 8% of the time, Pallas kernels for 11%

profile of v4, /device:TPU:0, one launch (start us, length us, event | category | flops | bytes accessed | tf_op | source)
XLA Modules:
  0.0 43.8 jit_solution(16486324739380609624)
XLA Ops:
  0.6 0.0 copy-start
  0.7 1.1 %dynamic-slice_bitcast_fusion = (f32[56,8,128]{2,1,0:T(8,128)S(1)}, f32[56,8,128]{2,1,0:T(8,128)S(1)}) fusion(f32[56,2,8,128]{3,2,1,0:T(8,128)} %param.6, s32[]{:T(128)S(6)} %select_n.71, s32[]{:T(128)S(6)} %select_n.70), kind=kLoop, calls=%fused_computation.12 | loop fusion | bytes 917512 | tf_op jit(solution)/shard_map/jit(dynamic_index_in_dim)/squeeze | solution.py:178
  1.8 0.5 %collective-permute-start = (f32[56,8,128]{2,1,0:T(8,128)S(1)}, f32[56,8,128]{2,1,0:T(8,128)S(1)}, u32[]{:S(2)}, u32[]{:S(2)}) collective-permute-start(f32[56,8,128]{2,1,0:T(8,128)S(1)} %get-tuple-element.58.other_own), channel_id=1, source_target_pairs={{0,1},{1,0},{2,3},{3,2},{4,5},{5,4},{6,7},{7,6},{8,9},{9,8},{10,11... | collective-permute-start | bytes 688136 | tf_op jit(solution)/shard_map/ppermute | solution.py:175
  2.3 2.6 %collective-permute-start.2 = (f32[56,8,128]{2,1,0:T(8,128)S(1)}, f32[56,8,128]{2,1,0:T(8,128)S(1)}, u32[]{:S(2)}, u32[]{:S(2)}) collective-permute-start(f32[56,8,128]{2,1,0:T(8,128)S(1)} %get-tuple-element.33.center_own), channel_id=1, source_target_pairs={{0,2},{1,8},{2,0},{3,10},{4,6},{5,12},{6,4},{7,14},{8,1},{9,16},{1... | collective-permute-start | bytes 688136 | tf_op jit(solution)/shard_map/ppermute | solution.py:216
  4.9 0.0 collective-permute-done.center_beside
  4.9 0.2 collective-permute-start.4
  5.1 0.1 fusion.23
  5.2 0.3 collective-permute-start.1
  5.5 0.1 concatenate.22
  5.6 0.1 fusion.22
  5.7 0.1 broadcast_select_fusion.4
  5.8 0.1 fusion.21
  5.8 1.4 %collective-permute-start.3 = (f32[56,8,128]{2,1,0:T(8,128)S(1)}, f32[56,8,128]{2,1,0:T(8,128)S(1)}, u32[]{:S(2)}, u32[]{:S(2)}) collective-permute-start(f32[56,8,128]{2,1,0:T(8,128)S(1)} %collective-permute-done.center_beside), channel_id=1, source_target_pairs={{0,2},{1,8},{2,0},{3,10},{4,6},{5,12},{6,4},{7,14},{8,1},{9,16},{1... | collective-permute-start | bytes 688136 | tf_op jit(solution)/shard_map/ppermute | solution.py:216
  7.3 0.1 copy.17
  7.4 0.1 copy.16
  7.5 0.1 copy.18
  7.6 2.0 %fusion.2 = f32[21,56,64]{2,0,1:T(8,128)S(1)} fusion(f32[56,41]{1,0:T(8,128)S(1)} %copy.18, s32[56,41]{1,0:T(8,128)S(1)} %copy.17, s32[56,41]{1,0:T(8,128)S(1)} %copy.16), kind=kOutput, calls=%fused_computation.3 | convolution fusion | flops 37371992 | bytes 328608 | tf_op jit(solution)/shard_map/isp,isk->kip/dot_general | solution.py:205
  9.5 0.1 copy.19
  9.7 0.1 bitcast_reduce-precision_fusion
  9.8 0.2 fusion.17
  10.0 0.3 collective-permute-start.8
  10.3 0.1 broadcast_select_fusion.5.rows
  10.3 0.0 collective-permute-done.4
  10.4 0.1 fusion.20
  10.4 0.1 concatenate.25
  10.5 0.1 fusion.19
  10.6 0.1 broadcast_select_fusion.1
  10.7 0.1 fusion.18
  10.8 0.1 broadcast_select_fusion.2.rows
  10.8 0.0 collective-permute-done.2.rest_0_.halo
  10.8 0.3 local.2
  11.2 0.2 images_1_3.2
  11.4 0.5 %collective-permute-done.3.halo = f32[56,8,128]{2,1,0:T(8,128)S(1)} collective-permute-done((f32[56,8,128]{2,1,0:T(8,128)S(1)}, f32[56,8,128]{2,1,0:T(8,128)S(1)}, u32[]{:S(2)}, u32[]{:S(2)}) %collective-permute-start.3) | collective-permute-done | bytes 229408 | tf_op jit(solution)/shard_map/ppermute | solution.py:216
  11.9 0.2 images_0_3.2
  12.1 1.6 %collective-permute-start.5 = (f32[256,128]{1,0:T(8,128)S(1)}, f32[256,128]{1,0:T(8,128)S(1)}, u32[]{:S(2)}, u32[]{:S(2)}) collective-permute-start(f32[256,128]{1,0:T(8,128)S(1)} %get-tuple-element.41), channel_id=1, source_target_pairs={{0,2},{1,3},{2,0},{3,1},{4,6},{5,7},{6,4},{7,5},{8,10},{9,11},{10,... | collective-permute-start | bytes 393224 | tf_op jit(solution)/shard_map/ppermute | solution.py:221
  13.6 1.5 %collective-permute-start.6 = (f32[256,128]{1,0:T(8,128)S(1)}, f32[256,128]{1,0:T(8,128)S(1)}, u32[]{:S(2)}, u32[]{:S(2)}) collective-permute-start(f32[256,128]{1,0:T(8,128)S(1)} %get-tuple-element.40.rest_1_), channel_id=1, source_target_pairs={{0,4},{1,5},{2,6},{3,7},{4,0},{5,1},{6,2},{7,3},{8,12},{9,13},{10,... | collective-permute-start | bytes 393224 | tf_op jit(solution)/shard_map/ppermute | solution.py:221
  15.2 0.4 %collective-permute-start.7 = (f32[256,128]{1,0:T(8,128)S(1)}, f32[256,128]{1,0:T(8,128)S(1)}, u32[]{:S(2)}, u32[]{:S(2)}) collective-permute-start(f32[256,128]{1,0:T(8,128)S(1)} %get-tuple-element.42), channel_id=1, source_target_pairs={{0,6},{1,7},{2,4},{3,5},{4,2},{5,3},{6,0},{7,1},{8,14},{9,15},{10,... | collective-permute-start | bytes 393224 | tf_op jit(solution)/shard_map/ppermute | solution.py:221
  15.6 0.1 images_0_0.2.rest_0_
  15.8 1.8 %collective-permute-done.5.rest_1_ = f32[256,128]{1,0:T(8,128)S(1)} collective-permute-done((f32[256,128]{1,0:T(8,128)S(1)}, f32[256,128]{1,0:T(8,128)S(1)}, u32[]{:S(2)}, u32[]{:S(2)}) %collective-permute-start.5) | collective-permute-done | bytes 131104 | tf_op jit(solution)/shard_map/ppermute | solution.py:221
  17.6 4.1 %collective-permute-done.6.rest_2_ = f32[256,128]{1,0:T(8,128)S(1)} collective-permute-done((f32[256,128]{1,0:T(8,128)S(1)}, f32[256,128]{1,0:T(8,128)S(1)}, u32[]{:S(2)}, u32[]{:S(2)}) %collective-permute-start.6) | collective-permute-done | bytes 131104 | tf_op jit(solution)/shard_map/ppermute | solution.py:221
  21.7 0.8 %product_0.2 = f32[448,128]{1,0:T(8,128)S(1)} custom-call(bf16[1176,128]{1,0:T(8,128)(2,1)S(1)} %get-tuple-element.54.weights, f32[21,8,128]{2,1,0:T(8,128)S(1)} %dynamic-slice_bitcast_fusion.2.modes, f32[256,128]{1,0:T(8,128)S(1)} %images_0_0.2.rest_0_, f32[256,128]{1,0:T(8,128)S(1)} %collective-permute-done.5.rest_1_, ...), custom_call_target="tpu_custom_call" | custom-call | flops 616562688 | bytes 1048576 | tf_op jit(solution)/shard_map/product_0/pallas_call | solution.py:123
  22.5 0.1 collective-permute-start.10
  22.6 1.3 %collective-permute-start.11 = (f32[56,8,128]{2,1,0:T(8,128)S(1)}, f32[56,8,128]{2,1,0:T(8,128)S(1)}, u32[]{:S(2)}, u32[]{:S(2)}) collective-permute-start(f32[56,8,128]{2,1,0:T(8,128)S(1)} %bitcast.18), channel_id=1, source_target_pairs={{0,2},{1,8},{2,0},{3,10},{4,6},{5,12},{6,4},{7,14},{8,1},{9,16},{1... | collective-permute-start | bytes 688136 | tf_op jit(solution)/shard_map/ppermute | solution.py:216
  23.9 0.8 %product_1.2 = f32[448,128]{1,0:T(8,128)S(1)} custom-call(f32[1176,128]{1,0:T(8,128)S(1)} %collective-permute-done.8.weights, f32[21,8,128]{2,1,0:T(8,128)S(1)} %dynamic-slice_bitcast_fusion.2.modes, f32[256,128]{1,0:T(8,128)S(1)} %images_0_0.2.rest_0_, f32[256,128]{1,0:T(8,128)S(1)} %collective-permute-done.5.rest_1_, ...), custom_call_target="tpu_custom_call" | custom-call | flops 616562688 | bytes 1048576 | tf_op jit(solution)/shard_map/product_1/pallas_call | solution.py:123
  24.7 0.3 collective-permute-start.9
  25.0 1.2 %collective-permute-start.12 = (f32[56,8,128]{2,1,0:T(8,128)S(1)}, f32[56,8,128]{2,1,0:T(8,128)S(1)}, u32[]{:S(2)}, u32[]{:S(2)}) collective-permute-start(f32[56,8,128]{2,1,0:T(8,128)S(1)} %bitcast.24), channel_id=1, source_target_pairs={{0,2},{1,8},{2,0},{3,10},{4,6},{5,12},{6,4},{7,14},{8,1},{9,16},{1... | collective-permute-start | bytes 688136 | tf_op jit(solution)/shard_map/ppermute | solution.py:216
  26.2 2.5 %collective-permute-done.11.rest_0_.halo = f32[56,8,128]{2,1,0:T(8,128)S(1)} collective-permute-done((f32[56,8,128]{2,1,0:T(8,128)S(1)}, f32[56,8,128]{2,1,0:T(8,128)S(1)}, u32[]{:S(2)}, u32[]{:S(2)}) %collective-permute-start.11) | collective-permute-done | bytes 229408 | tf_op jit(solution)/shard_map/ppermute | solution.py:216
  28.7 0.3 local.3
  29.0 0.2 images_1_3.3
  29.2 1.9 %collective-permute-done.12.halo = f32[56,8,128]{2,1,0:T(8,128)S(1)} collective-permute-done((f32[56,8,128]{2,1,0:T(8,128)S(1)}, f32[56,8,128]{2,1,0:T(8,128)S(1)}, u32[]{:S(2)}, u32[]{:S(2)}) %collective-permute-start.12) | collective-permute-done | bytes 229408 | tf_op jit(solution)/shard_map/ppermute | solution.py:216
  31.1 0.2 images_0_3.3
  31.3 1.3 %collective-permute-start.13 = (f32[256,128]{1,0:T(8,128)S(1)}, f32[256,128]{1,0:T(8,128)S(1)}, u32[]{:S(2)}, u32[]{:S(2)}) collective-permute-start(f32[256,128]{1,0:T(8,128)S(1)} %get-tuple-element.51), channel_id=1, source_target_pairs={{0,2},{1,3},{2,0},{3,1},{4,6},{5,7},{6,4},{7,5},{8,10},{9,11},{10,... | collective-permute-start | bytes 393224 | tf_op jit(solution)/shard_map/ppermute | solution.py:221
  32.6 0.8 %collective-permute-start.14 = (f32[256,128]{1,0:T(8,128)S(1)}, f32[256,128]{1,0:T(8,128)S(1)}, u32[]{:S(2)}, u32[]{:S(2)}) collective-permute-start(f32[256,128]{1,0:T(8,128)S(1)} %get-tuple-element.50.rest_1_), channel_id=1, source_target_pairs={{0,4},{1,5},{2,6},{3,7},{4,0},{5,1},{6,2},{7,3},{8,12},{9,13},{10,... | collective-permute-start | bytes 393224 | tf_op jit(solution)/shard_map/ppermute | solution.py:221
  33.4 1.4 %collective-permute-start.15 = (f32[256,128]{1,0:T(8,128)S(1)}, f32[256,128]{1,0:T(8,128)S(1)}, u32[]{:S(2)}, u32[]{:S(2)}) collective-permute-start(f32[256,128]{1,0:T(8,128)S(1)} %get-tuple-element.52), channel_id=1, source_target_pairs={{0,6},{1,7},{2,4},{3,5},{4,2},{5,3},{6,0},{7,1},{8,14},{9,15},{10,... | collective-permute-start | bytes 393224 | tf_op jit(solution)/shard_map/ppermute | solution.py:221
  34.9 0.1 images_0_0.3.rest_0_
  35.0 0.8 %write.2 = (f32[56,2,8,128]{3,2,1,0:T(8,128)}, f32[8,128]{1,0:T(8,128)S(1)}) custom-call(f32[56,8,128]{2,1,0:T(8,128)S(1)} %bitcast.21, f32[56,8,128]{2,1,0:T(8,128)S(1)} %collective-permute-done.9.there.other_own), custom_call_target="tpu_custom_call" | custom-call | tf_op jit(solution)/shard_map/write/pallas_call | solution.py:152
  35.8 1.7 %collective-permute-done.13.rest_1_ = f32[256,128]{1,0:T(8,128)S(1)} collective-permute-done((f32[256,128]{1,0:T(8,128)S(1)}, f32[256,128]{1,0:T(8,128)S(1)}, u32[]{:S(2)}, u32[]{:S(2)}) %collective-permute-start.13) | collective-permute-done | bytes 131104 | tf_op jit(solution)/shard_map/ppermute | solution.py:221
  37.5 1.5 %collective-permute-done.14.rest_2_ = f32[256,128]{1,0:T(8,128)S(1)} collective-permute-done((f32[256,128]{1,0:T(8,128)S(1)}, f32[256,128]{1,0:T(8,128)S(1)}, u32[]{:S(2)}, u32[]{:S(2)}) %collective-permute-start.14) | collective-permute-done | bytes 131104 | tf_op jit(solution)/shard_map/ppermute | solution.py:221
  39.0 1.6 %collective-permute-done.15.rest_3_ = f32[256,128]{1,0:T(8,128)S(1)} collective-permute-done((f32[256,128]{1,0:T(8,128)S(1)}, f32[256,128]{1,0:T(8,128)S(1)}, u32[]{:S(2)}, u32[]{:S(2)}) %collective-permute-start.15) | collective-permute-done | bytes 131104 | tf_op jit(solution)/shard_map/ppermute | solution.py:221
  40.7 0.8 %product_1.3 = f32[448,128]{1,0:T(8,128)S(1)} custom-call(f32[1176,128]{1,0:T(8,128)S(1)} %collective-permute-done.8.weights, f32[21,8,128]{2,1,0:T(8,128)S(1)} %dynamic-slice_bitcast_fusion.2.modes, f32[256,128]{1,0:T(8,128)S(1)} %images_0_0.3.rest_0_, f32[256,128]{1,0:T(8,128)S(1)} %collective-permute-done.13.rest_1_, ...), custom_call_target="tpu_custom_call" | custom-call | flops 616562688 | bytes 1048576 | tf_op jit(solution)/shard_map/product_1/pallas_call | solution.py:123
  41.5 0.1 collective-permute-start.16
  41.6 0.8 %product_0.3 = f32[448,128]{1,0:T(8,128)S(1)} custom-call(bf16[1176,128]{1,0:T(8,128)(2,1)S(1)} %get-tuple-element.54.weights, f32[21,8,128]{2,1,0:T(8,128)S(1)} %dynamic-slice_bitcast_fusion.2.modes, f32[256,128]{1,0:T(8,128)S(1)} %images_0_0.3.rest_0_, f32[256,128]{1,0:T(8,128)S(1)} %collective-permute-done.13.rest_1_, ...), custom_call_target="tpu_custom_call" | custom-call | flops 616562688 | bytes 1048576 | tf_op jit(solution)/shard_map/product_0/pallas_call | solution.py:123
  42.4 0.7 %collective-permute-done.16.there = f32[56,8,128]{2,1,0:T(8,128)S(1)} collective-permute-done((f32[56,8,128]{2,1,0:T(8,128)S(1)}, f32[56,8,128]{2,1,0:T(8,128)S(1)}, u32[]{:S(2)}, u32[]{:S(2)}) %collective-permute-start.16) | collective-permute-done | bytes 229408 | tf_op jit(solution)/shard_map/ppermute | solution.py:175
  43.0 0.8 %write.3 = f32[56,2,8,128]{3,2,1,0:T(8,128)} custom-call(f32[56,8,128]{2,1,0:T(8,128)S(1)} %bitcast.22, f32[56,8,128]{2,1,0:T(8,128)S(1)} %collective-permute-done.16.there), custom_call_target="tpu_custom_call" | custom-call | tf_op jit(solution)/shard_map/write/pallas_call | solution.py:152
  (19 shorter events, 0.1 us)
Async XLA Ops:
  0.6 15.0 %copy-start = (f32[21,2,8,128]{3,2,1,0:T(8,128)S(1)}, f32[21,2,8,128]{3,2,1,0:T(8,128)}, u32[]{:S(2)}) copy-start(f32[21,2,8,128]{3,2,1,0:T(8,128)} %param.7) | copy-start | bytes 516100
  0.6 6.7 %copy-start.3 = (s32[56,41]{0,1:T(8,128)S(1)}, s32[56,41]{0,1:T(8,128)}, u32[]{:S(2)}) copy-start(s32[56,41]{0,1:T(8,128)} %param.10) | copy-start | bytes 27556
  0.7 6.8 %copy-start.4 = (f32[56,41]{0,1:T(8,128)S(1)}, f32[56,41]{0,1:T(8,128)}, u32[]{:S(2)}) copy-start(f32[56,41]{0,1:T(8,128)} %param.11) | copy-start | bytes 27556
  0.7 4.3 %copy-start.1 = (s32[1,64]{1,0:T(1,128)S(1)}, s32[1,64]{1,0:T(1,128)}, u32[]{:S(2)}) copy-start(s32[1,64]{1,0:T(1,128)} %param.8) | copy-start | bytes 772
  0.7 6.6 %copy-start.2 = (s32[56,41]{0,1:T(8,128)S(1)}, s32[56,41]{0,1:T(8,128)}, u32[]{:S(2)}) copy-start(s32[56,41]{0,1:T(8,128)} %param.9) | copy-start | bytes 27556
  1.8 3.1 %collective-permute-start = (f32[56,8,128]{2,1,0:T(8,128)S(1)}, f32[56,8,128]{2,1,0:T(8,128)S(1)}, u32[]{:S(2)}, u32[]{:S(2)}) collective-permute-start(f32[56,8,128]{2,1,0:T(8,128)S(1)} %get-tuple-element.58.other_own), channel_id=1, source_target_pairs={{0,1},{1,0},{2,3},{3,2},{4,5},{5,4},{6,7},{7,6},{8,9},{9,8},{10,11... | collective-permute-start | bytes 688136 | tf_op jit(solution)/shard_map/ppermute | solution.py:175
  2.3 8.5 %collective-permute-start.2 = (f32[56,8,128]{2,1,0:T(8,128)S(1)}, f32[56,8,128]{2,1,0:T(8,128)S(1)}, u32[]{:S(2)}, u32[]{:S(2)}) collective-permute-start(f32[56,8,128]{2,1,0:T(8,128)S(1)} %get-tuple-element.33.center_own), channel_id=1, source_target_pairs={{0,2},{1,8},{2,0},{3,10},{4,6},{5,12},{6,4},{7,14},{8,1},{9,16},{1... | collective-permute-start | bytes 688136 | tf_op jit(solution)/shard_map/ppermute | solution.py:216
  4.9 5.4 %collective-permute-start.4 = (s32[1,64]{1,0:T(1,128)S(1)}, s32[1,64]{1,0:T(1,128)S(1)}, u32[]{:S(2)}, u32[]{:S(2)}) collective-permute-start(s32[1,64]{1,0:T(1,128)S(1)} %copy-done.1), channel_id=1, source_target_pairs={{0,1},{1,0},{2,3},{3,2},{4,5},{5,4},{6,7},{7,6},{8,9},{9,8},{10,11... | collective-permute-start | bytes 776 | tf_op jit(solution)/shard_map/ppermute | solution.py:175
  5.2 5.7 %collective-permute-start.1 = (f32[56,8,128]{2,1,0:T(8,128)S(1)}, f32[56,8,128]{2,1,0:T(8,128)S(1)}, u32[]{:S(2)}, u32[]{:S(2)}) collective-permute-start(f32[56,8,128]{2,1,0:T(8,128)S(1)} %get-tuple-element.33.center_own), channel_id=1, source_target_pairs={{0,1},{1,0},{2,3},{3,2},{4,5},{5,4},{6,7},{7,6},{8,9},{9,8},{10,11... | collective-permute-start | bytes 688136 | tf_op jit(solution)/shard_map/ppermute | solution.py:175
  5.8 6.0 %collective-permute-start.3 = (f32[56,8,128]{2,1,0:T(8,128)S(1)}, f32[56,8,128]{2,1,0:T(8,128)S(1)}, u32[]{:S(2)}, u32[]{:S(2)}) collective-permute-start(f32[56,8,128]{2,1,0:T(8,128)S(1)} %collective-permute-done.center_beside), channel_id=1, source_target_pairs={{0,2},{1,8},{2,0},{3,10},{4,6},{5,12},{6,4},{7,14},{8,1},{9,16},{1... | collective-permute-start | bytes 688136 | tf_op jit(solution)/shard_map/ppermute | solution.py:216
  10.0 13.9 %collective-permute-start.8 = (f32[1176,128]{1,0:T(8,128)S(1)}, f32[1176,128]{1,0:T(8,128)S(1)}, u32[]{:S(2)}, u32[]{:S(2)}) collective-permute-start(f32[1176,128]{1,0:T(8,128)S(1)} %get-tuple-element.55), channel_id=1, source_target_pairs={{0,1},{1,0},{2,3},{3,2},{4,5},{5,4},{6,7},{7,6},{8,9},{9,8},{10,11... | collective-permute-start | bytes 1806344 | tf_op jit(solution)/shard_map/ppermute | solution.py:175
  12.1 5.5 %collective-permute-start.5 = (f32[256,128]{1,0:T(8,128)S(1)}, f32[256,128]{1,0:T(8,128)S(1)}, u32[]{:S(2)}, u32[]{:S(2)}) collective-permute-start(f32[256,128]{1,0:T(8,128)S(1)} %get-tuple-element.41), channel_id=1, source_target_pairs={{0,2},{1,3},{2,0},{3,1},{4,6},{5,7},{6,4},{7,5},{8,10},{9,11},{10,... | collective-permute-start | bytes 393224 | tf_op jit(solution)/shard_map/ppermute | solution.py:221
  13.6 8.0 %collective-permute-start.6 = (f32[256,128]{1,0:T(8,128)S(1)}, f32[256,128]{1,0:T(8,128)S(1)}, u32[]{:S(2)}, u32[]{:S(2)}) collective-permute-start(f32[256,128]{1,0:T(8,128)S(1)} %get-tuple-element.40.rest_1_), channel_id=1, source_target_pairs={{0,4},{1,5},{2,6},{3,7},{4,0},{5,1},{6,2},{7,3},{8,12},{9,13},{10,... | collective-permute-start | bytes 393224 | tf_op jit(solution)/shard_map/ppermute | solution.py:221
  15.2 6.5 %collective-permute-start.7 = (f32[256,128]{1,0:T(8,128)S(1)}, f32[256,128]{1,0:T(8,128)S(1)}, u32[]{:S(2)}, u32[]{:S(2)}) collective-permute-start(f32[256,128]{1,0:T(8,128)S(1)} %get-tuple-element.42), channel_id=1, source_target_pairs={{0,6},{1,7},{2,4},{3,5},{4,2},{5,3},{6,0},{7,1},{8,14},{9,15},{10,... | collective-permute-start | bytes 393224 | tf_op jit(solution)/shard_map/ppermute | solution.py:221
  22.5 3.7 %collective-permute-start.10 = (f32[56,8,128]{2,1,0:T(8,128)S(1)}, f32[56,8,128]{2,1,0:T(8,128)S(1)}, u32[]{:S(2)}, u32[]{:S(2)}) collective-permute-start(f32[56,8,128]{2,1,0:T(8,128)S(1)} %bitcast.17), channel_id=1, source_target_pairs={{0,1},{1,0},{2,3},{3,2},{4,5},{5,4},{6,7},{7,6},{8,9},{9,8},{10,11... | collective-permute-start | bytes 688136 | tf_op jit(solution)/shard_map/ppermute | solution.py:175
  22.6 6.1 %collective-permute-start.11 = (f32[56,8,128]{2,1,0:T(8,128)S(1)}, f32[56,8,128]{2,1,0:T(8,128)S(1)}, u32[]{:S(2)}, u32[]{:S(2)}) collective-permute-start(f32[56,8,128]{2,1,0:T(8,128)S(1)} %bitcast.18), channel_id=1, source_target_pairs={{0,2},{1,8},{2,0},{3,10},{4,6},{5,12},{6,4},{7,14},{8,1},{9,16},{1... | collective-permute-start | bytes 688136 | tf_op jit(solution)/shard_map/ppermute | solution.py:216
  24.7 4.0 %collective-permute-start.9 = (f32[56,8,128]{2,1,0:T(8,128)S(1)}, f32[56,8,128]{2,1,0:T(8,128)S(1)}, u32[]{:S(2)}, u32[]{:S(2)}) collective-permute-start(f32[56,8,128]{2,1,0:T(8,128)S(1)} %bitcast.23), channel_id=1, source_target_pairs={{0,1},{1,0},{2,3},{3,2},{4,5},{5,4},{6,7},{7,6},{8,9},{9,8},{10,11... | collective-permute-start | bytes 688136 | tf_op jit(solution)/shard_map/ppermute | solution.py:175
  25.0 6.2 %collective-permute-start.12 = (f32[56,8,128]{2,1,0:T(8,128)S(1)}, f32[56,8,128]{2,1,0:T(8,128)S(1)}, u32[]{:S(2)}, u32[]{:S(2)}) collective-permute-start(f32[56,8,128]{2,1,0:T(8,128)S(1)} %bitcast.24), channel_id=1, source_target_pairs={{0,2},{1,8},{2,0},{3,10},{4,6},{5,12},{6,4},{7,14},{8,1},{9,16},{1... | collective-permute-start | bytes 688136 | tf_op jit(solution)/shard_map/ppermute | solution.py:216
  31.3 6.2 %collective-permute-start.13 = (f32[256,128]{1,0:T(8,128)S(1)}, f32[256,128]{1,0:T(8,128)S(1)}, u32[]{:S(2)}, u32[]{:S(2)}) collective-permute-start(f32[256,128]{1,0:T(8,128)S(1)} %get-tuple-element.51), channel_id=1, source_target_pairs={{0,2},{1,3},{2,0},{3,1},{4,6},{5,7},{6,4},{7,5},{8,10},{9,11},{10,... | collective-permute-start | bytes 393224 | tf_op jit(solution)/shard_map/ppermute | solution.py:221
  32.6 6.4 %collective-permute-start.14 = (f32[256,128]{1,0:T(8,128)S(1)}, f32[256,128]{1,0:T(8,128)S(1)}, u32[]{:S(2)}, u32[]{:S(2)}) collective-permute-start(f32[256,128]{1,0:T(8,128)S(1)} %get-tuple-element.50.rest_1_), channel_id=1, source_target_pairs={{0,4},{1,5},{2,6},{3,7},{4,0},{5,1},{6,2},{7,3},{8,12},{9,13},{10,... | collective-permute-start | bytes 393224 | tf_op jit(solution)/shard_map/ppermute | solution.py:221
  33.4 7.2 %collective-permute-start.15 = (f32[256,128]{1,0:T(8,128)S(1)}, f32[256,128]{1,0:T(8,128)S(1)}, u32[]{:S(2)}, u32[]{:S(2)}) collective-permute-start(f32[256,128]{1,0:T(8,128)S(1)} %get-tuple-element.52), channel_id=1, source_target_pairs={{0,6},{1,7},{2,4},{3,5},{4,2},{5,3},{6,0},{7,1},{8,14},{9,15},{10,... | collective-permute-start | bytes 393224 | tf_op jit(solution)/shard_map/ppermute | solution.py:221
  41.5 1.6 %collective-permute-start.16 = (f32[56,8,128]{2,1,0:T(8,128)S(1)}, f32[56,8,128]{2,1,0:T(8,128)S(1)}, u32[]{:S(2)}, u32[]{:S(2)}) collective-permute-start(f32[56,8,128]{2,1,0:T(8,128)S(1)} %bitcast.26), channel_id=1, source_target_pairs={{0,1},{1,0},{2,3},{3,2},{4,5},{5,4},{6,7},{7,6},{8,9},{9,8},{10,11... | collective-permute-start | bytes 688136 | tf_op jit(solution)/shard_map/ppermute | solution.py:175

commit v5 on v4

--- a/solution.py
+++ b/solution.py
@@ -62,49 +62,86 @@
     )(*centers, *others, *after)
 
 
-def images_kernel(a, blocks, chips, cap, rows, flag, partial, halo, *rest):
+def images_kernel(a, whole, chips, cap, rows, flag, partial, halo, *rest):
     outs = rest[-len(chips) :]
     gx, gy = partial.shape[1:]
     zero = jnp.zeros((gx, gy), jnp.float32)
     inside = flag[...] > 0
     terms = rows[...]
     for m, out in zip(chips, outs):
-        for n in range(4 * m, 4 * m + 4):
-            if blocks[n][0] == a:
-                picked = [terms[0, blocks[n][1] * cap + c] for c in range(cap)]
-                made = [partial[term] - jnp.where(inside, halo[term], zero) for term in picked]
-                for c in range(cap):
-                    out[pl.ds((n - 4 * m) * gx * cap + c, gx, stride=cap), :] = made[c]
-
-
-def images(a, blocks, chips, cap, rows, flag, partial, halos, begun=(), after=()):
-    gx, gy = halos[a].shape[1:]
-    out = jax.ShapeDtypeStruct((4 * gx * cap, gy), jnp.float32)
-    return pl.pallas_call(
-        functools.partial(images_kernel, a, blocks, chips, cap),
+        for b in range(2):
+            picked = [terms[0, (2 * m + b) * cap + c] for c in range(cap)]
+            made = [partial[term] - jnp.where(inside, halo[term], zero) for term in picked]
+            for c in range(cap):
+                out[pl.ds((2 * b + a if whole else b) * gx * cap + c, gx, stride=cap), :] = made[c]
+
+
+def images(a, whole, chips, cap, rows, flag, partial, halos, begun=(), after=()):
+    gx, gy = partial[a].shape[1:]
+    out = jax.ShapeDtypeStruct(((4 if whole else 2) * gx * cap, gy), jnp.float32)
+    return pl.pallas_call(
+        functools.partial(images_kernel, a, whole, chips, cap),
         out_shape=[out] * len(chips),
         in_specs=[VMEM] * (4 + len(begun)) + [ANY] * len(after),
         out_specs=[VMEM] * len(chips),
         input_output_aliases={4 + i: i for i in range(len(begun))},
         compiler_params=PARAMS,
-        cost_estimate=cost(out.size * len(chips)),
+        cost_estimate=cost(2 * gx * cap * gy * len(chips)),
         name=f"images_{a}_{chips[0]}",
     )(rows[a], flag, partial[a], halos[a], *begun, *after)
 
 
-def product_kernel(b, cap, count, weights, modes, *rest):
-    arrays, out = rest[:count], rest[-1]
+def halves_of(full):
+    high = full.astype(jnp.bfloat16)
+    return high, (full - high.astype(jnp.float32)).astype(jnp.bfloat16)
+
+
+def early_kernel(cap, orders, *rest):
+    arrays, (high, low) = rest[:-2], rest[-2:]
+    gx = arrays[0].shape[0] // (2 * cap)
+    count = len(arrays) * cap
+    for b in range(2):
+        for g in range(gx):
+            n = b * gx + g
+            full = jnp.concatenate([arrays[at][n * cap : (n + 1) * cap, :] for at in orders[b]], axis=0)
+            high[n * count : (n + 1) * count, :], low[n * count : (n + 1) * count, :] = halves_of(full)
+
+
+def early(cap, orders, arrays):
+    rows, gy = arrays[0].shape
+    out = jax.ShapeDtypeStruct((rows * len(arrays), gy), jnp.bfloat16)
+    return pl.pallas_call(
+        functools.partial(early_kernel, cap, orders),
+        out_shape=[out, out],
+        in_specs=[VMEM] * len(arrays),
+        out_specs=[VMEM] * 2,
+        compiler_params=PARAMS,
+        cost_estimate=cost(1000),
+        name="early",
+    )(*arrays)
+
+
+def product_kernel(b, cap, order, weights, modes, *rest):
+    out = rest[-1]
     halves = weights[...].astype(jnp.bfloat16)
     both = jnp.concatenate([halves, halves], axis=1)
     count_modes, gx, gy = modes.shape
     own_terms = weights.shape[0] // count_modes
+    count = len(order) * cap
+
+    def blocks(arrays, n):
+        return jnp.concatenate([arrays[at][n * cap : (n + 1) * cap, :] for at in order], axis=0)
 
     def column(g):
-        starts = [((b * 2 + (a ^ b)) * gx + g) * cap for a in range(2)]
-        full = jnp.concatenate([array[start : start + cap, :] for array in arrays for start in starts], axis=0)
-        high = full.astype(jnp.bfloat16)
-        low = (full - high.astype(jnp.float32)).astype(jnp.bfloat16)
-        return jnp.concatenate([high, high, low, low], axis=0)
+        if rest[0].dtype == jnp.bfloat16:
+            n = b * gx + g
+            late = halves_of(blocks(rest[2:], n))
+            pairs = [(own, other[n * count : (n + 1) * count, :]) for own, other in zip(late, rest[:2])]
+        else:
+            owned = [halves_of(blocks(rest, (2 * b + a) * gx + g)) for a in range(2)]
+            pairs = list(zip(*owned))
+        parts = [part for pair in pairs for part in 2 * (pair[::-1] if b else pair)]
+        return jnp.concatenate(parts, axis=0)
 
     for g in range(0, gx, 2):
         pool = jnp.concatenate([column(g), column(g + 1)], axis=1)
@@ -117,18 +154,18 @@
             out[pl.ds(g + side, own_terms, stride=gx), :] = total
 
 
-def product(b, cap, weights, modes, arrays, after=()):
+def product(b, cap, orders, weights, modes, pool, after=()):
     count_modes, gx, gy = modes.shape
     own_terms = weights.shape[0] // count_modes
     out = pl.pallas_call(
-        functools.partial(product_kernel, b, cap, len(arrays)),
+        functools.partial(product_kernel, b, cap, orders[b]),
         out_shape=jax.ShapeDtypeStruct((own_terms * gx, gy), jnp.float32),
-        in_specs=[VMEM] * (2 + len(arrays)) + [ANY] * len(after),
+        in_specs=[VMEM] * (2 + len(pool)) + [ANY] * len(after),
         out_specs=VMEM,
         compiler_params=PARAMS,
         cost_estimate=cost(4 * weights.shape[0] * weights.shape[1] * gx * gy),
         name=f"product_{b}",
-    )(weights, modes, *arrays, *after)
+    )(weights, modes, *pool, *after)
     return out.reshape(own_terms, gx, gy)
 
 
@@ -161,6 +198,37 @@
     )(here, there)
 
 
+def from_own_kernel(cap, listed, out):
+    own = lax.axis_index("chaos")
+    length, width = listed.shape[1], out.shape[1]
+    row = listed[...]
+    if width > length:
+        row = jnp.concatenate([row, jnp.zeros((1, width - length), row.dtype)], axis=1)
+    lane = lax.broadcasted_iota(jnp.int32, row.shape, 1)
+    size = cap
+    while size < length:
+        turned = jnp.where(lane & size > 0, pltpu.roll(row, size, 1), pltpu.roll(row, width - size, 1))
+        row = jnp.where((own & (size // cap)) > 0, turned, row)
+        size *= 2
+    chip = lane // (2 * cap)
+    turned = jnp.where(chip % 2 == 1, pltpu.roll(row, width - 2 * cap, 1), pltpu.roll(row, 2 * cap, 1))
+    moved = (chip > 0) & (chip < length // (2 * cap) // 2 * 2 - 1) & (own % 2 == 1)
+    out[...] = jnp.where(moved, turned, row)
+
+
+def from_own(cap, listed):
+    width = -(-listed.shape[1] // 128) * 128
+    return pl.pallas_call(
+        functools.partial(from_own_kernel, cap),
+        out_shape=jax.ShapeDtypeStruct((1, width), listed.dtype),
+        in_specs=[VMEM],
+        out_specs=VMEM,
+        compiler_params=PARAMS,
+        cost_estimate=cost(20_000_000_000),
+        name="from_own",
+    )(listed)
+
+
 def body(slabs, owners, field, modes, send_rows, pick, mode_ids, coef):
     space, own = lax.axis_index("space"), lax.axis_index("chaos")
     core = own % 2
@@ -187,48 +255,65 @@
     inside = jnp.where(core == 0, space > 0, space + 1 < slabs)
     flag = jnp.broadcast_to(inside.astype(jnp.int32), (1, field.shape[3]))
 
-    def from_own(listed, index):
-        for bit in range(owners.bit_length() - 1):
-            size = cap << bit
-            parts = [listed[:, start : start + size] for start in range(0, pool_size, size)]
-            turned = jnp.concatenate([parts[n ^ 1] for n in range(len(parts))], axis=1)
-            listed = jnp.where((index >> bit) & 1 == 1, turned, listed)
-        return listed
-
-    rows = from_own(send_rows, own), from_own(rows_beside, own ^ 1)
-    blocks = tuple((a, 2 * m + (b ^ a)) for m in range(chips) for b in range(2) for a in range(2))
-
-    entry = ((pick // cap) ^ own) * cap + pick % cap
-    place = (entry[:, :, None] == jnp.arange(pool_size, dtype=jnp.int32)).astype(jnp.float32)
-    place = place * coef[:, :, None]
-    which = (mode_ids[:, :, None] == jnp.arange(count_modes, dtype=jnp.int32)).astype(jnp.float32)
-    weights = jnp.einsum("isp,isk->kip", place, which, precision=lax.Precision.HIGHEST)
-    weights = weights.reshape(count_modes * own_terms, pool_size)
-
+    rows = from_own(cap, send_rows), from_own(cap, rows_beside)
+    def beside_chip(n):
+        paired = (n > 0) & (n < chips // 2 * 2 - 1)
+        return jnp.where(paired, jnp.where(n % 2 == 1, n + 1, n - 1), n)
+
+    away = tuple(range(1, chips))
+    turned = [n if n == 0 or n >= chips // 2 * 2 - 1 else n + 1 if n % 2 else n - 1 for n in range(chips)]
+    to_chip = [[(i, i ^ (2 * (turned[n] if i % 2 else n))) for i in range(owners)] for n in range(chips)]
+    def orders_of(emission):
+        held = (chips - 1, *(emission.index(n) for n in away))
+        return held, tuple(held[n] for n in turned)
+
+    emission, emission_early = away[::-1], away
+    orders = orders_of(emission)
+
+    block = (pick // cap) ^ own
+    step = jnp.where(core == 1, beside_chip(block // 2), block // 2)
+    entry = (block % 2 * chips + step) * cap + pick % cap
+    taken = entry[:, :, None] == jnp.arange(pool_size, dtype=jnp.int32)
+    high = lax.reduce_precision(coef, 8, 7)
+    place = jnp.concatenate(
+        [jnp.where(taken, part[:, :, None], 0.0).astype(jnp.bfloat16) for part in (high, coef - high)], axis=2
+    )
+    which = (mode_ids[:, :, None] == jnp.arange(count_modes, dtype=jnp.int32)).astype(jnp.bfloat16)
+    weights = jnp.einsum("isp,isk->kip", place, which, preferred_element_type=jnp.float32)
+    weights = weights.reshape(count_modes * own_terms, 2 * pool_size)
+    weights = weights[:, :pool_size] + weights[:, pool_size:]
     high = lax.reduce_precision(weights, 8, 7)
     weights = jnp.concatenate([high, weights - high], axis=1)
     weights = weights.astype(jnp.bfloat16), across(weights)
     mode_plane = plane(modes, core)
 
-    order = sorted(range(1, chips), key=lambda m: (-bin(m).count("1"), m))
-
-    def exchange(centers, others):
+    def send(sent, kept, steps):
+        return [lax.ppermute(sent[n - 1], "chaos", to_chip[n]) for n in steps] + [kept]
+
+    def exchange(whole, centers, others):
         halos = [lax.ppermute(center, AXES, to_slab) for center in centers]
         inputs = (cap, rows, flag, local(centers, others, halos[:1]), halos[::-1])
-        begun = images(1, blocks, (*order, 0), *inputs)
-        sent = images(0, blocks, order, *inputs, begun[:-1])
-        (kept,) = images(0, blocks, (0,), *inputs, begun[-1:], sent[-1:])
-        arrays = {m: lax.ppermute(x, "chaos", [(i, i ^ (2 * m)) for i in range(owners)]) for m, x in zip(order, sent)}
-        return [kept, *(arrays[m] for m in range(1, chips))]
-
-    pool = exchange((here, here_beside), (there, there_beside))
-    own_first = product(0, cap, weights[0], mode_plane, pool)
-    first = own_first, product(1, cap, weights[1], mode_plane, pool, (own_first,))
+        if whole:
+            begun = images(1, True, (*away, 0), *inputs)
+            sent = images(0, True, away, *inputs, begun[:-1])
+            (kept,) = images(0, True, (0,), *inputs, begun[-1:], sent[-1:])
+            return send(sent, kept, emission)
+        pool, after = [], ()
+        for a in (1, 0):
+            sent = images(a, False, away, *inputs, (), after)
+            (kept,) = images(a, False, (0,), *inputs, (), sent[-1:])
+            pool.append(send(sent, kept, emission_early if a else emission))
+            after = sent[-1:]
+        return [*early(cap, orders_of(emission_early), pool[0]), *pool[1]]
+
+    pool = exchange(True, (here, here_beside), (there, there_beside))
+    own_first = product(0, cap, orders, weights[0], mode_plane, pool)
+    first = own_first, product(1, cap, orders, weights[1], mode_plane, pool, (own_first,))
     beside = [across(x) for x in first]
     out, token = write(own_first, beside[1], True)
-    pool = exchange(first, beside[::-1])
-    theirs = across(product(1, cap, weights[1], mode_plane, pool, (token,)))
-    mine = product(0, cap, weights[0], mode_plane, pool)
+    pool = exchange(False, first, beside[::-1])
+    theirs = across(product(1, cap, orders, weights[1], mode_plane, pool, (token,)))
+    mine = product(0, cap, orders, weights[0], mode_plane, pool)
     return out, *write(mine, theirs, False)
 
 

time: 44 us -> 43.2 us (0.982)
  waiting for transfers between devices: 16.3 us -> 11.7 us
  starting transfers between devices: 15.3 us -> 19.1 us
  matrix products: 1.98 us -> 0.59 us
  other arithmetic: 0.68 us -> 2.02 us
  Pallas kernels: 6.45 us -> 7.11 us
  local copies, waits for them, and re-layouts: 2.17 us -> 1.64 us
    ppermute x6 -> x9, starting transfers between devices: 7.11 us -> 10.7 us  [send(): lax.ppermute(sent[n - 1], 'chaos', to_chip[n])]
    ppermute x6 -> x9, waiting for transfers between devices: 10.8 us -> 8.37 us  [send(): lax.ppermute(sent[n - 1], 'chaos', to_chip[n])]
    ppermute x4, waiting for transfers between devices: 4.87 us -> 2.63 us  [exchange(): halos = [lax.ppermute(center, AXES, to_slab) for center in centers]]
    convert_element_type x0 -> x1, other arithmetic: none -> 1.47 us  [body(): jnp.where(taken, part[:, :, None], 0.0).astype(jnp.bfloat16)]
    dot_general x1, matrix products: 1.98 us -> 0.59 us  [body(): jnp.einsum('isp,isk->kip', place, which, preferred_element_type=jnp.float32)]
    pallas_call x10 -> x14, Pallas kernels: 4.24 us -> 4.92 us  [the longest x4 3.23 us: product(): pl.pallas_call(functools.partial(product_kernel, b, cap, orders[b]), out_...]
    slice x6 -> x0, local copies, waits for them, and re-layouts: 0.45 us -> none  [from_own(): listed[:, start:start + size]]
  transfers between devices with their start and end apart: 17 -> 20, of which waited for: 9 -> 9; matrix products, arithmetic and copies ran while one was open for 8% -> 7% of each run, Pallas kernels for 11% -> 13%
where the time goes in v5:
time: 43.2 us; the launch traced here: 43.1 us
  starting transfers between devices  19.1 us (44%)
  waiting for transfers between devices  11.7 us (27%)
  Pallas kernels  7.11 us (16%)
  other arithmetic  2.02 us (5%)
  local copies, waits for them, and re-layouts  1.64 us (4%)
  between operations  0.91 us (2%)
  matrix products  0.59 us (1%)
    ppermute x9, starting transfers between devices, send(): lax.ppermute(sent[n - 1], 'chaos', to_chip[n])  10.7 us
    ppermute x9, waiting for transfers between devices, send(): lax.ppermute(sent[n - 1], 'chaos', to_chip[n])  8.37 us
    ppermute x4, starting transfers between devices, exchange(): halos = [lax.ppermute(center, AXES, to_slab) for center in centers]  6.9 us
    pallas_call x4, Pallas kernels, product(): pl.pallas_call(functools.partial(product_kernel, b, cap, orders[b]), out_...  3.23 us
    ppermute x4, waiting for transfers between devices, exchange(): halos = [lax.ppermute(center, AXES, to_slab) for center in centers]  2.63 us
    ppermute x7, starting transfers between devices, across(): return lax.ppermute(array, 'chaos', [(i, i ^ 1) for i in range(owners)])  1.58 us
    pallas_call x2, Pallas kernels, write(): pl.pallas_call(write_kernel, out_shape=[jax.ShapeDtypeStruct((terms, 2, g...  1.57 us
    convert_element_type x1, other arithmetic, body(): jnp.where(taken, part[:, :, None], 0.0).astype(jnp.bfloat16)  1.47 us
  transfers between devices with their start and end apart: 20, of which 9 were waited for; matrix products, arithmetic and copies ran while one was open for 7% of the time, Pallas kernels for 13%

profile of v5, /device:TPU:0, one launch (start us, length us, event | category | flops | bytes accessed | tf_op | source)
XLA Modules:
  0.0 43.1 jit_solution(10106208492054732559)
XLA Ops:
  0.6 0.0 copy-start
  0.7 1.1 %dynamic-slice_bitcast_fusion = (f32[56,8,128]{2,1,0:T(8,128)S(1)}, f32[56,8,128]{2,1,0:T(8,128)S(1)}) fusion(f32[56,2,8,128]{3,2,1,0:T(8,128)} %param.6, s32[]{:T(128)S(6)} %select_n.66, s32[]{:T(128)S(6)} %select_n.65), kind=kLoop, calls=%fused_computation.12 | loop fusion | bytes 917512 | tf_op jit(solution)/shard_map/jit(dynamic_index_in_dim)/squeeze | solution.py:246
  1.8 0.5 %collective-permute-start = (f32[56,8,128]{2,1,0:T(8,128)S(1)}, f32[56,8,128]{2,1,0:T(8,128)S(1)}, u32[]{:S(2)}, u32[]{:S(2)}) collective-permute-start(f32[56,8,128]{2,1,0:T(8,128)S(1)} %get-tuple-element.60.other_own), channel_id=1, source_target_pairs={{0,1},{1,0},{2,3},{3,2},{4,5},{5,4},{6,7},{7,6},{8,9},{9,8},{10,11... | collective-permute-start | bytes 688136 | tf_op jit(solution)/shard_map/ppermute | solution.py:243
  2.3 2.6 %collective-permute-start.2 = (f32[56,8,128]{2,1,0:T(8,128)S(1)}, f32[56,8,128]{2,1,0:T(8,128)S(1)}, u32[]{:S(2)}, u32[]{:S(2)}) collective-permute-start(f32[56,8,128]{2,1,0:T(8,128)S(1)} %get-tuple-element.34.center_own), channel_id=1, source_target_pairs={{0,2},{1,8},{2,0},{3,10},{4,6},{5,12},{6,4},{7,14},{8,1},{9,16},{1... | collective-permute-start | bytes 688136 | tf_op jit(solution)/shard_map/ppermute | solution.py:294
  4.9 0.0 collective-permute-done.center_beside
  4.9 0.3 collective-permute-start.4
  5.2 0.3 from_own.2.rows
  5.4 0.3 collective-permute-start.1
  5.8 1.3 %collective-permute-start.3 = (f32[56,8,128]{2,1,0:T(8,128)S(1)}, f32[56,8,128]{2,1,0:T(8,128)S(1)}, u32[]{:S(2)}, u32[]{:S(2)}) collective-permute-start(f32[56,8,128]{2,1,0:T(8,128)S(1)} %collective-permute-done.center_beside), channel_id=1, source_target_pairs={{0,2},{1,8},{2,0},{3,10},{4,6},{5,12},{6,4},{7,14},{8,1},{9,16},{1... | collective-permute-start | bytes 688136 | tf_op jit(solution)/shard_map/ppermute | solution.py:294
  7.1 0.1 fusion.9
  7.2 0.1 copy.13
  7.3 0.1 copy.14
  7.4 0.1 copy.15
  7.5 0.1 copy.12
  7.6 1.5 %select_convert_fusion.1 = (bf16[56,41,64]{2,1,0:T(8,128)(2,1)S(1)}, bf16[56,41,64]{2,1,0:T(8,128)(2,1)S(1)}) fusion(bf16[56,41]{1,0:T(8,128)(2,1)S(1)} %copy.14, s32[56,41]{1,0:T(8,128)S(1)} %copy.13, bf16[56,41]{1,0:T(8,128)(2,1)S(1)} %copy.15), kind=kLoop, calls=%fused_computation.1 | loop fusion | flops 440832 | bytes 606144 | tf_op jit(solution)/shard_map/convert_element_type | solution.py:279
  9.0 0.6 %convolution_bitcast_fusion = f32[21,56,128]{2,0,1:T(8,128)S(1)} fusion(bf16[56,41,64]{2,1,0:T(8,128)(2,1)S(1)} %get-tuple-element.63, bf16[56,41,64]{2,1,0:T(8,128)(2,1)S(1)} %get-tuple-element.62, s32[56,41]{1,0:T(8,128)S(1)} %copy.12), kind=kOutput, calls=%fused_computation.3 | convolution fusion | flops 13567064 | bytes 1199072 | tf_op jit(solution)/shard_map/isp,isk->kip/dot_general | solution.py:282
  9.6 0.1 copy.16
  9.8 0.2 fusion.4
  10.0 0.2 fusion.17
  10.2 0.3 collective-permute-start.8
  10.5 0.0 collective-permute-done.4.listed
  10.5 0.3 from_own.3.rows
  10.8 0.0 collective-permute-done.2.rest_0_.halo
  10.8 0.0 collective-permute-done.1.other_beside
  10.8 0.3 local.2
  11.1 0.2 images_1_1.2
  11.3 0.5 %collective-permute-done.3.halo = f32[56,8,128]{2,1,0:T(8,128)S(1)} collective-permute-done((f32[56,8,128]{2,1,0:T(8,128)S(1)}, f32[56,8,128]{2,1,0:T(8,128)S(1)}, u32[]{:S(2)}, u32[]{:S(2)}) %collective-permute-start.3) | collective-permute-done | bytes 229408 | tf_op jit(solution)/shard_map/ppermute | solution.py:294
  11.8 0.2 images_0_1.2
  12.0 2.6 %collective-permute-start.5 = (f32[256,128]{1,0:T(8,128)S(1)}, f32[256,128]{1,0:T(8,128)S(1)}, u32[]{:S(2)}, u32[]{:S(2)}) collective-permute-start(f32[256,128]{1,0:T(8,128)S(1)} %get-tuple-element.40.rest_1_), channel_id=1, source_target_pairs={{0,6},{1,7},{2,4},{3,5},{4,2},{5,3},{6,0},{7,1},{8,14},{9,15},{10,... | collective-permute-start | bytes 393224 | tf_op jit(solution)/shard_map/ppermute | solution.py:291
  14.6 0.5 %collective-permute-start.6 = (f32[256,128]{1,0:T(8,128)S(1)}, f32[256,128]{1,0:T(8,128)S(1)}, u32[]{:S(2)}, u32[]{:S(2)}) collective-permute-start(f32[256,128]{1,0:T(8,128)S(1)} %get-tuple-element.41), channel_id=1, source_target_pairs={{0,4},{1,3},{2,6},{3,1},{4,0},{5,7},{6,2},{7,5},{8,12},{9,11},{10,... | collective-permute-start | bytes 393224 | tf_op jit(solution)/shard_map/ppermute | solution.py:291
  15.1 0.4 %collective-permute-start.7 = (f32[256,128]{1,0:T(8,128)S(1)}, f32[256,128]{1,0:T(8,128)S(1)}, u32[]{:S(2)}, u32[]{:S(2)}) collective-permute-start(f32[256,128]{1,0:T(8,128)S(1)} %get-tuple-element.42), channel_id=1, source_target_pairs={{0,2},{1,5},{2,0},{3,7},{4,6},{5,1},{6,4},{7,3},{8,10},{9,13},{10,... | collective-permute-start | bytes 393224 | tf_op jit(solution)/shard_map/ppermute | solution.py:291
  15.5 0.1 images_0_0.2.rest_3_
  15.7 3.6 %collective-permute-done.5.rest_0_ = f32[256,128]{1,0:T(8,128)S(1)} collective-permute-done((f32[256,128]{1,0:T(8,128)S(1)}, f32[256,128]{1,0:T(8,128)S(1)}, u32[]{:S(2)}, u32[]{:S(2)}) %collective-permute-start.5) | collective-permute-done | bytes 131104 | tf_op jit(solution)/shard_map/ppermute | solution.py:291
  19.3 1.9 %collective-permute-done.6.rest_1_ = f32[256,128]{1,0:T(8,128)S(1)} collective-permute-done((f32[256,128]{1,0:T(8,128)S(1)}, f32[256,128]{1,0:T(8,128)S(1)}, u32[]{:S(2)}, u32[]{:S(2)}) %collective-permute-start.6) | collective-permute-done | bytes 131104 | tf_op jit(solution)/shard_map/ppermute | solution.py:291
  21.1 0.3 collective-permute-done.7.rest_2_
  21.4 0.8 %product_0.2 = f32[448,128]{1,0:T(8,128)S(1)} custom-call(bf16[1176,128]{1,0:T(8,128)(2,1)S(1)} %get-tuple-element.56.weights, f32[21,8,128]{2,1,0:T(8,128)S(1)} %dynamic-slice_bitcast_fusion.2.modes, f32[256,128]{1,0:T(8,128)S(1)} %collective-permute-done.5.rest_0_, f32[256,128]{1,0:T(8,128)S(1)} %collective-permute-done.6.rest_1_, ...), custom_call_target="tpu_custom_call" | custom-call | flops 616562688 | bytes 1048576 | tf_op jit(solution)/shard_map/product_0/pallas_call | solution.py:160
  22.2 0.1 collective-permute-start.10
  22.3 1.6 %collective-permute-start.11 = (f32[56,8,128]{2,1,0:T(8,128)S(1)}, f32[56,8,128]{2,1,0:T(8,128)S(1)}, u32[]{:S(2)}, u32[]{:S(2)}) collective-permute-start(f32[56,8,128]{2,1,0:T(8,128)S(1)} %bitcast.14), channel_id=1, source_target_pairs={{0,2},{1,8},{2,0},{3,10},{4,6},{5,12},{6,4},{7,14},{8,1},{9,16},{1... | collective-permute-start | bytes 688136 | tf_op jit(solution)/shard_map/ppermute | solution.py:294
  23.9 0.0 collective-permute-done.8.weights
  23.9 0.8 %product_1.2 = f32[448,128]{1,0:T(8,128)S(1)} custom-call(f32[1176,128]{1,0:T(8,128)S(1)} %collective-permute-done.8.weights, f32[21,8,128]{2,1,0:T(8,128)S(1)} %dynamic-slice_bitcast_fusion.2.modes, f32[256,128]{1,0:T(8,128)S(1)} %collective-permute-done.5.rest_0_, f32[256,128]{1,0:T(8,128)S(1)} %collective-permute-done.6.rest_1_, ...), custom_call_target="tpu_custom_call" | custom-call | flops 616562688 | bytes 1048576 | tf_op jit(solution)/shard_map/product_1/pallas_call | solution.py:160
  24.7 0.1 collective-permute-start.9
  24.8 1.4 %collective-permute-start.15 = (f32[56,8,128]{2,1,0:T(8,128)S(1)}, f32[56,8,128]{2,1,0:T(8,128)S(1)}, u32[]{:S(2)}, u32[]{:S(2)}) collective-permute-start(f32[56,8,128]{2,1,0:T(8,128)S(1)} %bitcast.20), channel_id=1, source_target_pairs={{0,2},{1,8},{2,0},{3,10},{4,6},{5,12},{6,4},{7,14},{8,1},{9,16},{1... | collective-permute-start | bytes 688136 | tf_op jit(solution)/shard_map/ppermute | solution.py:294
  26.2 0.0 collective-permute-done.10.other_beside
  26.2 2.2 %collective-permute-done.11.rest_0_.halo = f32[56,8,128]{2,1,0:T(8,128)S(1)} collective-permute-done((f32[56,8,128]{2,1,0:T(8,128)S(1)}, f32[56,8,128]{2,1,0:T(8,128)S(1)}, u32[]{:S(2)}, u32[]{:S(2)}) %collective-permute-start.11) | collective-permute-done | bytes 229408 | tf_op jit(solution)/shard_map/ppermute | solution.py:294
  28.4 0.3 local.3
  28.7 0.2 images_1_1.3
  28.9 1.6 %collective-permute-start.12 = (f32[128,128]{1,0:T(8,128)S(1)}, f32[128,128]{1,0:T(8,128)S(1)}, u32[]{:S(2)}, u32[]{:S(2)}) collective-permute-start(f32[128,128]{1,0:T(8,128)S(1)} %get-tuple-element.46), channel_id=1, source_target_pairs={{0,2},{1,5},{2,0},{3,7},{4,6},{5,1},{6,4},{7,3},{8,10},{9,13},{10,... | collective-permute-start | bytes 196616 | tf_op jit(solution)/shard_map/ppermute | solution.py:291
  30.5 1.4 %collective-permute-start.14 = (f32[128,128]{1,0:T(8,128)S(1)}, f32[128,128]{1,0:T(8,128)S(1)}, u32[]{:S(2)}, u32[]{:S(2)}) collective-permute-start(f32[128,128]{1,0:T(8,128)S(1)} %get-tuple-element.48.rest_0_), channel_id=1, source_target_pairs={{0,6},{1,7},{2,4},{3,5},{4,2},{5,3},{6,0},{7,1},{8,14},{9,15},{10,... | collective-permute-start | bytes 196616 | tf_op jit(solution)/shard_map/ppermute | solution.py:291
  31.9 0.2 images_0_1.3
  32.1 1.6 %collective-permute-start.16 = (f32[128,128]{1,0:T(8,128)S(1)}, f32[128,128]{1,0:T(8,128)S(1)}, u32[]{:S(2)}, u32[]{:S(2)}) collective-permute-start(f32[128,128]{1,0:T(8,128)S(1)} %get-tuple-element.52.rest_0_), channel_id=1, source_target_pairs={{0,6},{1,7},{2,4},{3,5},{4,2},{5,3},{6,0},{7,1},{8,14},{9,15},{10,... | collective-permute-start | bytes 196616 | tf_op jit(solution)/shard_map/ppermute | solution.py:291
  33.6 1.5 %collective-permute-start.13 = (f32[128,128]{1,0:T(8,128)S(1)}, f32[128,128]{1,0:T(8,128)S(1)}, u32[]{:S(2)}, u32[]{:S(2)}) collective-permute-start(f32[128,128]{1,0:T(8,128)S(1)} %get-tuple-element.47), channel_id=1, source_target_pairs={{0,4},{1,3},{2,6},{3,1},{4,0},{5,7},{6,2},{7,5},{8,12},{9,11},{10,... | collective-permute-start | bytes 196616 | tf_op jit(solution)/shard_map/ppermute | solution.py:291
  35.1 0.6 %collective-permute-start.17 = (f32[128,128]{1,0:T(8,128)S(1)}, f32[128,128]{1,0:T(8,128)S(1)}, u32[]{:S(2)}, u32[]{:S(2)}) collective-permute-start(f32[128,128]{1,0:T(8,128)S(1)} %get-tuple-element.53), channel_id=1, source_target_pairs={{0,4},{1,3},{2,6},{3,1},{4,0},{5,7},{6,2},{7,5},{8,12},{9,11},{10,... | collective-permute-start | bytes 196616 | tf_op jit(solution)/shard_map/ppermute | solution.py:291
  35.7 0.5 %collective-permute-start.18 = (f32[128,128]{1,0:T(8,128)S(1)}, f32[128,128]{1,0:T(8,128)S(1)}, u32[]{:S(2)}, u32[]{:S(2)}) collective-permute-start(f32[128,128]{1,0:T(8,128)S(1)} %get-tuple-element.54), channel_id=1, source_target_pairs={{0,2},{1,5},{2,0},{3,7},{4,6},{5,1},{6,4},{7,3},{8,10},{9,13},{10,... | collective-permute-start | bytes 196616 | tf_op jit(solution)/shard_map/ppermute | solution.py:291
  36.2 0.1 images_0_0.3.rest_5_
  36.3 0.1 images_1_0.1.rest_3_
  36.5 0.8 %write.2 = (f32[56,2,8,128]{3,2,1,0:T(8,128)}, f32[8,128]{1,0:T(8,128)S(1)}) custom-call(f32[56,8,128]{2,1,0:T(8,128)S(1)} %bitcast.17, f32[56,8,128]{2,1,0:T(8,128)S(1)} %collective-permute-done.9.there.other_own), custom_call_target="tpu_custom_call" | custom-call | tf_op jit(solution)/shard_map/write/pallas_call | solution.py:189
  37.3 1.7 %collective-permute-done.13.rest_1_ = f32[128,128]{1,0:T(8,128)S(1)} collective-permute-done((f32[128,128]{1,0:T(8,128)S(1)}, f32[128,128]{1,0:T(8,128)S(1)}, u32[]{:S(2)}, u32[]{:S(2)}) %collective-permute-start.13) | collective-permute-done | bytes 65568 | tf_op jit(solution)/shard_map/ppermute | solution.py:291
  39.0 0.8 %collective-permute-done.17.rest_3_ = f32[128,128]{1,0:T(8,128)S(1)} collective-permute-done((f32[128,128]{1,0:T(8,128)S(1)}, f32[128,128]{1,0:T(8,128)S(1)}, u32[]{:S(2)}, u32[]{:S(2)}) %collective-permute-start.17) | collective-permute-done | bytes 65568 | tf_op jit(solution)/shard_map/ppermute | solution.py:291
  39.7 0.2 collective-permute-done.18.rest_4_
  39.9 0.8 %product_1.3 = f32[448,128]{1,0:T(8,128)S(1)} custom-call(f32[1176,128]{1,0:T(8,128)S(1)} %collective-permute-done.8.weights, f32[21,8,128]{2,1,0:T(8,128)S(1)} %dynamic-slice_bitcast_fusion.2.modes, bf16[512,128]{1,0:T(8,128)(2,1)S(1)} %get-tuple-element.49.rest_0_, bf16[512,128]{1,0:T(8,128)(2,1)S(1)} %get-tuple-element.50.rest_1_, ...), custom_call_target="tpu_custom_call" | custom-call | flops 616562688 | bytes 1048576 | tf_op jit(solution)/shard_map/product_1/pallas_call | solution.py:160
  40.7 0.1 collective-permute-start.19
  40.8 0.8 %product_0.3 = f32[448,128]{1,0:T(8,128)S(1)} custom-call(bf16[1176,128]{1,0:T(8,128)(2,1)S(1)} %get-tuple-element.56.weights, f32[21,8,128]{2,1,0:T(8,128)S(1)} %dynamic-slice_bitcast_fusion.2.modes, bf16[512,128]{1,0:T(8,128)(2,1)S(1)} %get-tuple-element.49.rest_0_, bf16[512,128]{1,0:T(8,128)(2,1)S(1)} %get-tuple-element.50.rest_1_, ...), custom_call_target="tpu_custom_call" | custom-call | flops 616562688 | bytes 1048576 | tf_op jit(solution)/shard_map/product_0/pallas_call | solution.py:160
  41.6 0.7 %collective-permute-done.19.there = f32[56,8,128]{2,1,0:T(8,128)S(1)} collective-permute-done((f32[56,8,128]{2,1,0:T(8,128)S(1)}, f32[56,8,128]{2,1,0:T(8,128)S(1)}, u32[]{:S(2)}, u32[]{:S(2)}) %collective-permute-start.19) | collective-permute-done | bytes 229408 | tf_op jit(solution)/shard_map/ppermute | solution.py:243
  42.3 0.8 %write.3 = f32[56,2,8,128]{3,2,1,0:T(8,128)} custom-call(f32[56,8,128]{2,1,0:T(8,128)S(1)} %bitcast.18, f32[56,8,128]{2,1,0:T(8,128)S(1)} %collective-permute-done.19.there), custom_call_target="tpu_custom_call" | custom-call | tf_op jit(solution)/shard_map/write/pallas_call | solution.py:189
  (18 shorter events, 0.1 us)
Async XLA Ops:
  0.6 14.9 %copy-start = (f32[21,2,8,128]{3,2,1,0:T(8,128)S(1)}, f32[21,2,8,128]{3,2,1,0:T(8,128)}, u32[]{:S(2)}) copy-start(f32[21,2,8,128]{3,2,1,0:T(8,128)} %param.7) | copy-start | bytes 516100
  0.6 4.2 %copy-start.1 = (s32[1,64]{1,0:T(1,128)S(1)}, s32[1,64]{1,0:T(1,128)}, u32[]{:S(2)}) copy-start(s32[1,64]{1,0:T(1,128)} %listed) | copy-start | bytes 772
  1.8 3.1 %collective-permute-start = (f32[56,8,128]{2,1,0:T(8,128)S(1)}, f32[56,8,128]{2,1,0:T(8,128)S(1)}, u32[]{:S(2)}, u32[]{:S(2)}) collective-permute-start(f32[56,8,128]{2,1,0:T(8,128)S(1)} %get-tuple-element.60.other_own), channel_id=1, source_target_pairs={{0,1},{1,0},{2,3},{3,2},{4,5},{5,4},{6,7},{7,6},{8,9},{9,8},{10,11... | collective-permute-start | bytes 688136 | tf_op jit(solution)/shard_map/ppermute | solution.py:243
  2.3 8.5 %collective-permute-start.2 = (f32[56,8,128]{2,1,0:T(8,128)S(1)}, f32[56,8,128]{2,1,0:T(8,128)S(1)}, u32[]{:S(2)}, u32[]{:S(2)}) collective-permute-start(f32[56,8,128]{2,1,0:T(8,128)S(1)} %get-tuple-element.34.center_own), channel_id=1, source_target_pairs={{0,2},{1,8},{2,0},{3,10},{4,6},{5,12},{6,4},{7,14},{8,1},{9,16},{1... | collective-permute-start | bytes 688136 | tf_op jit(solution)/shard_map/ppermute | solution.py:294
  4.9 2.2 %copy-start.2 = (s32[56,41]{0,1:T(8,128)S(1)}, s32[56,41]{0,1:T(8,128)}, u32[]{:S(2)}) copy-start(s32[56,41]{0,1:T(8,128)} %param.9) | copy-start | bytes 27556
  4.9 2.4 %copy-start.3 = (f32[56,41]{0,1:T(8,128)S(1)}, f32[56,41]{0,1:T(8,128)}, u32[]{:S(2)}) copy-start(f32[56,41]{0,1:T(8,128)} %param.11) | copy-start | bytes 27556
  4.9 2.6 %copy-start.4 = (s32[56,41]{0,1:T(8,128)S(1)}, s32[56,41]{0,1:T(8,128)}, u32[]{:S(2)}) copy-start(s32[56,41]{0,1:T(8,128)} %param.10) | copy-start | bytes 27556
  4.9 5.6 %collective-permute-start.4 = (s32[1,64]{1,0:T(1,128)S(1)}, s32[1,64]{1,0:T(1,128)S(1)}, u32[]{:S(2)}, u32[]{:S(2)}) collective-permute-start(s32[1,64]{1,0:T(1,128)S(1)} %copy-done.1), channel_id=1, source_target_pairs={{0,1},{1,0},{2,3},{3,2},{4,5},{5,4},{6,7},{7,6},{8,9},{9,8},{10,11... | collective-permute-start | bytes 776 | tf_op jit(solution)/shard_map/ppermute | solution.py:243
  5.4 5.4 %collective-permute-start.1 = (f32[56,8,128]{2,1,0:T(8,128)S(1)}, f32[56,8,128]{2,1,0:T(8,128)S(1)}, u32[]{:S(2)}, u32[]{:S(2)}) collective-permute-start(f32[56,8,128]{2,1,0:T(8,128)S(1)} %get-tuple-element.34.center_own), channel_id=1, source_target_pairs={{0,1},{1,0},{2,3},{3,2},{4,5},{5,4},{6,7},{7,6},{8,9},{9,8},{10,11... | collective-permute-start | bytes 688136 | tf_op jit(solution)/shard_map/ppermute | solution.py:243
  5.8 6.0 %collective-permute-start.3 = (f32[56,8,128]{2,1,0:T(8,128)S(1)}, f32[56,8,128]{2,1,0:T(8,128)S(1)}, u32[]{:S(2)}, u32[]{:S(2)}) collective-permute-start(f32[56,8,128]{2,1,0:T(8,128)S(1)} %collective-permute-done.center_beside), channel_id=1, source_target_pairs={{0,2},{1,8},{2,0},{3,10},{4,6},{5,12},{6,4},{7,14},{8,1},{9,16},{1... | collective-permute-start | bytes 688136 | tf_op jit(solution)/shard_map/ppermute | solution.py:294
  10.2 13.6 %collective-permute-start.8 = (f32[1176,128]{1,0:T(8,128)S(1)}, f32[1176,128]{1,0:T(8,128)S(1)}, u32[]{:S(2)}, u32[]{:S(2)}) collective-permute-start(f32[1176,128]{1,0:T(8,128)S(1)} %get-tuple-element.57), channel_id=1, source_target_pairs={{0,1},{1,0},{2,3},{3,2},{4,5},{5,4},{6,7},{7,6},{8,9},{9,8},{10,11... | collective-permute-start | bytes 1806344 | tf_op jit(solution)/shard_map/ppermute | solution.py:243
  12.0 7.3 %collective-permute-start.5 = (f32[256,128]{1,0:T(8,128)S(1)}, f32[256,128]{1,0:T(8,128)S(1)}, u32[]{:S(2)}, u32[]{:S(2)}) collective-permute-start(f32[256,128]{1,0:T(8,128)S(1)} %get-tuple-element.40.rest_1_), channel_id=1, source_target_pairs={{0,6},{1,7},{2,4},{3,5},{4,2},{5,3},{6,0},{7,1},{8,14},{9,15},{10,... | collective-permute-start | bytes 393224 | tf_op jit(solution)/shard_map/ppermute | solution.py:291
  14.6 6.6 %collective-permute-start.6 = (f32[256,128]{1,0:T(8,128)S(1)}, f32[256,128]{1,0:T(8,128)S(1)}, u32[]{:S(2)}, u32[]{:S(2)}) collective-permute-start(f32[256,128]{1,0:T(8,128)S(1)} %get-tuple-element.41), channel_id=1, source_target_pairs={{0,4},{1,3},{2,6},{3,1},{4,0},{5,7},{6,2},{7,5},{8,12},{9,11},{10,... | collective-permute-start | bytes 393224 | tf_op jit(solution)/shard_map/ppermute | solution.py:291
  15.1 6.3 %collective-permute-start.7 = (f32[256,128]{1,0:T(8,128)S(1)}, f32[256,128]{1,0:T(8,128)S(1)}, u32[]{:S(2)}, u32[]{:S(2)}) collective-permute-start(f32[256,128]{1,0:T(8,128)S(1)} %get-tuple-element.42), channel_id=1, source_target_pairs={{0,2},{1,5},{2,0},{3,7},{4,6},{5,1},{6,4},{7,3},{8,10},{9,13},{10,... | collective-permute-start | bytes 393224 | tf_op jit(solution)/shard_map/ppermute | solution.py:291
  22.2 4.0 %collective-permute-start.10 = (f32[56,8,128]{2,1,0:T(8,128)S(1)}, f32[56,8,128]{2,1,0:T(8,128)S(1)}, u32[]{:S(2)}, u32[]{:S(2)}) collective-permute-start(f32[56,8,128]{2,1,0:T(8,128)S(1)} %bitcast.13), channel_id=1, source_target_pairs={{0,1},{1,0},{2,3},{3,2},{4,5},{5,4},{6,7},{7,6},{8,9},{9,8},{10,11... | collective-permute-start | bytes 688136 | tf_op jit(solution)/shard_map/ppermute | solution.py:243
  22.3 6.1 %collective-permute-start.11 = (f32[56,8,128]{2,1,0:T(8,128)S(1)}, f32[56,8,128]{2,1,0:T(8,128)S(1)}, u32[]{:S(2)}, u32[]{:S(2)}) collective-permute-start(f32[56,8,128]{2,1,0:T(8,128)S(1)} %bitcast.14), channel_id=1, source_target_pairs={{0,2},{1,8},{2,0},{3,10},{4,6},{5,12},{6,4},{7,14},{8,1},{9,16},{1... | collective-permute-start | bytes 688136 | tf_op jit(solution)/shard_map/ppermute | solution.py:294
  24.7 3.7 %collective-permute-start.9 = (f32[56,8,128]{2,1,0:T(8,128)S(1)}, f32[56,8,128]{2,1,0:T(8,128)S(1)}, u32[]{:S(2)}, u32[]{:S(2)}) collective-permute-start(f32[56,8,128]{2,1,0:T(8,128)S(1)} %bitcast.19), channel_id=1, source_target_pairs={{0,1},{1,0},{2,3},{3,2},{4,5},{5,4},{6,7},{7,6},{8,9},{9,8},{10,11... | collective-permute-start | bytes 688136 | tf_op jit(solution)/shard_map/ppermute | solution.py:243
  24.8 7.1 %collective-permute-start.15 = (f32[56,8,128]{2,1,0:T(8,128)S(1)}, f32[56,8,128]{2,1,0:T(8,128)S(1)}, u32[]{:S(2)}, u32[]{:S(2)}) collective-permute-start(f32[56,8,128]{2,1,0:T(8,128)S(1)} %bitcast.20), channel_id=1, source_target_pairs={{0,2},{1,8},{2,0},{3,10},{4,6},{5,12},{6,4},{7,14},{8,1},{9,16},{1... | collective-permute-start | bytes 688136 | tf_op jit(solution)/shard_map/ppermute | solution.py:294
  28.9 6.8 %collective-permute-start.12 = (f32[128,128]{1,0:T(8,128)S(1)}, f32[128,128]{1,0:T(8,128)S(1)}, u32[]{:S(2)}, u32[]{:S(2)}) collective-permute-start(f32[128,128]{1,0:T(8,128)S(1)} %get-tuple-element.46), channel_id=1, source_target_pairs={{0,2},{1,5},{2,0},{3,7},{4,6},{5,1},{6,4},{7,3},{8,10},{9,13},{10,... | collective-permute-start | bytes 196616 | tf_op jit(solution)/shard_map/ppermute | solution.py:291
  30.5 8.5 %collective-permute-start.14 = (f32[128,128]{1,0:T(8,128)S(1)}, f32[128,128]{1,0:T(8,128)S(1)}, u32[]{:S(2)}, u32[]{:S(2)}) collective-permute-start(f32[128,128]{1,0:T(8,128)S(1)} %get-tuple-element.48.rest_0_), channel_id=1, source_target_pairs={{0,6},{1,7},{2,4},{3,5},{4,2},{5,3},{6,0},{7,1},{8,14},{9,15},{10,... | collective-permute-start | bytes 196616 | tf_op jit(solution)/shard_map/ppermute | solution.py:291
  32.1 6.9 %collective-permute-start.16 = (f32[128,128]{1,0:T(8,128)S(1)}, f32[128,128]{1,0:T(8,128)S(1)}, u32[]{:S(2)}, u32[]{:S(2)}) collective-permute-start(f32[128,128]{1,0:T(8,128)S(1)} %get-tuple-element.52.rest_0_), channel_id=1, source_target_pairs={{0,6},{1,7},{2,4},{3,5},{4,2},{5,3},{6,0},{7,1},{8,14},{9,15},{10,... | collective-permute-start | bytes 196616 | tf_op jit(solution)/shard_map/ppermute | solution.py:291
  33.6 5.3 %collective-permute-start.13 = (f32[128,128]{1,0:T(8,128)S(1)}, f32[128,128]{1,0:T(8,128)S(1)}, u32[]{:S(2)}, u32[]{:S(2)}) collective-permute-start(f32[128,128]{1,0:T(8,128)S(1)} %get-tuple-element.47), channel_id=1, source_target_pairs={{0,4},{1,3},{2,6},{3,1},{4,0},{5,7},{6,2},{7,5},{8,12},{9,11},{10,... | collective-permute-start | bytes 196616 | tf_op jit(solution)/shard_map/ppermute | solution.py:291
  35.1 4.6 %collective-permute-start.17 = (f32[128,128]{1,0:T(8,128)S(1)}, f32[128,128]{1,0:T(8,128)S(1)}, u32[]{:S(2)}, u32[]{:S(2)}) collective-permute-start(f32[128,128]{1,0:T(8,128)S(1)} %get-tuple-element.53), channel_id=1, source_target_pairs={{0,4},{1,3},{2,6},{3,1},{4,0},{5,7},{6,2},{7,5},{8,12},{9,11},{10,... | collective-permute-start | bytes 196616 | tf_op jit(solution)/shard_map/ppermute | solution.py:291
  35.7 4.3 %collective-permute-start.18 = (f32[128,128]{1,0:T(8,128)S(1)}, f32[128,128]{1,0:T(8,128)S(1)}, u32[]{:S(2)}, u32[]{:S(2)}) collective-permute-start(f32[128,128]{1,0:T(8,128)S(1)} %get-tuple-element.54), channel_id=1, source_target_pairs={{0,2},{1,5},{2,0},{3,7},{4,6},{5,1},{6,4},{7,3},{8,10},{9,13},{10,... | collective-permute-start | bytes 196616 | tf_op jit(solution)/shard_map/ppermute | solution.py:291
  40.7 1.6 %collective-permute-start.19 = (f32[56,8,128]{2,1,0:T(8,128)S(1)}, f32[56,8,128]{2,1,0:T(8,128)S(1)}, u32[]{:S(2)}, u32[]{:S(2)}) collective-permute-start(f32[56,8,128]{2,1,0:T(8,128)S(1)} %bitcast.22), channel_id=1, source_target_pairs={{0,1},{1,0},{2,3},{3,2},{4,5},{5,4},{6,7},{7,6},{8,9},{9,8},{10,11... | collective-permute-start | bytes 688136 | tf_op jit(solution)/shard_map/ppermute | solution.py:243

commit v6 on v5

--- a/solution.py
+++ b/solution.py
@@ -245,7 +245,9 @@
     def plane(array, at):
         return lax.dynamic_index_in_dim(array, at, 1, keepdims=False)
 
-    here, there = plane(field, core), plane(field, 1 - core)
+    there = plane(field, 1 - core)
+    field, there = lax.optimization_barrier((field, there))
+    here = plane(field, core)
     here_beside = across(there)
     send_rows, pick, mode_ids, coef, other, here_beside = lax.optimization_barrier(
         (send_rows, pick, mode_ids, coef, here, here_beside)

time: 43.2 us -> 43.1 us (level)
    squeeze x2 -> x3, local copies, waits for them, and re-layouts: 1.12 us -> 0.04 us  [plane(): return lax.dynamic_index_in_dim(array, at, 1, keepdims=False)]
    unnamed x10 -> x12, local copies, waits for them, and re-layouts: 0.02 us -> 1.01 us
where the time goes in v6:
time: 43.1 us; the launch traced here: 43 us
  starting transfers between devices  19.2 us (45%)
  waiting for transfers between devices  11.7 us (27%)
  Pallas kernels  7.11 us (16%)
  other arithmetic  2.02 us (5%)
  local copies, waits for them, and re-layouts  1.54 us (4%)
  between operations  0.91 us (2%)
  matrix products  0.59 us (1%)
    ppermute x9, starting transfers between devices, send(): lax.ppermute(sent[n - 1], 'chaos', to_chip[n])  10.7 us
    ppermute x9, waiting for transfers between devices, send(): lax.ppermute(sent[n - 1], 'chaos', to_chip[n])  8.37 us
    ppermute x4, starting transfers between devices, exchange(): halos = [lax.ppermute(center, AXES, to_slab) for center in centers]  6.92 us
    pallas_call x4, Pallas kernels, product(): pl.pallas_call(functools.partial(product_kernel, b, cap, orders[b]), out_...  3.23 us
    ppermute x4, waiting for transfers between devices, exchange(): halos = [lax.ppermute(center, AXES, to_slab) for center in centers]  2.61 us
    ppermute x7, starting transfers between devices, across(): return lax.ppermute(array, 'chaos', [(i, i ^ 1) for i in range(owners)])  1.58 us
    pallas_call x2, Pallas kernels, write(): pl.pallas_call(write_kernel, out_shape=[jax.ShapeDtypeStruct((terms, 2, g...  1.57 us
    convert_element_type x1, other arithmetic, body(): jnp.where(taken, part[:, :, None], 0.0).astype(jnp.bfloat16)  1.47 us
  transfers between devices with their start and end apart: 20, of which 9 were waited for; matrix products, arithmetic and copies ran while one was open for 7% of the time, Pallas kernels for 13%

profile of v6, /device:TPU:0, one launch (start us, length us, event | category | flops | bytes accessed | tf_op | source)
XLA Modules:
  0.0 43.0 jit_solution(5744867032888795714)
XLA Ops:
  0.6 0.0 copy-start
  0.7 1.0 %copy-done = f32[56,2,8,128]{3,2,1,0:T(8,128)S(1)} copy-done((f32[56,2,8,128]{3,2,1,0:T(8,128)S(1)}, f32[56,2,8,128]{3,2,1,0:T(8,128)}, u32[]{:S(2)}) %copy-start) | copy-done | bytes 458776
  1.7 0.5 %collective-permute-start = (f32[56,8,128]{2,1,0:T(8,128)S(1)}, f32[56,8,128]{2,1,0:T(8,128)S(1)}, u32[]{:S(2)}, u32[]{:S(2)}) collective-permute-start(f32[56,8,128]{2,1,0:T(8,128)S(1)} %dynamic-slice_bitcast_fusion.1.other_own), channel_id=1, source_target_pairs={{0,1},{1,0},{2,3},{3,2},{4,5},{5,4},{6,7},{7,6},{8,9},{9,8},{10,11... | collective-permute-start | bytes 688136 | tf_op jit(solution)/shard_map/ppermute | solution.py:243
  2.2 2.6 %collective-permute-start.2 = (f32[56,8,128]{2,1,0:T(8,128)S(1)}, f32[56,8,128]{2,1,0:T(8,128)S(1)}, u32[]{:S(2)}, u32[]{:S(2)}) collective-permute-start(f32[56,8,128]{2,1,0:T(8,128)S(1)} %dynamic-slice_bitcast_fusion.center_own), channel_id=1, source_target_pairs={{0,2},{1,8},{2,0},{3,10},{4,6},{5,12},{6,4},{7,14},{8,1},{9,16},{1... | collective-permute-start | bytes 688136 | tf_op jit(solution)/shard_map/ppermute | solution.py:296
  4.8 0.0 collective-permute-done.center_beside
  4.8 0.3 collective-permute-start.4
  5.1 0.3 from_own.2.rows
  5.4 0.3 collective-permute-start.1
  5.7 1.3 %collective-permute-start.3 = (f32[56,8,128]{2,1,0:T(8,128)S(1)}, f32[56,8,128]{2,1,0:T(8,128)S(1)}, u32[]{:S(2)}, u32[]{:S(2)}) collective-permute-start(f32[56,8,128]{2,1,0:T(8,128)S(1)} %collective-permute-done.center_beside), channel_id=1, source_target_pairs={{0,2},{1,8},{2,0},{3,10},{4,6},{5,12},{6,4},{7,14},{8,1},{9,16},{1... | collective-permute-start | bytes 688136 | tf_op jit(solution)/shard_map/ppermute | solution.py:296
  7.0 0.1 fusion.9
  7.0 0.1 copy.13
  7.1 0.1 copy.14
  7.2 0.1 copy.15
  7.4 0.1 copy.12
  7.4 1.5 %select_convert_fusion.1 = (bf16[56,41,64]{2,1,0:T(8,128)(2,1)S(1)}, bf16[56,41,64]{2,1,0:T(8,128)(2,1)S(1)}) fusion(bf16[56,41]{1,0:T(8,128)(2,1)S(1)} %copy.14, s32[56,41]{1,0:T(8,128)S(1)} %copy.13, bf16[56,41]{1,0:T(8,128)(2,1)S(1)} %copy.15), kind=kLoop, calls=%fused_computation.1 | loop fusion | flops 440832 | bytes 606144 | tf_op jit(solution)/shard_map/convert_element_type | solution.py:281
  8.9 0.6 %convolution_bitcast_fusion = f32[21,56,128]{2,0,1:T(8,128)S(1)} fusion(bf16[56,41,64]{2,1,0:T(8,128)(2,1)S(1)} %get-tuple-element.65, bf16[56,41,64]{2,1,0:T(8,128)(2,1)S(1)} %get-tuple-element.64, s32[56,41]{1,0:T(8,128)S(1)} %copy.12), kind=kOutput, calls=%fused_computation.3 | convolution fusion | flops 13567064 | bytes 1199072 | tf_op jit(solution)/shard_map/isp,isk->kip/dot_general | solution.py:284
  9.5 0.1 copy.16
  9.6 0.2 fusion.4
  9.9 0.2 fusion.17
  10.1 0.3 collective-permute-start.8
  10.4 0.3 from_own.3.rows
  10.7 0.0 collective-permute-done.1.other_beside
  10.7 0.3 local.2
  11.0 0.0 copy-start.2
  11.0 0.2 images_1_1.2
  11.2 0.5 %collective-permute-done.3.halo = f32[56,8,128]{2,1,0:T(8,128)S(1)} collective-permute-done((f32[56,8,128]{2,1,0:T(8,128)S(1)}, f32[56,8,128]{2,1,0:T(8,128)S(1)}, u32[]{:S(2)}, u32[]{:S(2)}) %collective-permute-start.3) | collective-permute-done | bytes 229408 | tf_op jit(solution)/shard_map/ppermute | solution.py:296
  11.7 0.2 images_0_1.2
  11.9 2.6 %collective-permute-start.5 = (f32[256,128]{1,0:T(8,128)S(1)}, f32[256,128]{1,0:T(8,128)S(1)}, u32[]{:S(2)}, u32[]{:S(2)}) collective-permute-start(f32[256,128]{1,0:T(8,128)S(1)} %get-tuple-element.44.rest_1_), channel_id=1, source_target_pairs={{0,6},{1,7},{2,4},{3,5},{4,2},{5,3},{6,0},{7,1},{8,14},{9,15},{10,... | collective-permute-start | bytes 393224 | tf_op jit(solution)/shard_map/ppermute | solution.py:293
  14.5 0.5 %collective-permute-start.6 = (f32[256,128]{1,0:T(8,128)S(1)}, f32[256,128]{1,0:T(8,128)S(1)}, u32[]{:S(2)}, u32[]{:S(2)}) collective-permute-start(f32[256,128]{1,0:T(8,128)S(1)} %get-tuple-element.45), channel_id=1, source_target_pairs={{0,4},{1,3},{2,6},{3,1},{4,0},{5,7},{6,2},{7,5},{8,12},{9,11},{10,... | collective-permute-start | bytes 393224 | tf_op jit(solution)/shard_map/ppermute | solution.py:293
  15.0 0.4 %collective-permute-start.7 = (f32[256,128]{1,0:T(8,128)S(1)}, f32[256,128]{1,0:T(8,128)S(1)}, u32[]{:S(2)}, u32[]{:S(2)}) collective-permute-start(f32[256,128]{1,0:T(8,128)S(1)} %get-tuple-element.46), channel_id=1, source_target_pairs={{0,2},{1,5},{2,0},{3,7},{4,6},{5,1},{6,4},{7,3},{8,10},{9,13},{10,... | collective-permute-start | bytes 393224 | tf_op jit(solution)/shard_map/ppermute | solution.py:293
  15.4 0.1 images_0_0.2.rest_3_
  15.6 3.6 %collective-permute-done.5.rest_0_ = f32[256,128]{1,0:T(8,128)S(1)} collective-permute-done((f32[256,128]{1,0:T(8,128)S(1)}, f32[256,128]{1,0:T(8,128)S(1)}, u32[]{:S(2)}, u32[]{:S(2)}) %collective-permute-start.5) | collective-permute-done | bytes 131104 | tf_op jit(solution)/shard_map/ppermute | solution.py:293
  19.2 1.9 %collective-permute-done.6.rest_1_ = f32[256,128]{1,0:T(8,128)S(1)} collective-permute-done((f32[256,128]{1,0:T(8,128)S(1)}, f32[256,128]{1,0:T(8,128)S(1)}, u32[]{:S(2)}, u32[]{:S(2)}) %collective-permute-start.6) | collective-permute-done | bytes 131104 | tf_op jit(solution)/shard_map/ppermute | solution.py:293
  21.1 0.3 collective-permute-done.7.rest_2_
  21.3 0.8 %product_0.2 = f32[448,128]{1,0:T(8,128)S(1)} custom-call(bf16[1176,128]{1,0:T(8,128)(2,1)S(1)} %get-tuple-element.60.weights, f32[21,8,128]{2,1,0:T(8,128)S(1)} %dynamic-slice_bitcast_fusion.2.modes, f32[256,128]{1,0:T(8,128)S(1)} %collective-permute-done.5.rest_0_, f32[256,128]{1,0:T(8,128)S(1)} %collective-permute-done.6.rest_1_, ...), custom_call_target="tpu_custom_call" | custom-call | flops 616562688 | bytes 1048576 | tf_op jit(solution)/shard_map/product_0/pallas_call | solution.py:160
  22.1 0.1 collective-permute-start.10
  22.2 1.6 %collective-permute-start.11 = (f32[56,8,128]{2,1,0:T(8,128)S(1)}, f32[56,8,128]{2,1,0:T(8,128)S(1)}, u32[]{:S(2)}, u32[]{:S(2)}) collective-permute-start(f32[56,8,128]{2,1,0:T(8,128)S(1)} %bitcast.14), channel_id=1, source_target_pairs={{0,2},{1,8},{2,0},{3,10},{4,6},{5,12},{6,4},{7,14},{8,1},{9,16},{1... | collective-permute-start | bytes 688136 | tf_op jit(solution)/shard_map/ppermute | solution.py:296
  23.8 0.8 %product_1.2 = f32[448,128]{1,0:T(8,128)S(1)} custom-call(f32[1176,128]{1,0:T(8,128)S(1)} %collective-permute-done.8.weights, f32[21,8,128]{2,1,0:T(8,128)S(1)} %dynamic-slice_bitcast_fusion.2.modes, f32[256,128]{1,0:T(8,128)S(1)} %collective-permute-done.5.rest_0_, f32[256,128]{1,0:T(8,128)S(1)} %collective-permute-done.6.rest_1_, ...), custom_call_target="tpu_custom_call" | custom-call | flops 616562688 | bytes 1048576 | tf_op jit(solution)/shard_map/product_1/pallas_call | solution.py:160
  24.6 0.1 collective-permute-start.9
  24.7 1.5 %collective-permute-start.15 = (f32[56,8,128]{2,1,0:T(8,128)S(1)}, f32[56,8,128]{2,1,0:T(8,128)S(1)}, u32[]{:S(2)}, u32[]{:S(2)}) collective-permute-start(f32[56,8,128]{2,1,0:T(8,128)S(1)} %bitcast.20), channel_id=1, source_target_pairs={{0,2},{1,8},{2,0},{3,10},{4,6},{5,12},{6,4},{7,14},{8,1},{9,16},{1... | collective-permute-start | bytes 688136 | tf_op jit(solution)/shard_map/ppermute | solution.py:296
  26.2 0.0 collective-permute-done.10.other_beside
  26.2 2.1 %collective-permute-done.11.rest_0_.halo = f32[56,8,128]{2,1,0:T(8,128)S(1)} collective-permute-done((f32[56,8,128]{2,1,0:T(8,128)S(1)}, f32[56,8,128]{2,1,0:T(8,128)S(1)}, u32[]{:S(2)}, u32[]{:S(2)}) %collective-permute-start.11) | collective-permute-done | bytes 229408 | tf_op jit(solution)/shard_map/ppermute | solution.py:296
  28.3 0.3 local.3
  28.6 0.2 images_1_1.3
  28.8 1.6 %collective-permute-start.12 = (f32[128,128]{1,0:T(8,128)S(1)}, f32[128,128]{1,0:T(8,128)S(1)}, u32[]{:S(2)}, u32[]{:S(2)}) collective-permute-start(f32[128,128]{1,0:T(8,128)S(1)} %get-tuple-element.50), channel_id=1, source_target_pairs={{0,2},{1,5},{2,0},{3,7},{4,6},{5,1},{6,4},{7,3},{8,10},{9,13},{10,... | collective-permute-start | bytes 196616 | tf_op jit(solution)/shard_map/ppermute | solution.py:293
  30.4 1.4 %collective-permute-start.14 = (f32[128,128]{1,0:T(8,128)S(1)}, f32[128,128]{1,0:T(8,128)S(1)}, u32[]{:S(2)}, u32[]{:S(2)}) collective-permute-start(f32[128,128]{1,0:T(8,128)S(1)} %get-tuple-element.52.rest_0_), channel_id=1, source_target_pairs={{0,6},{1,7},{2,4},{3,5},{4,2},{5,3},{6,0},{7,1},{8,14},{9,15},{10,... | collective-permute-start | bytes 196616 | tf_op jit(solution)/shard_map/ppermute | solution.py:293
  31.8 0.0 collective-permute-done.15.halo
  31.8 0.2 images_0_1.3
  32.0 1.6 %collective-permute-start.16 = (f32[128,128]{1,0:T(8,128)S(1)}, f32[128,128]{1,0:T(8,128)S(1)}, u32[]{:S(2)}, u32[]{:S(2)}) collective-permute-start(f32[128,128]{1,0:T(8,128)S(1)} %get-tuple-element.56.rest_0_), channel_id=1, source_target_pairs={{0,6},{1,7},{2,4},{3,5},{4,2},{5,3},{6,0},{7,1},{8,14},{9,15},{10,... | collective-permute-start | bytes 196616 | tf_op jit(solution)/shard_map/ppermute | solution.py:293
  33.5 1.5 %collective-permute-start.13 = (f32[128,128]{1,0:T(8,128)S(1)}, f32[128,128]{1,0:T(8,128)S(1)}, u32[]{:S(2)}, u32[]{:S(2)}) collective-permute-start(f32[128,128]{1,0:T(8,128)S(1)} %get-tuple-element.51), channel_id=1, source_target_pairs={{0,4},{1,3},{2,6},{3,1},{4,0},{5,7},{6,2},{7,5},{8,12},{9,11},{10,... | collective-permute-start | bytes 196616 | tf_op jit(solution)/shard_map/ppermute | solution.py:293
  35.0 0.6 %collective-permute-start.17 = (f32[128,128]{1,0:T(8,128)S(1)}, f32[128,128]{1,0:T(8,128)S(1)}, u32[]{:S(2)}, u32[]{:S(2)}) collective-permute-start(f32[128,128]{1,0:T(8,128)S(1)} %get-tuple-element.57), channel_id=1, source_target_pairs={{0,4},{1,3},{2,6},{3,1},{4,0},{5,7},{6,2},{7,5},{8,12},{9,11},{10,... | collective-permute-start | bytes 196616 | tf_op jit(solution)/shard_map/ppermute | solution.py:293
  35.6 0.5 %collective-permute-start.18 = (f32[128,128]{1,0:T(8,128)S(1)}, f32[128,128]{1,0:T(8,128)S(1)}, u32[]{:S(2)}, u32[]{:S(2)}) collective-permute-start(f32[128,128]{1,0:T(8,128)S(1)} %get-tuple-element.58), channel_id=1, source_target_pairs={{0,2},{1,5},{2,0},{3,7},{4,6},{5,1},{6,4},{7,3},{8,10},{9,13},{10,... | collective-permute-start | bytes 196616 | tf_op jit(solution)/shard_map/ppermute | solution.py:293
  36.1 0.1 images_0_0.3.rest_5_
  36.2 0.1 images_1_0.1.rest_3_
  36.4 0.8 %write.2 = (f32[56,2,8,128]{3,2,1,0:T(8,128)}, f32[8,128]{1,0:T(8,128)S(1)}) custom-call(f32[56,8,128]{2,1,0:T(8,128)S(1)} %bitcast.17, f32[56,8,128]{2,1,0:T(8,128)S(1)} %collective-permute-done.9.there.other_own), custom_call_target="tpu_custom_call" | custom-call | tf_op jit(solution)/shard_map/write/pallas_call | solution.py:189
  37.2 1.7 %collective-permute-done.13.rest_1_ = f32[128,128]{1,0:T(8,128)S(1)} collective-permute-done((f32[128,128]{1,0:T(8,128)S(1)}, f32[128,128]{1,0:T(8,128)S(1)}, u32[]{:S(2)}, u32[]{:S(2)}) %collective-permute-start.13) | collective-permute-done | bytes 65568 | tf_op jit(solution)/shard_map/ppermute | solution.py:293
  38.8 0.0 collective-permute-done.14.rest_2_
  38.9 0.8 %collective-permute-done.17.rest_3_ = f32[128,128]{1,0:T(8,128)S(1)} collective-permute-done((f32[128,128]{1,0:T(8,128)S(1)}, f32[128,128]{1,0:T(8,128)S(1)}, u32[]{:S(2)}, u32[]{:S(2)}) %collective-permute-start.17) | collective-permute-done | bytes 65568 | tf_op jit(solution)/shard_map/ppermute | solution.py:293
  39.6 0.2 collective-permute-done.18.rest_4_
  39.8 0.8 %product_1.3 = f32[448,128]{1,0:T(8,128)S(1)} custom-call(f32[1176,128]{1,0:T(8,128)S(1)} %collective-permute-done.8.weights, f32[21,8,128]{2,1,0:T(8,128)S(1)} %dynamic-slice_bitcast_fusion.2.modes, bf16[512,128]{1,0:T(8,128)(2,1)S(1)} %get-tuple-element.53.rest_0_, bf16[512,128]{1,0:T(8,128)(2,1)S(1)} %get-tuple-element.54.rest_1_, ...), custom_call_target="tpu_custom_call" | custom-call | flops 616562688 | bytes 1048576 | tf_op jit(solution)/shard_map/product_1/pallas_call | solution.py:160
  40.7 0.1 collective-permute-start.19
  40.7 0.8 %product_0.3 = f32[448,128]{1,0:T(8,128)S(1)} custom-call(bf16[1176,128]{1,0:T(8,128)(2,1)S(1)} %get-tuple-element.60.weights, f32[21,8,128]{2,1,0:T(8,128)S(1)} %dynamic-slice_bitcast_fusion.2.modes, bf16[512,128]{1,0:T(8,128)(2,1)S(1)} %get-tuple-element.53.rest_0_, bf16[512,128]{1,0:T(8,128)(2,1)S(1)} %get-tuple-element.54.rest_1_, ...), custom_call_target="tpu_custom_call" | custom-call | flops 616562688 | bytes 1048576 | tf_op jit(solution)/shard_map/product_0/pallas_call | solution.py:160
  41.6 0.7 %collective-permute-done.19.there = f32[56,8,128]{2,1,0:T(8,128)S(1)} collective-permute-done((f32[56,8,128]{2,1,0:T(8,128)S(1)}, f32[56,8,128]{2,1,0:T(8,128)S(1)}, u32[]{:S(2)}, u32[]{:S(2)}) %collective-permute-start.19) | collective-permute-done | bytes 229408 | tf_op jit(solution)/shard_map/ppermute | solution.py:243
  42.2 0.8 %write.3 = f32[56,2,8,128]{3,2,1,0:T(8,128)} custom-call(f32[56,8,128]{2,1,0:T(8,128)S(1)} %bitcast.18, f32[56,8,128]{2,1,0:T(8,128)S(1)} %collective-permute-done.19.there), custom_call_target="tpu_custom_call" | custom-call | tf_op jit(solution)/shard_map/write/pallas_call | solution.py:189
  (21 shorter events, 0.1 us)
Async XLA Ops:
  0.6 1.0 %copy-start = (f32[56,2,8,128]{3,2,1,0:T(8,128)S(1)}, f32[56,2,8,128]{3,2,1,0:T(8,128)}, u32[]{:S(2)}) copy-start(f32[56,2,8,128]{3,2,1,0:T(8,128)} %param.6) | copy-start | bytes 1376260
  0.6 4.2 %copy-start.1 = (s32[1,64]{1,0:T(1,128)S(1)}, s32[1,64]{1,0:T(1,128)}, u32[]{:S(2)}) copy-start(s32[1,64]{1,0:T(1,128)} %listed) | copy-start | bytes 772
  1.7 3.1 %collective-permute-start = (f32[56,8,128]{2,1,0:T(8,128)S(1)}, f32[56,8,128]{2,1,0:T(8,128)S(1)}, u32[]{:S(2)}, u32[]{:S(2)}) collective-permute-start(f32[56,8,128]{2,1,0:T(8,128)S(1)} %dynamic-slice_bitcast_fusion.1.other_own), channel_id=1, source_target_pairs={{0,1},{1,0},{2,3},{3,2},{4,5},{5,4},{6,7},{7,6},{8,9},{9,8},{10,11... | collective-permute-start | bytes 688136 | tf_op jit(solution)/shard_map/ppermute | solution.py:243
  2.2 8.5 %collective-permute-start.2 = (f32[56,8,128]{2,1,0:T(8,128)S(1)}, f32[56,8,128]{2,1,0:T(8,128)S(1)}, u32[]{:S(2)}, u32[]{:S(2)}) collective-permute-start(f32[56,8,128]{2,1,0:T(8,128)S(1)} %dynamic-slice_bitcast_fusion.center_own), channel_id=1, source_target_pairs={{0,2},{1,8},{2,0},{3,10},{4,6},{5,12},{6,4},{7,14},{8,1},{9,16},{1... | collective-permute-start | bytes 688136 | tf_op jit(solution)/shard_map/ppermute | solution.py:296
  4.8 2.2 %copy-start.3 = (s32[56,41]{0,1:T(8,128)S(1)}, s32[56,41]{0,1:T(8,128)}, u32[]{:S(2)}) copy-start(s32[56,41]{0,1:T(8,128)} %param.9) | copy-start | bytes 27556
  4.8 2.3 %copy-start.4 = (f32[56,41]{0,1:T(8,128)S(1)}, f32[56,41]{0,1:T(8,128)}, u32[]{:S(2)}) copy-start(f32[56,41]{0,1:T(8,128)} %param.11) | copy-start | bytes 27556
  4.8 2.5 %copy-start.5 = (s32[56,41]{0,1:T(8,128)S(1)}, s32[56,41]{0,1:T(8,128)}, u32[]{:S(2)}) copy-start(s32[56,41]{0,1:T(8,128)} %param.10) | copy-start | bytes 27556
  4.8 5.6 %collective-permute-start.4 = (s32[1,64]{1,0:T(1,128)S(1)}, s32[1,64]{1,0:T(1,128)S(1)}, u32[]{:S(2)}, u32[]{:S(2)}) collective-permute-start(s32[1,64]{1,0:T(1,128)S(1)} %copy-done.1), channel_id=1, source_target_pairs={{0,1},{1,0},{2,3},{3,2},{4,5},{5,4},{6,7},{7,6},{8,9},{9,8},{10,11... | collective-permute-start | bytes 776 | tf_op jit(solution)/shard_map/ppermute | solution.py:243
  5.4 5.3 %collective-permute-start.1 = (f32[56,8,128]{2,1,0:T(8,128)S(1)}, f32[56,8,128]{2,1,0:T(8,128)S(1)}, u32[]{:S(2)}, u32[]{:S(2)}) collective-permute-start(f32[56,8,128]{2,1,0:T(8,128)S(1)} %dynamic-slice_bitcast_fusion.center_own), channel_id=1, source_target_pairs={{0,1},{1,0},{2,3},{3,2},{4,5},{5,4},{6,7},{7,6},{8,9},{9,8},{10,11... | collective-permute-start | bytes 688136 | tf_op jit(solution)/shard_map/ppermute | solution.py:243
  5.7 6.0 %collective-permute-start.3 = (f32[56,8,128]{2,1,0:T(8,128)S(1)}, f32[56,8,128]{2,1,0:T(8,128)S(1)}, u32[]{:S(2)}, u32[]{:S(2)}) collective-permute-start(f32[56,8,128]{2,1,0:T(8,128)S(1)} %collective-permute-done.center_beside), channel_id=1, source_target_pairs={{0,2},{1,8},{2,0},{3,10},{4,6},{5,12},{6,4},{7,14},{8,1},{9,16},{1... | collective-permute-start | bytes 688136 | tf_op jit(solution)/shard_map/ppermute | solution.py:296
  10.1 13.7 %collective-permute-start.8 = (f32[1176,128]{1,0:T(8,128)S(1)}, f32[1176,128]{1,0:T(8,128)S(1)}, u32[]{:S(2)}, u32[]{:S(2)}) collective-permute-start(f32[1176,128]{1,0:T(8,128)S(1)} %get-tuple-element.61), channel_id=1, source_target_pairs={{0,1},{1,0},{2,3},{3,2},{4,5},{5,4},{6,7},{7,6},{8,9},{9,8},{10,11... | collective-permute-start | bytes 1806344 | tf_op jit(solution)/shard_map/ppermute | solution.py:243
  11.0 4.4 %copy-start.2 = (f32[21,2,8,128]{3,2,1,0:T(8,128)S(1)}, f32[21,2,8,128]{3,2,1,0:T(8,128)}, u32[]{:S(2)}) copy-start(f32[21,2,8,128]{3,2,1,0:T(8,128)} %param.7) | copy-start | bytes 516100
  11.9 7.3 %collective-permute-start.5 = (f32[256,128]{1,0:T(8,128)S(1)}, f32[256,128]{1,0:T(8,128)S(1)}, u32[]{:S(2)}, u32[]{:S(2)}) collective-permute-start(f32[256,128]{1,0:T(8,128)S(1)} %get-tuple-element.44.rest_1_), channel_id=1, source_target_pairs={{0,6},{1,7},{2,4},{3,5},{4,2},{5,3},{6,0},{7,1},{8,14},{9,15},{10,... | collective-permute-start | bytes 393224 | tf_op jit(solution)/shard_map/ppermute | solution.py:293
  14.5 6.6 %collective-permute-start.6 = (f32[256,128]{1,0:T(8,128)S(1)}, f32[256,128]{1,0:T(8,128)S(1)}, u32[]{:S(2)}, u32[]{:S(2)}) collective-permute-start(f32[256,128]{1,0:T(8,128)S(1)} %get-tuple-element.45), channel_id=1, source_target_pairs={{0,4},{1,3},{2,6},{3,1},{4,0},{5,7},{6,2},{7,5},{8,12},{9,11},{10,... | collective-permute-start | bytes 393224 | tf_op jit(solution)/shard_map/ppermute | solution.py:293
  15.0 6.3 %collective-permute-start.7 = (f32[256,128]{1,0:T(8,128)S(1)}, f32[256,128]{1,0:T(8,128)S(1)}, u32[]{:S(2)}, u32[]{:S(2)}) collective-permute-start(f32[256,128]{1,0:T(8,128)S(1)} %get-tuple-element.46), channel_id=1, source_target_pairs={{0,2},{1,5},{2,0},{3,7},{4,6},{5,1},{6,4},{7,3},{8,10},{9,13},{10,... | collective-permute-start | bytes 393224 | tf_op jit(solution)/shard_map/ppermute | solution.py:293
  22.1 4.0 %collective-permute-start.10 = (f32[56,8,128]{2,1,0:T(8,128)S(1)}, f32[56,8,128]{2,1,0:T(8,128)S(1)}, u32[]{:S(2)}, u32[]{:S(2)}) collective-permute-start(f32[56,8,128]{2,1,0:T(8,128)S(1)} %bitcast.13), channel_id=1, source_target_pairs={{0,1},{1,0},{2,3},{3,2},{4,5},{5,4},{6,7},{7,6},{8,9},{9,8},{10,11... | collective-permute-start | bytes 688136 | tf_op jit(solution)/shard_map/ppermute | solution.py:243
  22.2 6.1 %collective-permute-start.11 = (f32[56,8,128]{2,1,0:T(8,128)S(1)}, f32[56,8,128]{2,1,0:T(8,128)S(1)}, u32[]{:S(2)}, u32[]{:S(2)}) collective-permute-start(f32[56,8,128]{2,1,0:T(8,128)S(1)} %bitcast.14), channel_id=1, source_target_pairs={{0,2},{1,8},{2,0},{3,10},{4,6},{5,12},{6,4},{7,14},{8,1},{9,16},{1... | collective-permute-start | bytes 688136 | tf_op jit(solution)/shard_map/ppermute | solution.py:296
  24.6 3.7 %collective-permute-start.9 = (f32[56,8,128]{2,1,0:T(8,128)S(1)}, f32[56,8,128]{2,1,0:T(8,128)S(1)}, u32[]{:S(2)}, u32[]{:S(2)}) collective-permute-start(f32[56,8,128]{2,1,0:T(8,128)S(1)} %bitcast.19), channel_id=1, source_target_pairs={{0,1},{1,0},{2,3},{3,2},{4,5},{5,4},{6,7},{7,6},{8,9},{9,8},{10,11... | collective-permute-start | bytes 688136 | tf_op jit(solution)/shard_map/ppermute | solution.py:243
  24.7 7.1 %collective-permute-start.15 = (f32[56,8,128]{2,1,0:T(8,128)S(1)}, f32[56,8,128]{2,1,0:T(8,128)S(1)}, u32[]{:S(2)}, u32[]{:S(2)}) collective-permute-start(f32[56,8,128]{2,1,0:T(8,128)S(1)} %bitcast.20), channel_id=1, source_target_pairs={{0,2},{1,8},{2,0},{3,10},{4,6},{5,12},{6,4},{7,14},{8,1},{9,16},{1... | collective-permute-start | bytes 688136 | tf_op jit(solution)/shard_map/ppermute | solution.py:296
  28.8 6.8 %collective-permute-start.12 = (f32[128,128]{1,0:T(8,128)S(1)}, f32[128,128]{1,0:T(8,128)S(1)}, u32[]{:S(2)}, u32[]{:S(2)}) collective-permute-start(f32[128,128]{1,0:T(8,128)S(1)} %get-tuple-element.50), channel_id=1, source_target_pairs={{0,2},{1,5},{2,0},{3,7},{4,6},{5,1},{6,4},{7,3},{8,10},{9,13},{10,... | collective-permute-start | bytes 196616 | tf_op jit(solution)/shard_map/ppermute | solution.py:293
  30.4 8.5 %collective-permute-start.14 = (f32[128,128]{1,0:T(8,128)S(1)}, f32[128,128]{1,0:T(8,128)S(1)}, u32[]{:S(2)}, u32[]{:S(2)}) collective-permute-start(f32[128,128]{1,0:T(8,128)S(1)} %get-tuple-element.52.rest_0_), channel_id=1, source_target_pairs={{0,6},{1,7},{2,4},{3,5},{4,2},{5,3},{6,0},{7,1},{8,14},{9,15},{10,... | collective-permute-start | bytes 196616 | tf_op jit(solution)/shard_map/ppermute | solution.py:293
  32.0 6.9 %collective-permute-start.16 = (f32[128,128]{1,0:T(8,128)S(1)}, f32[128,128]{1,0:T(8,128)S(1)}, u32[]{:S(2)}, u32[]{:S(2)}) collective-permute-start(f32[128,128]{1,0:T(8,128)S(1)} %get-tuple-element.56.rest_0_), channel_id=1, source_target_pairs={{0,6},{1,7},{2,4},{3,5},{4,2},{5,3},{6,0},{7,1},{8,14},{9,15},{10,... | collective-permute-start | bytes 196616 | tf_op jit(solution)/shard_map/ppermute | solution.py:293
  33.5 5.3 %collective-permute-start.13 = (f32[128,128]{1,0:T(8,128)S(1)}, f32[128,128]{1,0:T(8,128)S(1)}, u32[]{:S(2)}, u32[]{:S(2)}) collective-permute-start(f32[128,128]{1,0:T(8,128)S(1)} %get-tuple-element.51), channel_id=1, source_target_pairs={{0,4},{1,3},{2,6},{3,1},{4,0},{5,7},{6,2},{7,5},{8,12},{9,11},{10,... | collective-permute-start | bytes 196616 | tf_op jit(solution)/shard_map/ppermute | solution.py:293
  35.0 4.6 %collective-permute-start.17 = (f32[128,128]{1,0:T(8,128)S(1)}, f32[128,128]{1,0:T(8,128)S(1)}, u32[]{:S(2)}, u32[]{:S(2)}) collective-permute-start(f32[128,128]{1,0:T(8,128)S(1)} %get-tuple-element.57), channel_id=1, source_target_pairs={{0,4},{1,3},{2,6},{3,1},{4,0},{5,7},{6,2},{7,5},{8,12},{9,11},{10,... | collective-permute-start | bytes 196616 | tf_op jit(solution)/shard_map/ppermute | solution.py:293
  35.6 4.3 %collective-permute-start.18 = (f32[128,128]{1,0:T(8,128)S(1)}, f32[128,128]{1,0:T(8,128)S(1)}, u32[]{:S(2)}, u32[]{:S(2)}) collective-permute-start(f32[128,128]{1,0:T(8,128)S(1)} %get-tuple-element.58), channel_id=1, source_target_pairs={{0,2},{1,5},{2,0},{3,7},{4,6},{5,1},{6,4},{7,3},{8,10},{9,13},{10,... | collective-permute-start | bytes 196616 | tf_op jit(solution)/shard_map/ppermute | solution.py:293
  40.7 1.6 %collective-permute-start.19 = (f32[56,8,128]{2,1,0:T(8,128)S(1)}, f32[56,8,128]{2,1,0:T(8,128)S(1)}, u32[]{:S(2)}, u32[]{:S(2)}) collective-permute-start(f32[56,8,128]{2,1,0:T(8,128)S(1)} %bitcast.22), channel_id=1, source_target_pairs={{0,1},{1,0},{2,3},{3,2},{4,5},{5,4},{6,7},{7,6},{8,9},{9,8},{10,11... | collective-permute-start | bytes 688136 | tf_op jit(solution)/shard_map/ppermute | solution.py:243

commit v7 on v5

--- a/solution.py
+++ b/solution.py
@@ -28,8 +28,9 @@
     return pairs
 
 
-def local_kernel(center_own, center_beside, other_own, other_beside, *rest):
-    gx, gy = center_own.shape[1:]
+def local_kernel(center, other, *rest):
+    out = rest[-1]
+    gx, gy = center.shape[1:]
     sub = lax.broadcasted_iota(jnp.int32, (gx, gy), 0)
     lane = lax.broadcasted_iota(jnp.int32, (gx, gy), 1)
     zero = jnp.zeros((gx, gy), jnp.float32)
@@ -41,25 +42,23 @@
         beside = beside + jnp.where(lane < gy - 1, pltpu.roll(middle, gy - 1, 1), zero)
         return 6.0 * middle - (beside + other)
 
-    for center, other, out in zip((center_own, center_beside), (other_own, other_beside), rest[-2:]):
-        for start in range(0, center.shape[0], BATCH):
-            terms = range(start, min(start + BATCH, center.shape[0]))
-            made = [laplace(center[term], other[term]) for term in terms]
-            for term, value in zip(terms, made):
-                out[term] = value
-
-
-def local(centers, others, after=()):
-    out = jax.ShapeDtypeStruct(centers[0].shape, jnp.float32)
+    for start in range(0, center.shape[0], BATCH):
+        terms = range(start, min(start + BATCH, center.shape[0]))
+        made = [laplace(center[term], other[term]) for term in terms]
+        for term, value in zip(terms, made):
+            out[term] = value
+
+
+def local(a, center, other, *after):
     return pl.pallas_call(
         local_kernel,
-        out_shape=[out, out],
-        in_specs=[VMEM] * 4 + [ANY] * len(after),
-        out_specs=[VMEM] * 2,
-        compiler_params=PARAMS,
-        cost_estimate=cost(out.size * 16),
-        name="local",
-    )(*centers, *others, *after)
+        out_shape=jax.ShapeDtypeStruct(center.shape, jnp.float32),
+        in_specs=[VMEM] * 2 + [ANY] * len(after),
+        out_specs=VMEM,
+        compiler_params=PARAMS,
+        cost_estimate=cost(center.size * 8),
+        name=f"local_{a}",
+    )(center, other, *after)
 
 
 def images_kernel(a, whole, chips, cap, rows, flag, partial, halo, *rest):
@@ -292,18 +291,21 @@
 
     def exchange(whole, centers, others):
         halos = [lax.ppermute(center, AXES, to_slab) for center in centers]
-        inputs = (cap, rows, flag, local(centers, others, halos[:1]), halos[::-1])
+        partial = [None, local(1, centers[1], others[1], halos[0])]
+        inputs = (cap, rows, flag, partial, halos[::-1])
         if whole:
+            partial[0] = local(0, centers[0], others[0], halos[0])
             begun = images(1, True, (*away, 0), *inputs)
             sent = images(0, True, away, *inputs, begun[:-1])
-            (kept,) = images(0, True, (0,), *inputs, begun[-1:], sent[-1:])
+            (kept,) = images(0, True, (0,), *inputs, begun[-1:], sent[:1])
             return send(sent, kept, emission)
         pool, after = [], ()
         for a in (1, 0):
             sent = images(a, False, away, *inputs, (), after)
-            (kept,) = images(a, False, (0,), *inputs, (), sent[-1:])
+            (kept,) = images(a, False, (0,), *inputs, (), sent[-1:] if a else sent[:1])
             pool.append(send(sent, kept, emission_early if a else emission))
             after = sent[-1:]
+            partial[0] = local(0, centers[0], others[0], sent[-1])
         return [*early(cap, orders_of(emission_early), pool[0]), *pool[1]]
 
     pool = exchange(True, (here, here_beside), (there, there_beside))

time: 43.2 us -> 43.4 us (level)
    ppermute x4, starting transfers between devices: 6.9 us -> 6.39 us  [exchange(): halos = [lax.ppermute(center, AXES, to_slab) for center in centers]]
where the time goes in v7:
time: 43.4 us; the launch traced here: 43.2 us
  starting transfers between devices  18.9 us (44%)
  waiting for transfers between devices  11.7 us (27%)
  Pallas kernels  7.24 us (17%)
  other arithmetic  2 us (5%)
  local copies, waits for them, and re-layouts  1.87 us (4%)
  between operations  0.92 us (2%)
  matrix products  0.59 us (1%)
    ppermute x9, starting transfers between devices, send(): lax.ppermute(sent[n - 1], 'chaos', to_chip[n])  10.7 us
    ppermute x9, waiting for transfers between devices, send(): lax.ppermute(sent[n - 1], 'chaos', to_chip[n])  7.94 us
    ppermute x4, starting transfers between devices, exchange(): halos = [lax.ppermute(center, AXES, to_slab) for center in centers]  6.39 us
    pallas_call x4, Pallas kernels, product(): pl.pallas_call(functools.partial(product_kernel, b, cap, orders[b]), out_...  3.23 us
    ppermute x4, waiting for transfers between devices, exchange(): halos = [lax.ppermute(center, AXES, to_slab) for center in centers]  3.06 us
    ppermute x7, starting transfers between devices, across(): return lax.ppermute(array, 'chaos', [(i, i ^ 1) for i in range(owners)])  1.84 us
    pallas_call x2, Pallas kernels, write(): pl.pallas_call(write_kernel, out_shape=[jax.ShapeDtypeStruct((terms, 2, g...  1.57 us
    convert_element_type x1, other arithmetic, body(): jnp.where(taken, part[:, :, None], 0.0).astype(jnp.bfloat16)  1.47 us
  transfers between devices with their start and end apart: 20, of which 9 were waited for; matrix products, arithmetic and copies ran while one was open for 7% of the time, Pallas kernels for 13%

profile of v7, /device:TPU:0, one launch (start us, length us, event | category | flops | bytes accessed | tf_op | source)
XLA Modules:
  0.0 43.2 jit_solution(833772500059313580)
XLA Ops:
  0.6 0.0 copy-start
  0.7 1.1 %dynamic-slice_bitcast_fusion = (f32[56,8,128]{2,1,0:T(8,128)S(1)}, f32[56,8,128]{2,1,0:T(8,128)S(1)}) fusion(f32[56,2,8,128]{3,2,1,0:T(8,128)} %param.6, s32[]{:T(128)S(6)} %select_n.66, s32[]{:T(128)S(6)} %select_n.65), kind=kLoop, calls=%fused_computation.12 | loop fusion | bytes 917512 | tf_op jit(solution)/shard_map/jit(dynamic_index_in_dim)/squeeze | solution.py:245
  1.8 0.5 %collective-permute-start = (f32[56,8,128]{2,1,0:T(8,128)S(1)}, f32[56,8,128]{2,1,0:T(8,128)S(1)}, u32[]{:S(2)}, u32[]{:S(2)}) collective-permute-start(f32[56,8,128]{2,1,0:T(8,128)S(1)} %get-tuple-element.52.other), channel_id=1, source_target_pairs={{0,1},{1,0},{2,3},{3,2},{4,5},{5,4},{6,7},{7,6},{8,9},{9,8},{10,11... | collective-permute-start | bytes 688136 | tf_op jit(solution)/shard_map/ppermute | solution.py:242
  2.3 2.6 %collective-permute-start.1 = (f32[56,8,128]{2,1,0:T(8,128)S(1)}, f32[56,8,128]{2,1,0:T(8,128)S(1)}, u32[]{:S(2)}, u32[]{:S(2)}) collective-permute-start(f32[56,8,128]{2,1,0:T(8,128)S(1)} %get-tuple-element.30.center), channel_id=1, source_target_pairs={{0,2},{1,8},{2,0},{3,10},{4,6},{5,12},{6,4},{7,14},{8,1},{9,16},{1... | collective-permute-start | bytes 688136 | tf_op jit(solution)/shard_map/ppermute | solution.py:293
  4.9 0.3 from_own.2.rows
  5.2 0.2 collective-permute-start.3
  5.4 0.2 copy-done.2
  5.6 0.1 fusion.9
  5.7 0.1 copy.13
  5.8 0.1 copy.14
  5.9 0.1 copy.15
  6.0 0.1 copy.12
  6.1 0.2 collective-permute-start.4
  6.3 1.5 %collective-permute-start.2 = (f32[56,8,128]{2,1,0:T(8,128)S(1)}, f32[56,8,128]{2,1,0:T(8,128)S(1)}, u32[]{:S(2)}, u32[]{:S(2)}) collective-permute-start(f32[56,8,128]{2,1,0:T(8,128)S(1)} %collective-permute-done.center), channel_id=1, source_target_pairs={{0,2},{1,8},{2,0},{3,10},{4,6},{5,12},{6,4},{7,14},{8,1},{9,16},{1... | collective-permute-start | bytes 688136 | tf_op jit(solution)/shard_map/ppermute | solution.py:293
  7.8 1.5 %select_convert_fusion.1 = (bf16[56,41,64]{2,1,0:T(8,128)(2,1)S(1)}, bf16[56,41,64]{2,1,0:T(8,128)(2,1)S(1)}) fusion(bf16[56,41]{1,0:T(8,128)(2,1)S(1)} %copy.14, s32[56,41]{1,0:T(8,128)S(1)} %copy.13, bf16[56,41]{1,0:T(8,128)(2,1)S(1)} %copy.15), kind=kLoop, calls=%fused_computation.1 | loop fusion | flops 440832 | bytes 606144 | tf_op jit(solution)/shard_map/convert_element_type | solution.py:278
  9.3 0.6 %convolution_bitcast_fusion = f32[21,56,128]{2,0,1:T(8,128)S(1)} fusion(bf16[56,41,64]{2,1,0:T(8,128)(2,1)S(1)} %get-tuple-element.55, bf16[56,41,64]{2,1,0:T(8,128)(2,1)S(1)} %get-tuple-element.54, s32[56,41]{1,0:T(8,128)S(1)} %copy.12), kind=kOutput, calls=%fused_computation.3 | convolution fusion | flops 13567064 | bytes 1199072 | tf_op jit(solution)/shard_map/isp,isk->kip/dot_general | solution.py:281
  9.9 0.1 copy.16
  10.0 0.2 fusion.4
  10.2 0.2 fusion.17
  10.4 0.3 collective-permute-start.8
  10.7 0.0 collective-permute-done.1.rest_0_.halo
  10.7 0.2 local_0.2.partial
  10.9 0.3 from_own.3.rows
  11.2 0.0 collective-permute-done.4.other
  11.2 0.2 local_1.2.partial
  11.4 0.2 images_1_1.2
  11.6 0.7 %collective-permute-done.2.halo = f32[56,8,128]{2,1,0:T(8,128)S(1)} collective-permute-done((f32[56,8,128]{2,1,0:T(8,128)S(1)}, f32[56,8,128]{2,1,0:T(8,128)S(1)}, u32[]{:S(2)}, u32[]{:S(2)}) %collective-permute-start.2) | collective-permute-done | bytes 229408 | tf_op jit(solution)/shard_map/ppermute | solution.py:293
  12.3 0.2 images_0_1.2
  12.5 2.5 %collective-permute-start.5 = (f32[256,128]{1,0:T(8,128)S(1)}, f32[256,128]{1,0:T(8,128)S(1)}, u32[]{:S(2)}, u32[]{:S(2)}) collective-permute-start(f32[256,128]{1,0:T(8,128)S(1)} %get-tuple-element.34), channel_id=1, source_target_pairs={{0,6},{1,7},{2,4},{3,5},{4,2},{5,3},{6,0},{7,1},{8,14},{9,15},{10,... | collective-permute-start | bytes 393224 | tf_op jit(solution)/shard_map/ppermute | solution.py:290
  15.0 0.5 %collective-permute-start.6 = (f32[256,128]{1,0:T(8,128)S(1)}, f32[256,128]{1,0:T(8,128)S(1)}, u32[]{:S(2)}, u32[]{:S(2)}) collective-permute-start(f32[256,128]{1,0:T(8,128)S(1)} %get-tuple-element.35), channel_id=1, source_target_pairs={{0,4},{1,3},{2,6},{3,1},{4,0},{5,7},{6,2},{7,5},{8,12},{9,11},{10,... | collective-permute-start | bytes 393224 | tf_op jit(solution)/shard_map/ppermute | solution.py:290
  15.5 0.5 %collective-permute-start.7 = (f32[256,128]{1,0:T(8,128)S(1)}, f32[256,128]{1,0:T(8,128)S(1)}, u32[]{:S(2)}, u32[]{:S(2)}) collective-permute-start(f32[256,128]{1,0:T(8,128)S(1)} %get-tuple-element.36.rest_1_), channel_id=1, source_target_pairs={{0,2},{1,5},{2,0},{3,7},{4,6},{5,1},{6,4},{7,3},{8,10},{9,13},{10,... | collective-permute-start | bytes 393224 | tf_op jit(solution)/shard_map/ppermute | solution.py:290
  16.1 0.1 images_0_0.2.rest_3_
  16.2 3.6 %collective-permute-done.5.rest_0_ = f32[256,128]{1,0:T(8,128)S(1)} collective-permute-done((f32[256,128]{1,0:T(8,128)S(1)}, f32[256,128]{1,0:T(8,128)S(1)}, u32[]{:S(2)}, u32[]{:S(2)}) %collective-permute-start.5) | collective-permute-done | bytes 131104 | tf_op jit(solution)/shard_map/ppermute | solution.py:290
  19.8 1.9 %collective-permute-done.6.rest_1_ = f32[256,128]{1,0:T(8,128)S(1)} collective-permute-done((f32[256,128]{1,0:T(8,128)S(1)}, f32[256,128]{1,0:T(8,128)S(1)}, u32[]{:S(2)}, u32[]{:S(2)}) %collective-permute-start.6) | collective-permute-done | bytes 131104 | tf_op jit(solution)/shard_map/ppermute | solution.py:290
  21.7 0.1 collective-permute-done.7.rest_2_
  21.8 0.8 %product_0.2 = f32[448,128]{1,0:T(8,128)S(1)} custom-call(bf16[1176,128]{1,0:T(8,128)(2,1)S(1)} %get-tuple-element.48.weights, f32[21,8,128]{2,1,0:T(8,128)S(1)} %dynamic-slice_bitcast_fusion.2.modes, f32[256,128]{1,0:T(8,128)S(1)} %collective-permute-done.5.rest_0_, f32[256,128]{1,0:T(8,128)S(1)} %collective-permute-done.6.rest_1_, ...), custom_call_target="tpu_custom_call" | custom-call | flops 616562688 | bytes 1048576 | tf_op jit(solution)/shard_map/product_0/pallas_call | solution.py:159
  22.6 1.3 %collective-permute-start.11 = (f32[56,8,128]{2,1,0:T(8,128)S(1)}, f32[56,8,128]{2,1,0:T(8,128)S(1)}, u32[]{:S(2)}, u32[]{:S(2)}) collective-permute-start(f32[56,8,128]{2,1,0:T(8,128)S(1)} %bitcast.13), channel_id=1, source_target_pairs={{0,2},{1,8},{2,0},{3,10},{4,6},{5,12},{6,4},{7,14},{8,1},{9,16},{1... | collective-permute-start | bytes 688136 | tf_op jit(solution)/shard_map/ppermute | solution.py:293
  23.9 0.8 %product_1.2 = f32[448,128]{1,0:T(8,128)S(1)} custom-call(f32[1176,128]{1,0:T(8,128)S(1)} %collective-permute-done.8.weights, f32[21,8,128]{2,1,0:T(8,128)S(1)} %dynamic-slice_bitcast_fusion.2.modes, f32[256,128]{1,0:T(8,128)S(1)} %collective-permute-done.5.rest_0_, f32[256,128]{1,0:T(8,128)S(1)} %collective-permute-done.6.rest_1_, ...), custom_call_target="tpu_custom_call" | custom-call | flops 616562688 | bytes 1048576 | tf_op jit(solution)/shard_map/product_1/pallas_call | solution.py:159
  24.7 0.6 %collective-permute-start.9 = (f32[56,8,128]{2,1,0:T(8,128)S(1)}, f32[56,8,128]{2,1,0:T(8,128)S(1)}, u32[]{:S(2)}, u32[]{:S(2)}) collective-permute-start(f32[56,8,128]{2,1,0:T(8,128)S(1)} %bitcast.18), channel_id=1, source_target_pairs={{0,1},{1,0},{2,3},{3,2},{4,5},{5,4},{6,7},{7,6},{8,9},{9,8},{10,11... | collective-permute-start | bytes 688136 | tf_op jit(solution)/shard_map/ppermute | solution.py:242
  25.3 1.0 %collective-permute-start.15 = (f32[56,8,128]{2,1,0:T(8,128)S(1)}, f32[56,8,128]{2,1,0:T(8,128)S(1)}, u32[]{:S(2)}, u32[]{:S(2)}) collective-permute-start(f32[56,8,128]{2,1,0:T(8,128)S(1)} %bitcast.19), channel_id=1, source_target_pairs={{0,2},{1,8},{2,0},{3,10},{4,6},{5,12},{6,4},{7,14},{8,1},{9,16},{1... | collective-permute-start | bytes 688136 | tf_op jit(solution)/shard_map/ppermute | solution.py:293
  26.3 2.4 %collective-permute-done.11.rest_0_.halo = f32[56,8,128]{2,1,0:T(8,128)S(1)} collective-permute-done((f32[56,8,128]{2,1,0:T(8,128)S(1)}, f32[56,8,128]{2,1,0:T(8,128)S(1)}, u32[]{:S(2)}, u32[]{:S(2)}) %collective-permute-start.11) | collective-permute-done | bytes 229408 | tf_op jit(solution)/shard_map/ppermute | solution.py:293
  28.7 0.2 local_1.3.partial
  28.9 0.2 images_1_1.3
  29.0 1.3 %collective-permute-start.12 = (f32[128,128]{1,0:T(8,128)S(1)}, f32[128,128]{1,0:T(8,128)S(1)}, u32[]{:S(2)}, u32[]{:S(2)}) collective-permute-start(f32[128,128]{1,0:T(8,128)S(1)} %get-tuple-element.39), channel_id=1, source_target_pairs={{0,2},{1,5},{2,0},{3,7},{4,6},{5,1},{6,4},{7,3},{8,10},{9,13},{10,... | collective-permute-start | bytes 196616 | tf_op jit(solution)/shard_map/ppermute | solution.py:290
  30.4 1.5 %collective-permute-start.13 = (f32[128,128]{1,0:T(8,128)S(1)}, f32[128,128]{1,0:T(8,128)S(1)}, u32[]{:S(2)}, u32[]{:S(2)}) collective-permute-start(f32[128,128]{1,0:T(8,128)S(1)} %get-tuple-element.40), channel_id=1, source_target_pairs={{0,4},{1,3},{2,6},{3,1},{4,0},{5,7},{6,2},{7,5},{8,12},{9,11},{10,... | collective-permute-start | bytes 196616 | tf_op jit(solution)/shard_map/ppermute | solution.py:290
  31.8 0.8 %collective-permute-start.14 = (f32[128,128]{1,0:T(8,128)S(1)}, f32[128,128]{1,0:T(8,128)S(1)}, u32[]{:S(2)}, u32[]{:S(2)}) collective-permute-start(f32[128,128]{1,0:T(8,128)S(1)} %get-tuple-element.41.rest_0_), channel_id=1, source_target_pairs={{0,6},{1,7},{2,4},{3,5},{4,2},{5,3},{6,0},{7,1},{8,14},{9,15},{10,... | collective-permute-start | bytes 196616 | tf_op jit(solution)/shard_map/ppermute | solution.py:290
  32.6 0.0 collective-permute-done.9.there.other
  32.6 0.2 local_0.3.partial
  32.8 0.0 collective-permute-done.15.halo
  32.8 0.2 images_0_1.3
  33.0 2.2 %collective-permute-start.16 = (f32[128,128]{1,0:T(8,128)S(1)}, f32[128,128]{1,0:T(8,128)S(1)}, u32[]{:S(2)}, u32[]{:S(2)}) collective-permute-start(f32[128,128]{1,0:T(8,128)S(1)} %get-tuple-element.44), channel_id=1, source_target_pairs={{0,6},{1,7},{2,4},{3,5},{4,2},{5,3},{6,0},{7,1},{8,14},{9,15},{10,... | collective-permute-start | bytes 196616 | tf_op jit(solution)/shard_map/ppermute | solution.py:290
  35.2 0.6 %collective-permute-start.17 = (f32[128,128]{1,0:T(8,128)S(1)}, f32[128,128]{1,0:T(8,128)S(1)}, u32[]{:S(2)}, u32[]{:S(2)}) collective-permute-start(f32[128,128]{1,0:T(8,128)S(1)} %get-tuple-element.45), channel_id=1, source_target_pairs={{0,4},{1,3},{2,6},{3,1},{4,0},{5,7},{6,2},{7,5},{8,12},{9,11},{10,... | collective-permute-start | bytes 196616 | tf_op jit(solution)/shard_map/ppermute | solution.py:290
  35.8 0.8 %collective-permute-start.18 = (f32[128,128]{1,0:T(8,128)S(1)}, f32[128,128]{1,0:T(8,128)S(1)}, u32[]{:S(2)}, u32[]{:S(2)}) collective-permute-start(f32[128,128]{1,0:T(8,128)S(1)} %get-tuple-element.46.rest_0_), channel_id=1, source_target_pairs={{0,2},{1,5},{2,0},{3,7},{4,6},{5,1},{6,4},{7,3},{8,10},{9,13},{10,... | collective-permute-start | bytes 196616 | tf_op jit(solution)/shard_map/ppermute | solution.py:290
  36.5 0.1 images_1_0.1.rest_3_
  36.7 0.9 %collective-permute-done.14.rest_2_ = f32[128,128]{1,0:T(8,128)S(1)} collective-permute-done((f32[128,128]{1,0:T(8,128)S(1)}, f32[128,128]{1,0:T(8,128)S(1)}, u32[]{:S(2)}, u32[]{:S(2)}) %collective-permute-start.14) | collective-permute-done | bytes 65568 | tf_op jit(solution)/shard_map/ppermute | solution.py:290
  37.6 0.1 images_0_0.3.rest_5_
  37.8 0.8 %write.2 = (f32[56,2,8,128]{3,2,1,0:T(8,128)}, f32[8,128]{1,0:T(8,128)S(1)}) custom-call(f32[56,8,128]{2,1,0:T(8,128)S(1)} %bitcast.17, f32[56,8,128]{2,1,0:T(8,128)S(1)} %collective-permute-done.9.there.other), custom_call_target="tpu_custom_call" | custom-call | tf_op jit(solution)/shard_map/write/pallas_call | solution.py:188
  38.6 0.9 %collective-permute-done.17.rest_3_ = f32[128,128]{1,0:T(8,128)S(1)} collective-permute-done((f32[128,128]{1,0:T(8,128)S(1)}, f32[128,128]{1,0:T(8,128)S(1)}, u32[]{:S(2)}, u32[]{:S(2)}) %collective-permute-start.17) | collective-permute-done | bytes 65568 | tf_op jit(solution)/shard_map/ppermute | solution.py:290
  39.5 0.6 %collective-permute-done.18.rest_4_ = f32[128,128]{1,0:T(8,128)S(1)} collective-permute-done((f32[128,128]{1,0:T(8,128)S(1)}, f32[128,128]{1,0:T(8,128)S(1)}, u32[]{:S(2)}, u32[]{:S(2)}) %collective-permute-start.18) | collective-permute-done | bytes 65568 | tf_op jit(solution)/shard_map/ppermute | solution.py:290
  40.0 0.8 %product_1.3 = f32[448,128]{1,0:T(8,128)S(1)} custom-call(f32[1176,128]{1,0:T(8,128)S(1)} %collective-permute-done.8.weights, f32[21,8,128]{2,1,0:T(8,128)S(1)} %dynamic-slice_bitcast_fusion.2.modes, bf16[512,128]{1,0:T(8,128)(2,1)S(1)} %get-tuple-element.42.rest_0_, bf16[512,128]{1,0:T(8,128)(2,1)S(1)} %get-tuple-element.43.rest_1_, ...), custom_call_target="tpu_custom_call" | custom-call | flops 616562688 | bytes 1048576 | tf_op jit(solution)/shard_map/product_1/pallas_call | solution.py:159
  40.9 0.1 collective-permute-start.19
  40.9 0.8 %product_0.3 = f32[448,128]{1,0:T(8,128)S(1)} custom-call(bf16[1176,128]{1,0:T(8,128)(2,1)S(1)} %get-tuple-element.48.weights, f32[21,8,128]{2,1,0:T(8,128)S(1)} %dynamic-slice_bitcast_fusion.2.modes, bf16[512,128]{1,0:T(8,128)(2,1)S(1)} %get-tuple-element.42.rest_0_, bf16[512,128]{1,0:T(8,128)(2,1)S(1)} %get-tuple-element.43.rest_1_, ...), custom_call_target="tpu_custom_call" | custom-call | flops 616562688 | bytes 1048576 | tf_op jit(solution)/shard_map/product_0/pallas_call | solution.py:159
  41.7 0.7 %collective-permute-done.19.there = f32[56,8,128]{2,1,0:T(8,128)S(1)} collective-permute-done((f32[56,8,128]{2,1,0:T(8,128)S(1)}, f32[56,8,128]{2,1,0:T(8,128)S(1)}, u32[]{:S(2)}, u32[]{:S(2)}) %collective-permute-start.19) | collective-permute-done | bytes 229408 | tf_op jit(solution)/shard_map/ppermute | solution.py:242
  42.4 0.8 %write.3 = f32[56,2,8,128]{3,2,1,0:T(8,128)} custom-call(f32[56,8,128]{2,1,0:T(8,128)S(1)} %bitcast.21, f32[56,8,128]{2,1,0:T(8,128)S(1)} %collective-permute-done.19.there), custom_call_target="tpu_custom_call" | custom-call | tf_op jit(solution)/shard_map/write/pallas_call | solution.py:188
  (20 shorter events, 0.1 us)
Async XLA Ops:
  0.6 15.4 %copy-start = (f32[21,2,8,128]{3,2,1,0:T(8,128)S(1)}, f32[21,2,8,128]{3,2,1,0:T(8,128)}, u32[]{:S(2)}) copy-start(f32[21,2,8,128]{3,2,1,0:T(8,128)} %param.7) | copy-start | bytes 516100
  0.6 4.2 %copy-start.1 = (s32[1,64]{1,0:T(1,128)S(1)}, s32[1,64]{1,0:T(1,128)}, u32[]{:S(2)}) copy-start(s32[1,64]{1,0:T(1,128)} %listed) | copy-start | bytes 772
  1.8 3.1 %collective-permute-start = (f32[56,8,128]{2,1,0:T(8,128)S(1)}, f32[56,8,128]{2,1,0:T(8,128)S(1)}, u32[]{:S(2)}, u32[]{:S(2)}) collective-permute-start(f32[56,8,128]{2,1,0:T(8,128)S(1)} %get-tuple-element.52.other), channel_id=1, source_target_pairs={{0,1},{1,0},{2,3},{3,2},{4,5},{5,4},{6,7},{7,6},{8,9},{9,8},{10,11... | collective-permute-start | bytes 688136 | tf_op jit(solution)/shard_map/ppermute | solution.py:242
  2.3 8.4 %collective-permute-start.1 = (f32[56,8,128]{2,1,0:T(8,128)S(1)}, f32[56,8,128]{2,1,0:T(8,128)S(1)}, u32[]{:S(2)}, u32[]{:S(2)}) collective-permute-start(f32[56,8,128]{2,1,0:T(8,128)S(1)} %get-tuple-element.30.center), channel_id=1, source_target_pairs={{0,2},{1,8},{2,0},{3,10},{4,6},{5,12},{6,4},{7,14},{8,1},{9,16},{1... | collective-permute-start | bytes 688136 | tf_op jit(solution)/shard_map/ppermute | solution.py:293
  4.9 0.7 %copy-start.2 = (s32[56,41]{0,1:T(8,128)S(1)}, s32[56,41]{0,1:T(8,128)}, u32[]{:S(2)}) copy-start(s32[56,41]{0,1:T(8,128)} %param.9) | copy-start | bytes 27556
  4.9 0.9 %copy-start.3 = (f32[56,41]{0,1:T(8,128)S(1)}, f32[56,41]{0,1:T(8,128)}, u32[]{:S(2)}) copy-start(f32[56,41]{0,1:T(8,128)} %param.11) | copy-start | bytes 27556
  4.9 1.1 %copy-start.4 = (s32[56,41]{0,1:T(8,128)S(1)}, s32[56,41]{0,1:T(8,128)}, u32[]{:S(2)}) copy-start(s32[56,41]{0,1:T(8,128)} %param.10) | copy-start | bytes 27556
  5.2 5.7 %collective-permute-start.3 = (s32[1,64]{1,0:T(1,128)S(1)}, s32[1,64]{1,0:T(1,128)S(1)}, u32[]{:S(2)}, u32[]{:S(2)}) collective-permute-start(s32[1,64]{1,0:T(1,128)S(1)} %copy-done.1), channel_id=1, source_target_pairs={{0,1},{1,0},{2,3},{3,2},{4,5},{5,4},{6,7},{7,6},{8,9},{9,8},{10,11... | collective-permute-start | bytes 776 | tf_op jit(solution)/shard_map/ppermute | solution.py:242
  6.1 5.1 %collective-permute-start.4 = (f32[56,8,128]{2,1,0:T(8,128)S(1)}, f32[56,8,128]{2,1,0:T(8,128)S(1)}, u32[]{:S(2)}, u32[]{:S(2)}) collective-permute-start(f32[56,8,128]{2,1,0:T(8,128)S(1)} %get-tuple-element.30.center), channel_id=1, source_target_pairs={{0,1},{1,0},{2,3},{3,2},{4,5},{5,4},{6,7},{7,6},{8,9},{9,8},{10,11... | collective-permute-start | bytes 688136 | tf_op jit(solution)/shard_map/ppermute | solution.py:242
  6.3 6.0 %collective-permute-start.2 = (f32[56,8,128]{2,1,0:T(8,128)S(1)}, f32[56,8,128]{2,1,0:T(8,128)S(1)}, u32[]{:S(2)}, u32[]{:S(2)}) collective-permute-start(f32[56,8,128]{2,1,0:T(8,128)S(1)} %collective-permute-done.center), channel_id=1, source_target_pairs={{0,2},{1,8},{2,0},{3,10},{4,6},{5,12},{6,4},{7,14},{8,1},{9,16},{1... | collective-permute-start | bytes 688136 | tf_op jit(solution)/shard_map/ppermute | solution.py:293
  10.4 13.5 %collective-permute-start.8 = (f32[1176,128]{1,0:T(8,128)S(1)}, f32[1176,128]{1,0:T(8,128)S(1)}, u32[]{:S(2)}, u32[]{:S(2)}) collective-permute-start(f32[1176,128]{1,0:T(8,128)S(1)} %get-tuple-element.49), channel_id=1, source_target_pairs={{0,1},{1,0},{2,3},{3,2},{4,5},{5,4},{6,7},{7,6},{8,9},{9,8},{10,11... | collective-permute-start | bytes 1806344 | tf_op jit(solution)/shard_map/ppermute | solution.py:242
  12.5 7.3 %collective-permute-start.5 = (f32[256,128]{1,0:T(8,128)S(1)}, f32[256,128]{1,0:T(8,128)S(1)}, u32[]{:S(2)}, u32[]{:S(2)}) collective-permute-start(f32[256,128]{1,0:T(8,128)S(1)} %get-tuple-element.34), channel_id=1, source_target_pairs={{0,6},{1,7},{2,4},{3,5},{4,2},{5,3},{6,0},{7,1},{8,14},{9,15},{10,... | collective-permute-start | bytes 393224 | tf_op jit(solution)/shard_map/ppermute | solution.py:290
  15.0 6.7 %collective-permute-start.6 = (f32[256,128]{1,0:T(8,128)S(1)}, f32[256,128]{1,0:T(8,128)S(1)}, u32[]{:S(2)}, u32[]{:S(2)}) collective-permute-start(f32[256,128]{1,0:T(8,128)S(1)} %get-tuple-element.35), channel_id=1, source_target_pairs={{0,4},{1,3},{2,6},{3,1},{4,0},{5,7},{6,2},{7,5},{8,12},{9,11},{10,... | collective-permute-start | bytes 393224 | tf_op jit(solution)/shard_map/ppermute | solution.py:290
  15.5 6.2 %collective-permute-start.7 = (f32[256,128]{1,0:T(8,128)S(1)}, f32[256,128]{1,0:T(8,128)S(1)}, u32[]{:S(2)}, u32[]{:S(2)}) collective-permute-start(f32[256,128]{1,0:T(8,128)S(1)} %get-tuple-element.36.rest_1_), channel_id=1, source_target_pairs={{0,2},{1,5},{2,0},{3,7},{4,6},{5,1},{6,4},{7,3},{8,10},{9,13},{10,... | collective-permute-start | bytes 393224 | tf_op jit(solution)/shard_map/ppermute | solution.py:290
  22.6 6.1 %collective-permute-start.11 = (f32[56,8,128]{2,1,0:T(8,128)S(1)}, f32[56,8,128]{2,1,0:T(8,128)S(1)}, u32[]{:S(2)}, u32[]{:S(2)}) collective-permute-start(f32[56,8,128]{2,1,0:T(8,128)S(1)} %bitcast.13), channel_id=1, source_target_pairs={{0,2},{1,8},{2,0},{3,10},{4,6},{5,12},{6,4},{7,14},{8,1},{9,16},{1... | collective-permute-start | bytes 688136 | tf_op jit(solution)/shard_map/ppermute | solution.py:293
  23.9 4.8 %collective-permute-start.10 = (f32[56,8,128]{2,1,0:T(8,128)S(1)}, f32[56,8,128]{2,1,0:T(8,128)S(1)}, u32[]{:S(2)}, u32[]{:S(2)}) collective-permute-start(f32[56,8,128]{2,1,0:T(8,128)S(1)} %bitcast.14), channel_id=1, source_target_pairs={{0,1},{1,0},{2,3},{3,2},{4,5},{5,4},{6,7},{7,6},{8,9},{9,8},{10,11... | collective-permute-start | bytes 688136 | tf_op jit(solution)/shard_map/ppermute | solution.py:242
  24.7 7.9 %collective-permute-start.9 = (f32[56,8,128]{2,1,0:T(8,128)S(1)}, f32[56,8,128]{2,1,0:T(8,128)S(1)}, u32[]{:S(2)}, u32[]{:S(2)}) collective-permute-start(f32[56,8,128]{2,1,0:T(8,128)S(1)} %bitcast.18), channel_id=1, source_target_pairs={{0,1},{1,0},{2,3},{3,2},{4,5},{5,4},{6,7},{7,6},{8,9},{9,8},{10,11... | collective-permute-start | bytes 688136 | tf_op jit(solution)/shard_map/ppermute | solution.py:242
  25.3 7.5 %collective-permute-start.15 = (f32[56,8,128]{2,1,0:T(8,128)S(1)}, f32[56,8,128]{2,1,0:T(8,128)S(1)}, u32[]{:S(2)}, u32[]{:S(2)}) collective-permute-start(f32[56,8,128]{2,1,0:T(8,128)S(1)} %bitcast.19), channel_id=1, source_target_pairs={{0,2},{1,8},{2,0},{3,10},{4,6},{5,12},{6,4},{7,14},{8,1},{9,16},{1... | collective-permute-start | bytes 688136 | tf_op jit(solution)/shard_map/ppermute | solution.py:293
  29.0 6.7 %collective-permute-start.12 = (f32[128,128]{1,0:T(8,128)S(1)}, f32[128,128]{1,0:T(8,128)S(1)}, u32[]{:S(2)}, u32[]{:S(2)}) collective-permute-start(f32[128,128]{1,0:T(8,128)S(1)} %get-tuple-element.39), channel_id=1, source_target_pairs={{0,2},{1,5},{2,0},{3,7},{4,6},{5,1},{6,4},{7,3},{8,10},{9,13},{10,... | collective-permute-start | bytes 196616 | tf_op jit(solution)/shard_map/ppermute | solution.py:290
  30.4 6.3 %collective-permute-start.13 = (f32[128,128]{1,0:T(8,128)S(1)}, f32[128,128]{1,0:T(8,128)S(1)}, u32[]{:S(2)}, u32[]{:S(2)}) collective-permute-start(f32[128,128]{1,0:T(8,128)S(1)} %get-tuple-element.40), channel_id=1, source_target_pairs={{0,4},{1,3},{2,6},{3,1},{4,0},{5,7},{6,2},{7,5},{8,12},{9,11},{10,... | collective-permute-start | bytes 196616 | tf_op jit(solution)/shard_map/ppermute | solution.py:290
  31.8 5.8 %collective-permute-start.14 = (f32[128,128]{1,0:T(8,128)S(1)}, f32[128,128]{1,0:T(8,128)S(1)}, u32[]{:S(2)}, u32[]{:S(2)}) collective-permute-start(f32[128,128]{1,0:T(8,128)S(1)} %get-tuple-element.41.rest_0_), channel_id=1, source_target_pairs={{0,6},{1,7},{2,4},{3,5},{4,2},{5,3},{6,0},{7,1},{8,14},{9,15},{10,... | collective-permute-start | bytes 196616 | tf_op jit(solution)/shard_map/ppermute | solution.py:290
  33.0 5.6 %collective-permute-start.16 = (f32[128,128]{1,0:T(8,128)S(1)}, f32[128,128]{1,0:T(8,128)S(1)}, u32[]{:S(2)}, u32[]{:S(2)}) collective-permute-start(f32[128,128]{1,0:T(8,128)S(1)} %get-tuple-element.44), channel_id=1, source_target_pairs={{0,6},{1,7},{2,4},{3,5},{4,2},{5,3},{6,0},{7,1},{8,14},{9,15},{10,... | collective-permute-start | bytes 196616 | tf_op jit(solution)/shard_map/ppermute | solution.py:290
  35.2 4.3 %collective-permute-start.17 = (f32[128,128]{1,0:T(8,128)S(1)}, f32[128,128]{1,0:T(8,128)S(1)}, u32[]{:S(2)}, u32[]{:S(2)}) collective-permute-start(f32[128,128]{1,0:T(8,128)S(1)} %get-tuple-element.45), channel_id=1, source_target_pairs={{0,4},{1,3},{2,6},{3,1},{4,0},{5,7},{6,2},{7,5},{8,12},{9,11},{10,... | collective-permute-start | bytes 196616 | tf_op jit(solution)/shard_map/ppermute | solution.py:290
  35.8 4.3 %collective-permute-start.18 = (f32[128,128]{1,0:T(8,128)S(1)}, f32[128,128]{1,0:T(8,128)S(1)}, u32[]{:S(2)}, u32[]{:S(2)}) collective-permute-start(f32[128,128]{1,0:T(8,128)S(1)} %get-tuple-element.46.rest_0_), channel_id=1, source_target_pairs={{0,2},{1,5},{2,0},{3,7},{4,6},{5,1},{6,4},{7,3},{8,10},{9,13},{10,... | collective-permute-start | bytes 196616 | tf_op jit(solution)/shard_map/ppermute | solution.py:290
  40.9 1.6 %collective-permute-start.19 = (f32[56,8,128]{2,1,0:T(8,128)S(1)}, f32[56,8,128]{2,1,0:T(8,128)S(1)}, u32[]{:S(2)}, u32[]{:S(2)}) collective-permute-start(f32[56,8,128]{2,1,0:T(8,128)S(1)} %bitcast.22), channel_id=1, source_target_pairs={{0,1},{1,0},{2,3},{3,2},{4,5},{5,4},{6,7},{7,6},{8,9},{9,8},{10,11... | collective-permute-start | bytes 688136 | tf_op jit(solution)/shard_map/ppermute | solution.py:242
